TPU v7x, 128 devices: a whole 4x4x4 slice. The times are simulated.
128 devices in a mesh: ctx: 32 (over y, z, core), fsdp: 4 (over x).
Axes of the slice: x: 4, y: 4, z: 4, core: 2. Of those that a mesh axis runs over, the one named last changes fastest.
Arguments:
- tokens: bfloat16 [4, 4096, 768], P('fsdp', 'ctx'), may hold values from -6 to 6
- cotangent: bfloat16 [4, 4096, 768], P('fsdp', 'ctx'), may hold values from -6 to 6
- w_qkv: float32 [768, 2304], P(('ctx', 'fsdp')), may hold values from -0.3125 to 0.3125
- qkv_m: float32 [768, 2304], P(('ctx', 'fsdp')), may hold values from -40 to 40
- qkv_v: float32 [768, 2304], P(('ctx', 'fsdp')), may hold values from 2.048 to 32.768
- w_out: float32 [768, 768], P(('ctx', 'fsdp')), may hold values from -1.25 to 1.25
- out_m: float32 [768, 768], P(('ctx', 'fsdp')), may hold values from -40 to 40
- out_v: float32 [768, 768], P(('ctx', 'fsdp')), may hold values from 2.048 to 32.768
- w_fc: float32 [768, 3072], P(('ctx', 'fsdp')), may hold values from -0.21875 to 0.21875
- fc_m: float32 [768, 3072], P(('ctx', 'fsdp')), may hold values from -40 to 40
- fc_v: float32 [768, 3072], P(('ctx', 'fsdp')), may hold values from 2.048 to 32.768
- w_proj: float32 [3072, 768], P(('ctx', 'fsdp')), may hold values from -0.109375 to 0.109375
- proj_m: float32 [3072, 768], P(('ctx', 'fsdp')), may hold values from -40 to 40
- proj_v: float32 [3072, 768], P(('ctx', 'fsdp')), may hold values from 2.048 to 32.768
- vectors: float32 [768, 12], P(('ctx', 'fsdp')), may hold values from -0.6 to 1.3
- vec_m: float32 [768, 12], P(('ctx', 'fsdp')), may hold values from -80 to 80
- vec_v: float32 [768, 12], P(('ctx', 'fsdp')), may hold values from 8.192 to 131.072
Outputs:
- output: float32 [4, 4096, 768], P('fsdp', 'ctx')
- grad_tokens: float32 [4, 4096, 768], P('fsdp', 'ctx')
- new_w_qkv: float32 [768, 2304], P(('ctx', 'fsdp'))
- new_qkv_m: float32 [768, 2304], P(('ctx', 'fsdp'))
- new_qkv_v: float32 [768, 2304], P(('ctx', 'fsdp'))
- new_w_out: float32 [768, 768], P(('ctx', 'fsdp'))
- new_out_m: float32 [768, 768], P(('ctx', 'fsdp'))
- new_out_v: float32 [768, 768], P(('ctx', 'fsdp'))
- new_w_fc: float32 [768, 3072], P(('ctx', 'fsdp'))
- new_fc_m: float32 [768, 3072], P(('ctx', 'fsdp'))
- new_fc_v: float32 [768, 3072], P(('ctx', 'fsdp'))
- new_w_proj: float32 [3072, 768], P(('ctx', 'fsdp'))
- new_proj_m: float32 [3072, 768], P(('ctx', 'fsdp'))
- new_proj_v: float32 [3072, 768], P(('ctx', 'fsdp'))
- new_vectors: float32 [768, 12], P(('ctx', 'fsdp'))
- new_vec_m: float32 [768, 12], P(('ctx', 'fsdp'))
- new_vec_v: float32 [768, 12], P(('ctx', 'fsdp'))
All inputs are finite; a program needn't handle non-finite values.
Results may differ from a plain program's by a relative error of at most 0.015.
The roundings to bfloat16 on the way count: a program that leaves them out, or rounds other values in their place, can miss the bound.
Values may be sent and summed in bfloat16 or wider, within the bound.
A program may use at most 192 MiB of HBM per device.

v0:
```python
import jax
import jax.numpy as jnp
from jax import lax
from jax.sharding import PartitionSpec as P

H = 12
HD = 64
STEP = 10


EPSILON = 1e-05
BETA_ONE = 0.9
BETA_TWO = 0.999
ADAM_EPSILON = 1e-08


def layer_norm(inputs, gain, shift):
    row_mean = jnp.mean(inputs, -1, keepdims=True)
    centered = inputs - row_mean
    variance = jnp.mean(centered * centered, -1, keepdims=True)
    return centered * lax.rsqrt(variance + EPSILON) * gain + shift


def gelu_tanh(values):
    return (
        0.5
        * values
        * (1.0 + jnp.tanh(0.7978845608028654 * (values + 0.044715 * values * values * values)))
    )


def split_heads(matrix, group_count):
    return matrix.reshape(matrix.shape[0], group_count, -1, HD).transpose(1, 2, 0, 3)


def join_heads(blocks):
    return blocks.transpose(2, 0, 1, 3).reshape(blocks.shape[2], -1)


def adam_update(weight, moment_one, moment_two, gradient, rate, decay):
    new_one = BETA_ONE * moment_one + (1.0 - BETA_ONE) * gradient
    new_two = BETA_TWO * moment_two + (1.0 - BETA_TWO) * gradient * gradient
    fix_one = 1.0 - BETA_ONE**STEP
    fix_two = 1.0 - BETA_TWO**STEP
    direction = new_one / fix_one / (jnp.sqrt(new_two / fix_two) + ADAM_EPSILON)
    return (weight - rate * (direction + decay * weight), new_one, new_two)


def shards(
    tokens,
    cotangent,
    w_qkv,
    qkv_m,
    qkv_v,
    w_out,
    out_m,
    out_v,
    w_fc,
    fc_m,
    fc_v,
    w_proj,
    proj_m,
    proj_v,
    vectors,
    vec_m,
    vec_v,
):
    low_qkv = w_qkv.astype(jnp.bfloat16)
    low_out = w_out.astype(jnp.bfloat16)
    low_fc = w_fc.astype(jnp.bfloat16)
    low_proj = w_proj.astype(jnp.bfloat16)
    low_vec = vectors.astype(jnp.bfloat16)
    full_qkv, full_out, full_fc, full_proj, full_vec = (
        lax.all_gather(low_qkv, ("ctx", "fsdp"), axis=0, tiled=True),
        lax.all_gather(low_out, ("ctx", "fsdp"), axis=0, tiled=True),
        lax.all_gather(low_fc, ("ctx", "fsdp"), axis=0, tiled=True),
        lax.all_gather(low_proj, ("ctx", "fsdp"), axis=0, tiled=True),
        lax.all_gather(low_vec, ("ctx", "fsdp"), axis=0, tiled=True),
    )
    inputs = tokens[0].astype(jnp.float32)
    width = inputs.shape[1]
    block_rows = inputs.shape[0]
    group_count = H // 4
    vector_cols = full_vec.astype(jnp.float32)
    gain_one = vector_cols[:, 0]
    shift_one = vector_cols[:, 1]
    q_bias = vector_cols[:, 2]
    v_bias = vector_cols[:, 3]
    out_bias = vector_cols[:, 4]
    gain_two = vector_cols[:, 5]
    shift_two = vector_cols[:, 6]
    proj_bias = vector_cols[:, 7]
    fc_bias = vector_cols[:, 8:].T.reshape(-1)
    normed_one, ln_one_back = jax.vjp(layer_norm, inputs, gain_one, shift_one)
    act_one = normed_one.astype(jnp.bfloat16)
    mixed = jnp.dot(act_one, full_qkv, preferred_element_type=jnp.float32)
    query = (mixed[:, :width] + q_bias).astype(jnp.bfloat16)
    key_rows = mixed[:, width : 2 * width].astype(jnp.bfloat16)
    value_rows = (mixed[:, 2 * width :] + v_bias).astype(jnp.bfloat16)
    key_all, value_all = (
        lax.all_gather(key_rows, "ctx", axis=0, tiled=True),
        lax.all_gather(value_rows, "ctx", axis=0, tiled=True),
    )
    length = key_all.shape[0]
    first_row = lax.axis_index("ctx") * block_rows
    query_pos = first_row + jnp.arange(block_rows, dtype=jnp.int32)
    all_pos = jnp.arange(length, dtype=jnp.int32)
    visible = query_pos[:, None] >= all_pos[None, :]
    query_groups = split_heads(query, group_count)
    key_groups = split_heads(key_all, group_count)
    value_groups = split_heads(value_all, group_count)

    def forward_group(operands):
        query_blk, key_blk, value_blk = operands
        scores = (
            jnp.einsum("hqd,hkd->hqk", query_blk, key_blk, preferred_element_type=jnp.float32)
            * 0.125
        )
        scores = jnp.where(visible, scores, -1000000000.0)
        row_max = jnp.max(scores, -1, keepdims=True)
        exponent = jnp.exp(scores - row_max)
        row_total = jnp.sum(exponent, -1, keepdims=True)
        attn_prob = (exponent / row_total).astype(jnp.bfloat16)
        head_blk = jnp.einsum(
            "hqk,hkd->hqd", attn_prob, value_blk, preferred_element_type=jnp.float32
        )
        return (head_blk.astype(jnp.bfloat16), row_max[..., 0] + jnp.log(row_total[..., 0]))

    head_groups, log_totals = lax.map(forward_group, (query_groups, key_groups, value_groups))
    heads = join_heads(head_groups)
    x_two = inputs + jnp.dot(heads, full_out, preferred_element_type=jnp.float32) + out_bias
    normed_two, ln_two_back = jax.vjp(layer_norm, x_two, gain_two, shift_two)
    act_two = normed_two.astype(jnp.bfloat16)
    hidden = jnp.dot(act_two, full_fc, preferred_element_type=jnp.float32) + fc_bias
    gelu_out, gelu_back = jax.vjp(gelu_tanh, hidden)
    act_three = gelu_out.astype(jnp.bfloat16)
    output = x_two + jnp.dot(act_three, full_proj, preferred_element_type=jnp.float32) + proj_bias
    back_qkv, back_out, back_fc, back_proj = (
        lax.all_gather(low_qkv, ("ctx", "fsdp"), axis=0, tiled=True),
        lax.all_gather(low_out, ("ctx", "fsdp"), axis=0, tiled=True),
        lax.all_gather(low_fc, ("ctx", "fsdp"), axis=0, tiled=True),
        lax.all_gather(low_proj, ("ctx", "fsdp"), axis=0, tiled=True),
    )
    grad_output = cotangent[0]
    grad_output_f = grad_output.astype(jnp.float32)
    grad_w_proj = jnp.dot(act_three.T, grad_output, preferred_element_type=jnp.float32)
    grad_proj_bias = jnp.sum(grad_output_f, 0)
    grad_act = jnp.dot(grad_output, back_proj.T, preferred_element_type=jnp.float32)
    grad_hidden = gelu_back(grad_act)[0].astype(jnp.bfloat16)
    grad_w_fc = jnp.dot(act_two.T, grad_hidden, preferred_element_type=jnp.float32)
    grad_fc_bias = jnp.sum(grad_hidden.astype(jnp.float32), 0)
    grad_norm_two = jnp.dot(grad_hidden, back_fc.T, preferred_element_type=jnp.float32)
    grad_ln_two, grad_gain_two, grad_shift_two = ln_two_back(grad_norm_two)
    grad_x_two = grad_output_f + grad_ln_two
    grad_branch = grad_x_two.astype(jnp.bfloat16)
    grad_w_out = jnp.dot(heads.T, grad_branch, preferred_element_type=jnp.float32)
    grad_out_bias = jnp.sum(grad_branch.astype(jnp.float32), 0)
    grad_heads = jnp.dot(grad_branch, back_out.T, preferred_element_type=jnp.float32).astype(
        jnp.bfloat16
    )
    grad_head_groups = split_heads(grad_heads, group_count)

    def key_group(operands):
        query_blk, key_blk, value_blk, grad_blk, total_blk = operands
        scores = (
            jnp.einsum("hqd,hkd->hqk", query_blk, key_blk, preferred_element_type=jnp.float32)
            * 0.125
        )
        scores = jnp.where(visible, scores, -1000000000.0)
        attn_prob = jnp.exp(scores - total_blk[..., None])
        grad_prob = jnp.einsum(
            "hqd,hkd->hqk", grad_blk, value_blk, preferred_element_type=jnp.float32
        )
        delta_rows = jnp.sum(attn_prob * grad_prob, -1, keepdims=True)
        grad_scores = (attn_prob * (grad_prob - delta_rows)).astype(jnp.bfloat16)
        value_part = jnp.einsum(
            "hqk,hqd->hkd",
            attn_prob.astype(jnp.bfloat16),
            grad_blk,
            preferred_element_type=jnp.float32,
        )
        key_part = (
            jnp.einsum("hqk,hqd->hkd", grad_scores, query_blk, preferred_element_type=jnp.float32)
            * 0.125
        )
        query_part = (
            jnp.einsum("hqk,hkd->hqd", grad_scores, key_blk, preferred_element_type=jnp.float32)
            * 0.125
        )
        return (query_part, key_part, value_part)

    query_parts, key_parts, value_parts = lax.map(
        key_group, (query_groups, key_groups, value_groups, grad_head_groups, log_totals)
    )
    grad_query = join_heads(query_parts)
    pair_terms = jnp.concatenate([join_heads(key_parts), join_heads(value_parts)], 1)
    pair_sums = lax.psum_scatter(
        pair_terms.astype(jnp.bfloat16), "ctx", scatter_dimension=0, tiled=True
    ).astype(jnp.float32)
    grad_key = pair_sums[:, :width]
    grad_value = pair_sums[:, width:]
    grad_query = grad_query.astype(jnp.bfloat16)
    grad_key = grad_key.astype(jnp.bfloat16)
    grad_value = grad_value.astype(jnp.bfloat16)
    grad_mixed = jnp.concatenate([grad_query, grad_key, grad_value], 1)
    grad_w_qkv = jnp.dot(act_one.T, grad_mixed, preferred_element_type=jnp.float32)
    grad_q_bias = jnp.sum(grad_query.astype(jnp.float32), 0)
    grad_v_bias = jnp.sum(grad_value.astype(jnp.float32), 0)
    grad_norm_one = jnp.dot(grad_mixed, back_qkv.T, preferred_element_type=jnp.float32)
    grad_ln_one, grad_gain_one, grad_shift_one = ln_one_back(grad_norm_one)
    grad_inputs = grad_x_two + grad_ln_one
    grad_columns = jnp.stack(
        [
            grad_gain_one,
            grad_shift_one,
            grad_q_bias,
            grad_v_bias,
            grad_out_bias,
            grad_gain_two,
            grad_shift_two,
            grad_proj_bias,
        ],
        1,
    )
    grad_vec = jnp.concatenate([grad_columns, grad_fc_bias.reshape(-1, width).T], 1)
    sum_qkv, sum_out, sum_fc, sum_proj, sum_vec = (
        lax.psum_scatter(grad_w_qkv, ("ctx", "fsdp"), scatter_dimension=0, tiled=True),
        lax.psum_scatter(grad_w_out, ("ctx", "fsdp"), scatter_dimension=0, tiled=True),
        lax.psum_scatter(grad_w_fc, ("ctx", "fsdp"), scatter_dimension=0, tiled=True),
        lax.psum_scatter(grad_w_proj, ("ctx", "fsdp"), scatter_dimension=0, tiled=True),
        lax.psum_scatter(grad_vec, ("ctx", "fsdp"), scatter_dimension=0, tiled=True),
    )
    new_qkv = adam_update(w_qkv, qkv_m, qkv_v, sum_qkv, 0.1, 0.1)
    new_out = adam_update(w_out, out_m, out_v, sum_out, 0.3, 0.1)
    new_fc = adam_update(w_fc, fc_m, fc_v, sum_fc, 0.05, 0.1)
    new_proj = adam_update(w_proj, proj_m, proj_v, sum_proj, 0.03, 0.1)
    new_vec = adam_update(vectors, vec_m, vec_v, sum_vec, 0.5, 0.0)
    return (
        output[None],
        grad_inputs[None],
        new_qkv[0],
        new_qkv[1],
        new_qkv[2],
        new_out[0],
        new_out[1],
        new_out[2],
        new_fc[0],
        new_fc[1],
        new_fc[2],
        new_proj[0],
        new_proj[1],
        new_proj[2],
        new_vec[0],
        new_vec[1],
        new_vec[2],
    )


def solution(mesh):
    in_specs = (
        P("fsdp", "ctx", None),
        P("fsdp", "ctx", None),
        P(("ctx", "fsdp"), None),
        P(("ctx", "fsdp"), None),
        P(("ctx", "fsdp"), None),
        P(("ctx", "fsdp"), None),
        P(("ctx", "fsdp"), None),
        P(("ctx", "fsdp"), None),
        P(("ctx", "fsdp"), None),
        P(("ctx", "fsdp"), None),
        P(("ctx", "fsdp"), None),
        P(("ctx", "fsdp"), None),
        P(("ctx", "fsdp"), None),
        P(("ctx", "fsdp"), None),
        P(("ctx", "fsdp"), None),
        P(("ctx", "fsdp"), None),
        P(("ctx", "fsdp"), None),
    )
    out_specs = (
        P("fsdp", "ctx", None),
        P("fsdp", "ctx", None),
        P(("ctx", "fsdp"), None),
        P(("ctx", "fsdp"), None),
        P(("ctx", "fsdp"), None),
        P(("ctx", "fsdp"), None),
        P(("ctx", "fsdp"), None),
        P(("ctx", "fsdp"), None),
        P(("ctx", "fsdp"), None),
        P(("ctx", "fsdp"), None),
        P(("ctx", "fsdp"), None),
        P(("ctx", "fsdp"), None),
        P(("ctx", "fsdp"), None),
        P(("ctx", "fsdp"), None),
        P(("ctx", "fsdp"), None),
        P(("ctx", "fsdp"), None),
        P(("ctx", "fsdp"), None),
    )
    return jax.shard_map(shards, mesh=mesh, in_specs=in_specs, out_specs=out_specs, check_vma=False)
```

profile of v0, /device:TPU:29, one launch (start us, length us, event | category | flops | bytes accessed | tf_op | source)
XLA Modules:
  0.0 1706.2 jit_solution(8533595029417177290)
XLA Ops:
  12.5 59.3 %all-gather = bf16[128,6,12]{2,1,0:T(8,128)(2,1)S(1)} all-gather(bf16[1,6,12]{2,1,0:T(8,128)(2,1)S(1)} %convert_bitcast_fusion.4), channel_id=1, replica_groups=mesh['ctx'=32,'fsdp'=4] {'ctx','fsdp'}, dimensions={0}, use_global_device_ids=true | all-gather | bytes 18576 | tf_op jit(solution)/shard_map/all_gather | solution.py:78
  92.4 51.3 %all-gather.19.cloned.1.call-done = bf16[128,6,768]{2,1,0:T(8,128)(2,1)} async-done(((bf16[1,6,768]{2,1,0:T(8,128)(2,1)}), bf16[128,6,768]{2,1,0:T(8,128)(2,1)}) %all-gather.19.cloned.1.call-update) | async-done | bytes 1179664 | tf_op jit(solution)/shard_map/all_gather | solution.py:75
  148.0 65.0 %all-gather.21.cloned.1.call-done = bf16[128,6,3072]{2,1,0:T(8,128)(2,1)} async-done(((bf16[1,6,3072]{2,1,0:T(8,128)(2,1)}), bf16[128,6,3072]{2,1,0:T(8,128)(2,1)}) %all-gather.21.cloned.1.call-update) | async-done | bytes 4718608 | tf_op jit(solution)/shard_map/all_gather | solution.py:76
  220.8 42.7 %all-gather.11.cloned.1.call-done = bf16[4096,768]{1,0:T(8,128)(2,1)} async-done(((bf16[128,768]{1,0:T(8,128)(2,1)}), bf16[4096,768]{1,0:T(8,128)(2,1)}) %all-gather.11.cloned.1.call-update) | async-done | bytes 6291472 | tf_op jit(solution)/shard_map/all_gather | solution.py:101
  263.5 8.7 copy.65
  272.2 42.2 %all-gather.13.cloned.1.call-done = bf16[4096,768]{1,0:T(8,128)(2,1)} async-done(((bf16[128,768]{1,0:T(8,128)(2,1)}), bf16[4096,768]{1,0:T(8,128)(2,1)}) %all-gather.13.cloned.1.call-update) | async-done | bytes 6291472 | tf_op jit(solution)/shard_map/all_gather | solution.py:102
  314.3 8.8 copy.66
  323.1 30.7 %while.28 = (s32[]{:T(128)}, bf16[3,4,128,64]{2,3,1,0:T(8,128)(2,1)S(1)}, f32[3,4,128]{2,1,0:T(4,128)S(1)}, bf16[3,4,128,64]{2,3,1,0:T(8,128)(2,1)S(1)}, bf16[3,...) while((s32[]{:T(128)}, ...), condition=%wide.region_5.6_spmd.clone, body=%wide.region_2.5_spmd.clone.sunk | while | flops 562593280 | bytes 31607392 | solution.py:129
  364.1 212.0 %reduce-scatter.12.cloned.1.call-done = f32[24,768]{1,0:T(8,128)} async-done(((f32[3072,768]{1,0:T(8,128)}), f32[24,768]{1,0:T(8,128)}) %reduce-scatter.12.cloned.1.call-update) | async-done | bytes 73744 | tf_op jit(solution)/shard_map/reduce_scatter | solution.py:230
  578.3 68.0 %all-gather.15.cloned.1.call-done = bf16[3072,768]{1,0:T(8,128)(2,1)} async-done(((bf16[24,768]{1,0:T(8,128)(2,1)}), bf16[3072,768]{1,0:T(8,128)(2,1)}) %all-gather.15.cloned.1.call-update) | async-done | bytes 4718608 | tf_op jit(solution)/shard_map/all_gather | solution.py:77
  659.5 88.0 %while.29 = (s32[]{:T(128)}, bf16[3,4,128,64]{2,3,1,0:T(8,128)(2,1)S(1)}, bf16[3,4,4096,64]{2,3,1,0:T(8,128)(2,1)}, bf16[3,4,4096,64]{2,3,1,0:T(8,128)(2,1)}, bf...) while((s32[]{:T(128)}, ...), condition=%wide.region_12.13_spmd.clone, body=%wide.region_10.12_spmd.clone.sunk | while | flops 1362656768 | bytes 137772752 | solution.py:192
  662.8 9.8 multiply_reduce_fusion.5
  692.1 9.8 multiply_reduce_fusion.5
  721.4 9.8 multiply_reduce_fusion.5
  747.5 14.3 pad_maximum_fusion
  761.8 16.8 copy.71
  786.4 94.7 %reduce-scatter.14.cloned.1.call-done = bf16[128,1536]{1,0:T(8,128)(2,1)} async-done(((bf16[4096,1536]{1,0:T(8,128)(2,1)}), bf16[128,1536]{1,0:T(8,128)(2,1)}) %reduce-scatter.14.cloned.1.call-update) | async-done | bytes 393232
  886.5 339.3 %fusion.112 = (f32[8,2304]{1,0:T(8,128)S(1)}, f32[8,768]{1,0:T(8,128)S(1)}, f32[8,3072]{1,0:T(8,128)S(1)}) fusion(f32[768,2304]{1,0:T(8,128)} %fusion.88, f32[768,768]{1,0:T(8,128)} %fusion.121, f32[768,3072]{1,0:T(8,128)} %fusion.110), kind=kCustom, calls=%all-reduce-scatter.3 | all-reduce-scatter fusion | flops 6291457 | bytes 19070976
  1239.7 39.0 %collective-permute-start.56 = (f32[8,768]{1,0:T(8,128)S(1)}, f32[8,768]{1,0:T(8,128)S(1)}, u32[]{:S(2)}, u32[]{:S(2)}) collective-permute-start(f32[8,768]{1,0:T(8,128)S(1)} %get-tuple-element.241), channel_id=1, source_target_pairs={{0,25},{1,26},{2,27},{3,28},{4,29},{5,30},{6,31},{7,32},{8,33},{9,... | collective-permute-start | bytes 73736
  1432.6 16.4 collective-permute-done.95
  1464.3 81.2 %all-reduce.3 = f32[768,12]{0,1:T(8,128)S(1)} all-reduce(f32[768,12]{0,1:T(8,128)S(1)} %concatenate.13), channel_id=7, replica_groups=mesh['ctx'=32,'fsdp'=4] {'ctx','fsdp'}, use_global_device_ids=true, to_apply=%region_29.30.clone | all-reduce | flops 9216 | bytes 73728
  1578.7 27.2 %concatenate.15 = f32[262,768]{1,0:T(8,128)S(1)} concatenate(f32[6,768]{1,0:T(8,128)} %copy-done.89, f32[8,768]{1,0:T(8,128)} %copy-done.87, f32[8,768]{1,0:T(8,128)} %copy-done.88, f32[8,768]{1,0:T(8,128)} %copy-done.90, f32[8,768]{1,0:T(8,128)} %copy-done.91, f32[8,768]{1,0:T(8,128)} %copy-done.92, f32[8,768]{1,0:T(8,128)} %copy-done.93, f32[8,768]{1,0:T(8,128)} %copy-done.94, ...), dimensions={0} | concatenate | bytes 1609728
  1616.5 31.7 %concatenate.14 = f32[262,2304]{1,0:T(8,128)S(1)} concatenate(f32[6,2304]{1,0:T(8,128)} %copy-done.60, f32[8,2304]{1,0:T(8,128)S(1)} %collective-permute-done.30, f32[8,2304]{1,0:T(8,128)} %copy-done.58, f32[8,2304]{1,0:T(8,128)} %copy-done.59, f32[8,2304]{1,0:T(8,128)} %copy-done.61, f32[8,2304]{1,0:T(8,128)} %copy-done.62, f32[8,2304]{1,0:T(8,128)} %copy-done.63, ...), dimensions={0} | concatenate | bytes 4829184
  1664.2 33.3 %concatenate.16 = f32[262,3072]{1,0:T(8,128)S(1)} concatenate(f32[6,3072]{1,0:T(8,128)} %copy-done.29, f32[8,3072]{1,0:T(8,128)} %copy-done.28, f32[8,3072]{1,0:T(8,128)} %copy-done.30, f32[8,3072]{1,0:T(8,128)} %copy-done.31, f32[8,3072]{1,0:T(8,128)} %copy-done.32, f32[8,3072]{1,0:T(8,128)} %copy-done.33, f32[8,3072]{1,0:T(8,128)} %copy-done.34, f32[8,3072]{1,0:T(8,128)} %copy-done.35, ...), dimensions={0} | concatenate | bytes 6438912
  (603 shorter events, 407.1 us)
Async XLA Ops:
  7.2 71.6 %all-gather.17.cloned.1.call-start = ((), (), s32[]{:S(2)}) async-start(), calls=%async_computation.6 | async-start | bytes 4755456 | tf_op jit(solution)/shard_map/all_gather | solution.py:74
  8.8 134.9 %all-gather.19.cloned.1.call-start = ((), (), s32[]{:S(2)}) async-start(), calls=%async_computation.7 | async-start | bytes 1585152 | tf_op jit(solution)/shard_map/all_gather | solution.py:75
  10.2 202.9 %all-gather.21.cloned.1.call-start = ((), (), s32[]{:S(2)}) async-start(), calls=%async_computation.8 | async-start | bytes 6340608 | tf_op jit(solution)/shard_map/all_gather | solution.py:76
  11.8 251.7 %all-gather.11.cloned.1.call-start = ((), (), s32[]{:S(2)}) async-start(), calls=%async_computation.2 | async-start | bytes 6488064 | tf_op jit(solution)/shard_map/all_gather | solution.py:101
  87.5 226.9 %all-gather.13.cloned.1.call-start = ((), (), s32[]{:S(2)}) async-start(), calls=%async_computation.3 | async-start | bytes 6488064 | tf_op jit(solution)/shard_map/all_gather | solution.py:102
  89.5 486.7 %reduce-scatter.12.cloned.1.call-start = ((), (), s32[]{:S(2)}) async-start(), calls=%async_computation.5 | async-start | bytes 9510912 | tf_op jit(solution)/shard_map/reduce_scatter | solution.py:230
  364.1 282.2 %all-gather.15.cloned.1.call-start = ((), (), s32[]{:S(2)}) async-start(), calls=%async_computation.4 | async-start | bytes 4755456 | tf_op jit(solution)/shard_map/all_gather | solution.py:77
  577.8 303.3 %reduce-scatter.14.cloned.1.call-start = ((), (), s32[]{:S(2)}) async-start(), calls=%async_computation.9 | async-start | bytes 12976128
  1229.8 49.0 %collective-permute-start.60 = (f32[8,768]{1,0:T(8,128)S(1)}, f32[8,768]{1,0:T(8,128)S(1)}, u32[]{:S(2)}, u32[]{:S(2)}) collective-permute-start(f32[8,768]{1,0:T(8,128)S(1)} %get-tuple-element.241), channel_id=1, source_target_pairs={{0,29},{1,30},{2,31},{3,32},{4,33},{5,34},{6,35},{7,36},{8,37},{9,... | collective-permute-start | bytes 73736
  1231.1 49.6 %collective-permute-start.59 = (f32[8,768]{1,0:T(8,128)S(1)}, f32[8,768]{1,0:T(8,128)S(1)}, u32[]{:S(2)}, u32[]{:S(2)}) collective-permute-start(f32[8,768]{1,0:T(8,128)S(1)} %get-tuple-element.241), channel_id=1, source_target_pairs={{0,28},{1,29},{2,30},{3,31},{4,32},{5,33},{6,34},{7,35},{8,36},{9,... | collective-permute-start | bytes 73736
  1237.1 46.0 %collective-permute-start.58 = (f32[8,768]{1,0:T(8,128)S(1)}, f32[8,768]{1,0:T(8,128)S(1)}, u32[]{:S(2)}, u32[]{:S(2)}) collective-permute-start(f32[8,768]{1,0:T(8,128)S(1)} %get-tuple-element.241), channel_id=1, source_target_pairs={{0,27},{1,28},{2,29},{3,30},{4,31},{5,32},{6,33},{7,34},{8,35},{9,... | collective-permute-start | bytes 73736
  1238.4 47.4 %collective-permute-start.57 = (f32[8,768]{1,0:T(8,128)S(1)}, f32[8,768]{1,0:T(8,128)S(1)}, u32[]{:S(2)}, u32[]{:S(2)}) collective-permute-start(f32[8,768]{1,0:T(8,128)S(1)} %get-tuple-element.241), channel_id=1, source_target_pairs={{0,26},{1,27},{2,28},{3,29},{4,30},{5,31},{6,32},{7,33},{8,34},{9,... | collective-permute-start | bytes 73736
  1239.7 49.2 %collective-permute-start.56 = (f32[8,768]{1,0:T(8,128)S(1)}, f32[8,768]{1,0:T(8,128)S(1)}, u32[]{:S(2)}, u32[]{:S(2)}) collective-permute-start(f32[8,768]{1,0:T(8,128)S(1)} %get-tuple-element.241), channel_id=1, source_target_pairs={{0,25},{1,26},{2,27},{3,28},{4,29},{5,30},{6,31},{7,32},{8,33},{9,... | collective-permute-start | bytes 73736
  1453.4 92.1 %collective-permute-start.88 = (f32[8,3072]{1,0:T(8,128)S(1)}, f32[8,3072]{1,0:T(8,128)S(1)}, u32[]{:S(2)}, u32[]{:S(2)}) collective-permute-start(f32[8,3072]{1,0:T(8,128)S(1)} %get-tuple-element.242), channel_id=1, source_target_pairs={{0,25},{1,26},{2,27},{3,28},{4,29},{5,30},{6,31},{7,32},{8,33},{9,... | collective-permute-start | bytes 294920
  1455.3 93.0 %collective-permute-start.87 = (f32[8,3072]{1,0:T(8,128)S(1)}, f32[8,3072]{1,0:T(8,128)S(1)}, u32[]{:S(2)}, u32[]{:S(2)}) collective-permute-start(f32[8,3072]{1,0:T(8,128)S(1)} %get-tuple-element.242), channel_id=1, source_target_pairs={{0,24},{1,25},{2,26},{3,27},{4,28},{5,29},{6,30},{7,31},{8,32},{9,... | collective-permute-start | bytes 294920
  1457.3 94.1 %collective-permute-start.86 = (f32[8,3072]{1,0:T(8,128)S(1)}, f32[8,3072]{1,0:T(8,128)S(1)}, u32[]{:S(2)}, u32[]{:S(2)}) collective-permute-start(f32[8,3072]{1,0:T(8,128)S(1)} %get-tuple-element.242), channel_id=1, source_target_pairs={{0,23},{1,24},{2,25},{3,26},{4,27},{5,28},{6,29},{7,30},{8,31},{9,... | collective-permute-start | bytes 294920
  1459.2 94.1 %collective-permute-start.85 = (f32[8,3072]{1,0:T(8,128)S(1)}, f32[8,3072]{1,0:T(8,128)S(1)}, u32[]{:S(2)}, u32[]{:S(2)}) collective-permute-start(f32[8,3072]{1,0:T(8,128)S(1)} %get-tuple-element.242), channel_id=1, source_target_pairs={{0,22},{1,23},{2,24},{3,25},{4,26},{5,27},{6,28},{7,29},{8,30},{9,... | collective-permute-start | bytes 294920
  1461.2 94.1 %collective-permute-start.84 = (f32[8,3072]{1,0:T(8,128)S(1)}, f32[8,3072]{1,0:T(8,128)S(1)}, u32[]{:S(2)}, u32[]{:S(2)}) collective-permute-start(f32[8,3072]{1,0:T(8,128)S(1)} %get-tuple-element.242), channel_id=1, source_target_pairs={{0,21},{1,22},{2,23},{3,24},{4,25},{5,26},{6,27},{7,28},{8,29},{9,... | collective-permute-start | bytes 294920
  1557.4 48.5 %collective-permute-start.78 = (f32[8,3072]{1,0:T(8,128)S(1)}, f32[8,3072]{1,0:T(8,128)S(1)}, u32[]{:S(2)}, u32[]{:S(2)}) collective-permute-start(f32[8,3072]{1,0:T(8,128)S(1)} %get-tuple-element.242), channel_id=1, source_target_pairs={{0,15},{1,16},{2,17},{3,18},{4,19},{5,20},{6,21},{7,22},{8,23},{9,... | collective-permute-start | bytes 294920
  1559.3 48.5 %collective-permute-start.77 = (f32[8,3072]{1,0:T(8,128)S(1)}, f32[8,3072]{1,0:T(8,128)S(1)}, u32[]{:S(2)}, u32[]{:S(2)}) collective-permute-start(f32[8,3072]{1,0:T(8,128)S(1)} %get-tuple-element.242), channel_id=1, source_target_pairs={{0,14},{1,15},{2,16},{3,17},{4,18},{5,19},{6,20},{7,21},{8,22},{9,... | collective-permute-start | bytes 294920
  1562.3 47.5 %collective-permute-start.76 = (f32[8,3072]{1,0:T(8,128)S(1)}, f32[8,3072]{1,0:T(8,128)S(1)}, u32[]{:S(2)}, u32[]{:S(2)}) collective-permute-start(f32[8,3072]{1,0:T(8,128)S(1)} %get-tuple-element.242), channel_id=1, source_target_pairs={{0,13},{1,14},{2,15},{3,16},{4,17},{5,18},{6,19},{7,20},{8,21},{9,... | collective-permute-start | bytes 294920
  1565.3 46.4 %collective-permute-start.75 = (f32[8,3072]{1,0:T(8,128)S(1)}, f32[8,3072]{1,0:T(8,128)S(1)}, u32[]{:S(2)}, u32[]{:S(2)}) collective-permute-start(f32[8,3072]{1,0:T(8,128)S(1)} %get-tuple-element.242), channel_id=1, source_target_pairs={{0,12},{1,13},{2,14},{3,15},{4,16},{5,17},{6,18},{7,19},{8,20},{9,... | collective-permute-start | bytes 294920
  1607.9 43.0 %collective-permute-start.72 = (f32[8,3072]{1,0:T(8,128)S(1)}, f32[8,3072]{1,0:T(8,128)}, u32[]{:S(2)}, u32[]{:S(2)}) collective-permute-start(f32[8,3072]{1,0:T(8,128)S(1)} %get-tuple-element.242), channel_id=1, source_target_pairs={{0,9},{1,10},{2,11},{3,12},{4,13},{5,14},{6,15},{7,16},{8,17},{9,1... | collective-permute-start | bytes 294920
  1613.7 45.0 %collective-permute-start.69 = (f32[8,3072]{1,0:T(8,128)S(1)}, f32[8,3072]{1,0:T(8,128)}, u32[]{:S(2)}, u32[]{:S(2)}) collective-permute-start(f32[8,3072]{1,0:T(8,128)S(1)} %get-tuple-element.242), channel_id=1, source_target_pairs={{0,6},{1,7},{2,8},{3,9},{4,10},{5,11},{6,12},{7,13},{8,14},{9,15},... | collective-permute-start | bytes 294920
  (222 other events, 11483.0 us)
Sparse Core Ops, SparseCore 0:
  11.4 67.2 all-gather.16
  82.1 61.5 all-gather.18
  147.4 65.6 all-gather.20
  215.1 48.2 all-gather.10
  266.2 48.1 all-gather.12
  364.2 211.9 reduce-scatter.11
  579.6 66.6 all-gather.14
  778.8 102.3 reduce-scatter.13
where the time goes:
time: 1740 us; the launch traced here: 1710 us
  waiting for transfers between devices  629 us (36%)
  blocking collectives  480 us (28%)
  starting transfers between devices  227 us (13%)
  local copies, waits for them, and re-layouts  162 us (9%)
  matrix products  124 us (7%)
  other arithmetic  67 us (4%)
  between operations  17.6 us (1%)
    unnamed x2, blocking collectives  421 us
    unnamed x97, starting transfers between devices  227 us
    reduce_scatter x1, waiting for transfers between devices, shards(): lax.psum_scatter(grad_w_proj, ('ctx', 'fsdp'), scatter_dimension=0, tiled...  212 us
    unnamed x105, waiting for transfers between devices  145 us
    unnamed x278, local copies, waits for them, and re-layouts  132 us
    all_gather x1, waiting for transfers between devices, shards(): lax.all_gather(low_proj, ('ctx', 'fsdp'), axis=0, tiled=True)  68 us
    all_gather x1, waiting for transfers between devices, shards(): lax.all_gather(low_fc, ('ctx', 'fsdp'), axis=0, tiled=True)  65 us
    all_gather x1, blocking collectives, shards(): lax.all_gather(low_vec, ('ctx', 'fsdp'), axis=0, tiled=True)  59.3 us
  transfers between devices with their start and end apart: 104, of which 26 were waited for; matrix products, arithmetic and copies ran while one was open for 7% of the time, Pallas kernels for 0%

commit v1 on v0

v1 whole, which is shorter than its diff:
```python
import jax
import jax.numpy as jnp
from jax import lax
from jax.experimental import pallas as pl
from jax.experimental.pallas import tpu as pltpu
from jax.sharding import PartitionSpec as P

STEP = 10
EPSILON = 1e-05
BETA_ONE = 0.9
BETA_TWO = 0.999
ADAM_EPSILON = 1e-08
MESH = pl.DeviceIdType.MESH
BF = jnp.bfloat16
F32 = jnp.float32
ANY = pl.BlockSpec(memory_space=pl.ANY)
VMEM = pl.BlockSpec(memory_space=pltpu.VMEM)
LIMIT = 56 * 1024 * 1024


def coords():
    c = lax.axis_index("ctx")
    return c // 8, (c // 2) % 4, c % 2, lax.axis_index("fsdp")


def device(y, z, k, x):
    return ((y * 4 + z) * 2 + k, x)


def ring(v, step):
    return lax.rem(v + step, 4)


def greet(devices):
    barrier = pltpu.get_barrier_semaphore()
    for one in devices:
        pl.semaphore_signal(barrier, inc=1, device_id=one, device_id_type=MESH)
    pl.semaphore_wait(barrier, len(devices))


def remote(src, dst, send, recv, to):
    return pltpu.make_async_remote_copy(
        src, dst, send, recv, device_id=to, device_id_type=MESH
    )


def comm(kernel, outs, cid, sems, args, scratch=(), spaces=None, name=None):
    return pl.pallas_call(
        kernel,
        out_shape=outs,
        in_specs=[ANY] * len(args) if spaces is None else spaces[0],
        out_specs=[ANY] * len(outs) if spaces is None else spaces[1],
        scratch_shapes=list(scratch) + [pltpu.SemaphoreType.DMA((n,)) for n in sems],
        compiler_params=pltpu.CompilerParams(
            collective_id=cid, has_side_effects=True, vmem_limit_bytes=LIMIT
        ),
        name=name,
    )(*args)


def first_gather(w_qkv, w_fc, w_out, w_proj, vectors, rows):
    width = 4736

    def kernel(
        wq_ref, wf_ref, wo_ref, wp_ref, wv_ref, r_ref,
        q_out, f_out, o_out, p_out, ro_ref,
        wide, packed, got, fc48, qkv48, out48, proj_wide, q_send, f_send, o_send, p_send,
        ms, mr, fs, fr, s1, r1, s2, r2, ps, pr, xs_s, xs_r, xf_s, xf_r, rs, rr, cs, cr, loc,
    ):
        y, z, k, x = coords()
        me = y * 4 + z
        sib = device(y, z, 1 - k, x)
        steps = (1, 2, 3)
        greet(
            [sib]
            + [device(y, z, k, ring(x, d)) for d in steps]
            + [
                device(ring(y, a), ring(z, b), k, x)
                for a in range(4)
                for b in range(4)
                if (a, b) != (0, 0)
            ]
        )
        own_r = pltpu.make_async_copy(r_ref, ro_ref.at[k, z], loc.at[0])
        own_r.start()
        row_copies = []
        for d in steps:
            c = remote(
                r_ref, ro_ref.at[k, z], rs.at[d], rr.at[d], device(y, ring(z, d), k, x)
            )
            row_copies.append(c)
        wide[...] = jnp.zeros_like(wide)
        wide[0:6, 0:3072] = wf_ref[...]
        wide[6:12, 0:2304] = wq_ref[...]
        wide[6:12, 2304:3072] = wo_ref[...]
        wide[0:12, 3072:3840] = wp_ref[0:12]
        wide[0:12, 3840:4608] = wp_ref[12:24]
        wide[0:6, 4608:4620] = wv_ref[...]
        t = k * 4 + x
        packed[...] = wide[...].astype(BF)
        got[t] = packed[...]
        message = []
        for d in steps:
            c = remote(packed, got.at[t], ms.at[d], mr.at[d], device(y, z, k, ring(x, d)))
            c.start()
            message.append(c)
        c = remote(packed, got.at[t], fs.at[0], fr.at[0], sib)
        c.start()
        forward = [c]
        for c in row_copies:
            c.start()
        c = remote(r_ref, ro_ref.at[k, z], cs.at[0], cr.at[0], sib)
        c.start()
        row_forward = [c]
        for d in steps:
            message[d - 1].wait_recv()
            src = k * 4 + ring(x, 4 - d)
            f = remote(got.at[src], got.at[src], fs.at[d], fr.at[d], sib)
            f.start()
            forward.append(f)
        for f in forward:
            f.wait_recv()
        for i in range(8):
            piece = got[i].astype(F32)
            at = slice(6 * i, 6 * i + 6)
            fc48[at] = piece[0:6, 0:3072]
            qkv48[at] = piece[6:12, 0:2304]
            out48[at, 0:768] = piece[6:12, 2304:3072]
            out48[at, 768:896] = piece[0:6, 4608:4736]
            proj_wide[24 * i : 24 * i + 12] = piece[0:12, 3072:3840]
            proj_wide[24 * i + 12 : 24 * i + 24] = piece[0:12, 3840:4608]
        for j in range(4):
            q_send[j, :, 0:192] = qkv48[:, 192 * j : 192 * j + 192].astype(BF)
            q_send[j, :, 192:384] = qkv48[:, 768 + 192 * j : 960 + 192 * j].astype(BF)
            q_send[j, :, 384:576] = qkv48[:, 1536 + 192 * j : 1728 + 192 * j].astype(BF)
            q_send[j, :, 576:640] = out48[:, 768:832].astype(BF)
        for j in range(8):
            f_send[j] = fc48[:, 384 * j : 384 * j + 384].astype(BF)
        o_send[0] = out48[:, 0:384].astype(BF)
        o_send[1] = out48[:, 384:768].astype(BF)
        p_send[...] = proj_wide[...].astype(BF)

        group = pl.ds(pl.multiple_of(16 * jnp.minimum(x, 2), 16), 16)

        def to_of(m):
            return ring(y, m // 4), ring(z, m % 4)

        def q_copy(m):
            ty, tz = to_of(m)
            return remote(
                q_send.at[tz, group], q_out.at[me, group], s1.at[m], r1.at[m],
                device(ty, tz, k, x),
            )

        def f_copy(m):
            ty, tz = to_of(m)
            return remote(
                f_send.at[tz * 2 + k], f_out.at[me], s2.at[m], r2.at[m], device(ty, tz, k, x)
            )

        def o_copy(m):
            ty, tz = to_of(m)
            return remote(o_send.at[k], o_out.at[me], s2.at[m], r2.at[m], device(ty, tz, k, x))

        def p_copy(a):
            return remote(
                p_send, p_out.at[z % 2], ps.at[a], pr.at[z % 2], device(ring(y, a), y, k, x)
            )

        def each(copy, what):
            def step(m, carry):
                what(copy(m))
                return carry

            lax.fori_loop(1, 16, step, 0)

        start = lambda c: c.start()
        finish = lambda c: c.wait()

        @pl.when(x < 3)
        def _():
            each(q_copy, start)
            c = pltpu.make_async_copy(q_send.at[z, group], q_out.at[me, group], loc.at[1])
            c.start()
            c.wait()

        @pl.when(x == 1)
        def _():
            each(f_copy, start)
            c = pltpu.make_async_copy(f_send.at[z * 2 + k], f_out.at[me], loc.at[2])
            c.start()
            c.wait()

        @pl.when(x == 2)
        def _():
            each(o_copy, start)
            c = pltpu.make_async_copy(o_send.at[k], o_out.at[me], loc.at[2])
            c.start()
            c.wait()

        @pl.when((x == 3) & (k == z // 2))
        def _():
            for a in range(1, 4):
                p_copy(a).start()

            @pl.when(z != y)
            def _():
                p_copy(0).start()

            @pl.when(z == y)
            def _():
                c = pltpu.make_async_copy(p_send, p_out.at[z % 2], loc.at[2])
                c.start()
                c.wait()

        half = pl.ds(8 * k, 8)
        other_half = pl.ds(8 * (1 - k), 8)

        def rows_of(plane):
            return pl.ds(pl.multiple_of(16 * plane, 16), 16)

        @pl.when(x < 3)
        def _():
            each(q_copy, finish)
            for d in steps:
                remote(
                    q_out.at[half, group], q_out.at[half, group], xs_s.at[d], xs_r.at[x],
                    device(y, z, k, ring(x, d)),
                ).start()

        def pass_on(a):
            return remote(
                q_out.at[half, rows_of(a)], q_out.at[half, rows_of(a)], xf_s.at[a], xf_r.at[a], sib
            )

        for a in range(3):

            @pl.when(x != a)
            def _():
                remote(
                    q_out.at[half, rows_of(a)], q_out.at[half, rows_of(a)], xs_s.at[0],
                    xs_r.at[a], sib,
                ).wait_recv()
                pass_on(a).start()

        for d in steps:
            row_copies[d - 1].wait_recv()
            src = ring(z, 4 - d)
            f = remote(ro_ref.at[k, src], ro_ref.at[k, src], cs.at[d], cr.at[d], sib)
            f.start()
            row_forward.append(f)

        @pl.when(x == 1)
        def _():
            each(f_copy, finish)

        @pl.when(x == 2)
        def _():
            each(o_copy, finish)

        @pl.when((x == 3) & (k == z // 2))
        def _():
            for a in range(1, 4):
                p_copy(a).wait_send()

            @pl.when(z != y)
            def _():
                p_copy(0).wait_send()

        for j in range(2):
            @pl.when((x == 3) & jnp.logical_not((y == z) & (z == 2 * k + j)))
            def _():
                remote(p_send, p_out.at[j], ps.at[0], pr.at[j], sib).wait_recv()

        @pl.when(x < 3)
        def _():
            for d in steps:
                remote(
                    q_out.at[half, group], q_out.at[half, group], xs_s.at[d], xs_r.at[x],
                    device(y, z, k, ring(x, d)),
                ).wait_send()

        for a in range(3):

            @pl.when(x != a)
            def _():
                pass_on(a).wait_send()
                remote(
                    q_out.at[other_half, rows_of(a)], q_out.at[other_half, rows_of(a)],
                    xf_s.at[a], xf_r.at[a], sib,
                ).wait_recv()

        for c in message + row_copies + forward:
            c.wait_send()
        for c in row_forward:
            c.wait()
        own_r.wait()

    return comm(
        kernel,
        [
            jax.ShapeDtypeStruct((16, 48, 640), BF),
            jax.ShapeDtypeStruct((16, 48, 384), BF),
            jax.ShapeDtypeStruct((16, 48, 384), BF),
            jax.ShapeDtypeStruct((2, 192, 768), BF),
            jax.ShapeDtypeStruct((2, 4) + rows.shape, BF),
        ],
        0,
        (4, 4, 4, 4, 16, 16, 16, 16, 4, 2, 4, 4, 4, 4, 4, 4, 4, 4, 3),
        (w_qkv, w_fc, w_out, w_proj, vectors, rows),
        scratch=[
            pltpu.VMEM((16, width), F32),
            pltpu.VMEM((16, width), BF),
            pltpu.VMEM((8, 16, width), BF),
            pltpu.VMEM((48, 3072), F32),
            pltpu.VMEM((48, 2304), F32),
            pltpu.VMEM((48, 896), F32),
            pltpu.VMEM((192, 768), F32),
            pltpu.VMEM((4, 48, 640), BF),
            pltpu.VMEM((8, 48, 384), BF),
            pltpu.VMEM((2, 48, 384), BF),
            pltpu.VMEM((192, 768), BF),
        ],
        spaces=([VMEM] * 5 + [ANY], [ANY] * 5),
        name="first_gather",
    )


def kv_gather(kv, rows, fc, out, proj):
    def kernel(
        v_ref, r_ref, f_ref, o_ref, p_ref, vo_ref, ro_ref, fo_ref, oo_ref, po_ref,
        vs, vr, rs, rr, cs, cr, ds, dr, ws, wr, os, orr, loc,
    ):
        y, z, k, x = coords()
        sib = device(y, z, 1 - k, x)
        ys = [(d, ring(y, d)) for d in (1, 2, 3)]
        zs = [(d, ring(z, d)) for d in (1, 2, 3)]
        greet(
            [sib]
            + [device(b, z, k, x) for _, b in ys]
            + [device(y, b, k, x) for _, b in zs]
            + [device(y, z, k, ring(x, d)) for d in (1, 2, 3)]
        )
        own = [
            pltpu.make_async_copy(v_ref, vo_ref.at[y, k], loc.at[0]),
            pltpu.make_async_copy(r_ref, ro_ref.at[k, z], loc.at[1]),
        ]
        for c in own:
            c.start()
        kv_copies, row_copies, forward = [], [], []
        for d, b in ys:
            c = remote(v_ref, vo_ref.at[y, k], vs.at[d], vr.at[d], device(b, z, k, x))
            c.start()
            kv_copies.append(c)
        for d, b in zs:
            c = remote(r_ref, ro_ref.at[k, z], rs.at[d], rr.at[d], device(y, b, k, x))
            c.start()
            row_copies.append(c)

        weights = ((1, f_ref, fo_ref), (2, o_ref, oo_ref.at[k]), (3, p_ref, po_ref))

        def weight_copy(a, d):
            _, src, dst = weights[a - 1]
            return remote(src, dst, ws.at[d], wr.at[a], device(y, z, k, ring(x, d)))

        for a in (1, 2, 3):

            @pl.when(x == a)
            def _():
                for d in (1, 2, 3):
                    weight_copy(a, d).start()
                _, src, dst = weights[a - 1]
                c = pltpu.make_async_copy(src, dst, loc.at[2])
                c.start()
                c.wait()

        c = remote(v_ref, vo_ref.at[y, k], cs.at[0], cr.at[0], sib)
        c.start()
        forward.append(c)
        c = remote(r_ref, ro_ref.at[k, z], ds.at[0], dr.at[0], sib)
        c.start()
        forward.append(c)
        for c, (d, b) in zip(row_copies, zs):
            c.wait_recv()
            src = ring(z, 4 - d)
            f = remote(ro_ref.at[k, src], ro_ref.at[k, src], ds.at[d], dr.at[d], sib)
            f.start()
            forward.append(f)
        for c, (d, b) in zip(kv_copies, ys):
            c.wait_recv()
            src = ring(y, 4 - d)
            f = remote(vo_ref.at[src, k], vo_ref.at[src, k], cs.at[d], cr.at[d], sib)
            f.start()
            forward.append(f)
        for a in (2, 1, 3):

            @pl.when(x != a)
            def _():
                weight_copy(a, 1).wait_recv()

            if a == 2:
                c = remote(oo_ref.at[k], oo_ref.at[k], os.at[0], orr.at[0], sib)
                c.start()
                forward.append(c)
        for a in (1, 2, 3):

            @pl.when(x == a)
            def _():
                for d in (1, 2, 3):
                    weight_copy(a, d).wait_send()

        for c in kv_copies + row_copies:
            c.wait_send()
        for c in forward:
            c.wait()
        for c in own:
            c.wait()

    return comm(
        kernel,
        [
            jax.ShapeDtypeStruct((4, 2) + kv.shape, BF),
            jax.ShapeDtypeStruct((2, 4) + rows.shape, BF),
            jax.ShapeDtypeStruct((16, 48, 384), BF),
            jax.ShapeDtypeStruct((2, 16, 48, 384), BF),
            jax.ShapeDtypeStruct((2, 192, 768), BF),
        ],
        2,
        (4, 4, 4, 4, 4, 4, 4, 4, 4, 4, 1, 1, 3),
        (kv, rows, fc, out, proj),
        name="kv_gather",
    )


def heads_gather(heads):
    def kernel(h_ref, ho_ref, hs, hr, cs, cr, loc):
        y, z, k, x = coords()
        sib = device(y, z, 1 - k, x)
        zs = [(d, ring(z, d)) for d in (1, 2, 3)]
        greet([sib] + [device(y, b, k, x) for _, b in zs])
        own = pltpu.make_async_copy(h_ref, ho_ref.at[z, k], loc.at[0])
        own.start()
        copies = []
        for d, b in zs:
            c = remote(h_ref, ho_ref.at[z, k], hs.at[d], hr.at[d], device(y, b, k, x))
            c.start()
            copies.append(c)
        c = remote(h_ref, ho_ref.at[z, k], cs.at[0], cr.at[0], sib)
        c.start()
        forward = [c]
        for c, (d, b) in zip(copies, zs):
            c.wait_recv()
            src = ring(z, 4 - d)
            f = remote(ho_ref.at[src, k], ho_ref.at[src, k], cs.at[d], cr.at[d], sib)
            f.start()
            forward.append(f)
        for c in copies:
            c.wait_send()
        for c in forward:
            c.wait()
        own.wait()

    return comm(
        kernel,
        [jax.ShapeDtypeStruct((4, 2) + heads.shape, BF)],
        3,
        (4, 4, 4, 4, 1),
        (heads,),
        name="heads_gather",
    )[0]


def z_gather(rows):
    def kernel(r_ref, ro_ref, rs, rr, loc):
        y, z, k, x = coords()
        zs = [(d, ring(z, d)) for d in (1, 2, 3)]
        greet([device(y, b, k, x) for _, b in zs])
        own = pltpu.make_async_copy(r_ref, ro_ref.at[z], loc.at[0])
        own.start()
        copies = []
        for d, b in zs:
            c = remote(r_ref, ro_ref.at[z], rs.at[d], rr.at[d], device(y, b, k, x))
            c.start()
            copies.append(c)
        for c in copies:
            c.wait()
        own.wait()

    return comm(
        kernel,
        [jax.ShapeDtypeStruct((4,) + rows.shape, BF)],
        4,
        (4, 4, 1),
        (rows,),
        name="z_gather",
    )[0]


def group_sum(parts, cid, name):
    n = parts.shape[0]
    rows, cols = parts.shape[3:]

    def kernel(p_ref, o_ref, got, mine, far, cs, cr, zs, zr):
        y, z, k, x = coords()
        sib = device(y, z, 1 - k, x)
        ring_z = [(d, ring(z, d)) for d in (1, 2, 3)]
        greet([sib] + [device(y, b, k, x) for _, b in ring_z])
        order = ring_z + [(0, z)]
        pairs = []
        for i in range(n):
            for d, b in order:
                c = remote(
                    p_ref.at[i, 1 - k, b], got.at[i, b], cs.at[4 * i + d], cr.at[4 * i + d], sib
                )
                c.start()
                pairs.append(c)
        copies = []
        for i in range(n):
            for d, b in order:
                pairs[4 * i + (d - 1) % 4].wait_recv()
                total = p_ref[i, k, b].astype(F32) + got[i, b].astype(F32)
                if d == 0:
                    o_ref[i] = total
                else:
                    mine[i, d - 1] = total.astype(BF)
                    c = remote(
                        mine.at[i, d - 1],
                        far.at[i, d - 1],
                        zs.at[3 * i + d - 1],
                        zr.at[3 * i + d - 1],
                        device(y, b, k, x),
                    )
                    c.start()
                    copies.append(c)
        for i in range(n):
            for d in range(3):
                copies[3 * i + d].wait_recv()
            o_ref[i] = (
                o_ref[i] + far[i, 0].astype(F32) + far[i, 1].astype(F32) + far[i, 2].astype(F32)
            )
        for c in copies:
            c.wait_send()
        for c in pairs:
            c.wait_send()

    return comm(
        kernel,
        [jax.ShapeDtypeStruct((n, rows, cols), F32)],
        cid,
        (4 * n, 4 * n, 3 * n, 3 * n),
        (parts,),
        scratch=[
            pltpu.VMEM((n, 4, rows, cols), BF),
            pltpu.VMEM((n, 3, rows, cols), BF),
            pltpu.VMEM((n, 3, rows, cols), BF),
        ],
        spaces=([VMEM], [VMEM]),
        name=name,
    )[0]


def kv_sum(parts, fc, proj):
    rows, cols = parts.shape[2:]

    def kernel(
        p_ref, f_ref, w_ref, o_ref, fo_ref, wo_ref, got, mine, far, f_far, w_far,
        cs, cr, ys, yr, fs, fr, ws, wr,
    ):
        y, z, k, x = coords()
        sib = device(y, z, 1 - k, x)
        ring_y = [(d, ring(y, d)) for d in (1, 2, 3)]
        greet(
            [sib]
            + [device(b, z, k, x) for _, b in ring_y]
            + [device(y, z, k, ring(x, d)) for d in (1, 2, 3)]
        )
        order = ring_y + [(0, y)]
        pairs = []
        for d, b in order:
            c = remote(p_ref.at[b, 1 - k], got.at[b], cs.at[d], cr.at[b], sib)
            c.start()
            pairs.append(c)
        weights = []
        for d in (1, 2, 3):
            b = ring(x, d)
            to = device(y, z, k, b)
            weights.append(
                remote(f_ref.at[:, b], f_far.at[d - 1], fs.at[d - 1], fr.at[d - 1], to)
            )
            weights.append(
                remote(w_ref.at[:, b], w_far.at[d - 1], ws.at[d - 1], wr.at[d - 1], to)
            )
        for c in weights:
            c.start()
        copies = []
        for i, (d, b) in enumerate(order):
            pairs[i].wait_recv()
            total = p_ref[b, k].astype(F32) + got[b].astype(F32)
            if d == 0:
                o_ref[...] = total
            else:
                mine[d - 1] = total.astype(BF)
                c = remote(
                    mine.at[d - 1], far.at[d - 1], ys.at[d - 1], yr.at[d - 1], device(b, z, k, x)
                )
                c.start()
                copies.append(c)
        for c in weights:
            c.wait()
        fo_ref[...] = (
            f_ref[:, x].astype(F32)
            + f_far[0].astype(F32)
            + f_far[1].astype(F32)
            + f_far[2].astype(F32)
        ).astype(BF)
        wo_ref[...] = (
            w_ref[:, x].astype(F32)
            + w_far[0].astype(F32)
            + w_far[1].astype(F32)
            + w_far[2].astype(F32)
        ).astype(BF)
        for c in copies:
            c.wait_recv()
        o_ref[...] = (
            o_ref[...] + far[0].astype(F32) + far[1].astype(F32) + far[2].astype(F32)
        )
        for c in copies:
            c.wait_send()
        for c in pairs:
            c.wait_send()

    return comm(
        kernel,
        [
            jax.ShapeDtypeStruct((rows, cols), F32),
            jax.ShapeDtypeStruct((4, 48, 384), BF),
            jax.ShapeDtypeStruct((2, 48, 768), BF),
        ],
        5,
        (4, 4, 3, 3, 3, 3, 3, 3),
        (parts, fc, proj),
        scratch=[
            pltpu.VMEM((4, rows, cols), BF),
            pltpu.VMEM((3, rows, cols), BF),
            pltpu.VMEM((3, rows, cols), BF),
            pltpu.VMEM((3, 4, 48, 384), BF),
            pltpu.VMEM((3, 2, 48, 768), BF),
        ],
        spaces=([VMEM] * 3, [VMEM] * 3),
        name="kv_sum",
    )


def last_sums(one, mix, vec, fc, proj):
    wide = 3200

    def kernel(
        one_ref, mix_ref, vec_ref, fc_ref, proj_ref, one_out, rows_out, proj_out,
        one_far, mix_got, mix_sum, mix_far, vec_far, mix_mine, vec_mine,
        mix_all, fc_all, vec_all, proj_all, proj_sum, out_send,
        zs, zr, cs, cr, s1, r1, s2, r2, s3, r3, s4, r4, s5, r5, s6, r6, s7, r7, s8, r8, loc,
    ):
        y, z, k, x = coords()
        me = y * 4 + z
        sib = device(y, z, 1 - k, x)
        steps = (1, 2, 3)
        greet(
            [sib]
            + [device(y, z, j, ring(x, d)) for d in steps for j in (k, 1 - k)]
            + [
                device(ring(y, a), ring(z, b), k, x)
                for a in range(4)
                for b in range(4)
                if (a, b) != (0, 0)
            ]
        )
        mine_at = pl.ds(pl.multiple_of(384 * k, 128), 384)
        other_at = pl.ds(pl.multiple_of(384 * (1 - k), 128), 384)
        swap = []
        for d in (1, 2, 3, 0):
            b = ring(x, d)
            c = remote(mix_ref.at[:, b, :, other_at], mix_got.at[b], cs.at[d], cr.at[d], sib)
            c.start()
            swap.append(c)
        along = []
        for d in steps:
            b = ring(x, d)
            to = device(y, z, k, b)
            c = remote(vec_ref.at[:, b], vec_far.at[d - 1], s2.at[d - 1], r2.at[d - 1], to)
            c.start()
            along.append(c)
            swap[d - 1].wait_recv()
            mix_sum[d] = (
                mix_ref[:, b, :, mine_at].astype(F32) + mix_got[b].astype(F32)
            ).astype(BF)
            c = remote(mix_sum.at[d], mix_far.at[d - 1], s1.at[d - 1], r1.at[d - 1], to)
            c.start()
            along.append(c)
        ones = []
        for d in steps:
            c = remote(
                one_ref.at[ring(z, d)], one_far.at[d - 1], zs.at[d - 1], zr.at[d - 1],
                device(y, ring(z, d), k, x),
            )
            c.start()
            ones.append(c)

        def plane(src, dst, send, recv, a):
            return remote(src.at[a], dst.at[me], send.at[a], recv.at[me], device(a, x, k, x))

        def all_start(src, dst, send, recv):
            for a in range(4):
                here = (a == y) & (z == x)

                @pl.when(jnp.logical_not(here))
                def _():
                    plane(src, dst, send, recv, a).start()

                @pl.when(here)
                def _():
                    c = pltpu.make_async_copy(src.at[a], dst.at[me], loc.at[0])
                    c.start()
                    c.wait()

        def all_finish(src, dst, send, recv):
            for a in range(4):

                @pl.when(jnp.logical_not((a == y) & (z == x)))
                def _():
                    plane(src, dst, send, recv, a).wait_send()

        def all_receive(src, dst, send, recv):
            def step(i, carry):
                @pl.when(i != me)
                def _():
                    remote(src.at[0], dst.at[i], send.at[0], recv.at[i], sib).wait_recv()

                return carry

            lax.fori_loop(0, 16, step, 0)

        all_start(fc_ref, fc_all, s4, r4)

        def proj_copy(j):
            return remote(
                proj_ref.at[j], proj_all.at[y], s6.at[j], r6.at[y], device(z, 2 * k + j, k, x)
            )

        for j in range(2):
            here = (y == z) & (z == 2 * k + j)

            @pl.when(jnp.logical_not(here))
            def _():
                proj_copy(j).start()

            @pl.when(here)
            def _():
                c = pltpu.make_async_copy(proj_ref.at[j], proj_all.at[y], loc.at[1])
                c.start()
                c.wait()

        swap[3].wait_recv()
        for c in along:
            c.wait_recv()
        mix_mine[...] = (
            mix_ref[:, x, :, mine_at].astype(F32)
            + mix_got[x].astype(F32)
            + mix_far[0].astype(F32)
            + mix_far[1].astype(F32)
            + mix_far[2].astype(F32)
        ).astype(BF)
        vec_mine[...] = (
            vec_ref[:, x].astype(F32)
            + vec_far[0].astype(F32)
            + vec_far[1].astype(F32)
            + vec_far[2].astype(F32)
        ).astype(BF)
        all_start(mix_mine, mix_all, s3, r3)
        all_start(vec_mine, vec_all, s5, r5)
        for c in ones:
            c.wait_recv()
        one_out[...] = (
            one_ref[z].astype(F32)
            + one_far[0].astype(F32)
            + one_far[1].astype(F32)
            + one_far[2].astype(F32)
        )

        def proj_last(i):
            return remote(
                proj_sum.at[i], proj_out, s8.at[i], r8.at[0],
                device(y, z, x // 2, lax.rem(2 * x + i, 4)),
            )

        def proj_here(i):
            return (k == x // 2) & (x == lax.rem(2 * x + i, 4))

        holder = k == z // 2
        for a in range(4):

            @pl.when(holder & jnp.logical_not((a == y) & (z == y)))
            def _():
                remote(proj_ref.at[0], proj_all.at[a], s6.at[0], r6.at[a], sib).wait_recv()

        @pl.when(holder)
        def _():
            total = (
                proj_all[0].astype(F32)
                + proj_all[1].astype(F32)
                + proj_all[2].astype(F32)
                + proj_all[3].astype(F32)
            )
            for i in range(2):
                proj_sum[i] = total[24 * i : 24 * i + 24]

                @pl.when(jnp.logical_not(proj_here(i)))
                def _():
                    proj_last(i).start()

                @pl.when(proj_here(i))
                def _():
                    c = pltpu.make_async_copy(proj_sum.at[i], proj_out, loc.at[2])
                    c.start()
                    c.wait()

        def last_copy(i):
            return remote(
                out_send.at[i], rows_out.at[k], s7.at[i], r7.at[k], device(y, z, i // 4, i % 4)
            )

        def last_here(i):
            return k * 4 + x == i

        @pl.when(z == x)
        def _():
            all_receive(fc_ref, fc_all, s4, r4)
            all_receive(mix_mine, mix_all, s3, r3)
            all_receive(vec_mine, vec_all, s5, r5)

            def four(ref, b):
                return (
                    ref[b].astype(F32)
                    + ref[4 + b].astype(F32)
                    + ref[8 + b].astype(F32)
                    + ref[12 + b].astype(F32)
                )

            for b in range(4):
                m, f = four(mix_all, b), four(fc_all, b)
                for i in range(8):
                    rows = slice(6 * i, 6 * i + 6)
                    out_send[i, 0:6, 384 * b : 384 * b + 384] = m[rows]
                    out_send[i, 0:6, 1536 + 384 * b : 1920 + 384 * b] = f[rows]
            v = four(vec_all, 0) + four(vec_all, 1) + four(vec_all, 2) + four(vec_all, 3)
            for i in range(8):
                out_send[i, 0:6, 3072:3200] = v[6 * i : 6 * i + 6]
                out_send[i, 6:8, :] = jnp.zeros((2, wide), F32)
            for i in range(8):

                @pl.when(jnp.logical_not(last_here(i)))
                def _():
                    last_copy(i).start()

                @pl.when(last_here(i))
                def _():
                    c = pltpu.make_async_copy(out_send.at[i], rows_out.at[k], loc.at[3])
                    c.start()
                    c.wait()

        for j in range(2):

            @pl.when(jnp.logical_not((z == x) & (k == j)))
            def _():
                remote(out_send.at[0], rows_out.at[j], s7.at[0], r7.at[j], sib).wait_recv()

        @pl.when(jnp.logical_not((k == z // 2) & (x == (4 * k + x) // 2)))
        def _():
            remote(proj_sum.at[0], proj_out, s8.at[0], r8.at[0], sib).wait_recv()

        @pl.when(z == x)
        def _():
            for i in range(8):

                @pl.when(jnp.logical_not(last_here(i)))
                def _():
                    last_copy(i).wait_send()

        for i in range(2):

            @pl.when(holder & jnp.logical_not(proj_here(i)))
            def _():
                proj_last(i).wait_send()

        for j in range(2):

            @pl.when(jnp.logical_not((y == z) & (z == 2 * k + j)))
            def _():
                proj_copy(j).wait_send()

        all_finish(fc_ref, fc_all, s4, r4)
        all_finish(mix_mine, mix_all, s3, r3)
        all_finish(vec_mine, vec_all, s5, r5)
        for c in swap + along + ones:
            c.wait_send()

    return comm(
        kernel,
        [
            jax.ShapeDtypeStruct((128, 768), F32),
            jax.ShapeDtypeStruct((2, 8, wide), F32),
            jax.ShapeDtypeStruct((24, 768), F32),
        ],
        6,
        (3, 3, 4, 4, 3, 3, 3, 3, 4, 16, 4, 16, 4, 16, 2, 4, 8, 2, 2, 1, 4),
        (one, mix, vec, fc, proj),
        scratch=[
            pltpu.VMEM((3, 128, 768), BF),
            pltpu.VMEM((4, 4, 48, 384), BF),
            pltpu.VMEM((4, 4, 48, 384), BF),
            pltpu.VMEM((3, 4, 48, 384), BF),
            pltpu.VMEM((3, 4, 48, 128), BF),
            pltpu.VMEM((4, 48, 384), BF),
            pltpu.VMEM((4, 48, 128), BF),
            pltpu.VMEM((16, 48, 384), BF),
            pltpu.VMEM((16, 48, 384), BF),
            pltpu.VMEM((16, 48, 128), BF),
            pltpu.VMEM((4, 48, 768), BF),
            pltpu.VMEM((2, 24, 768), F32),
            pltpu.VMEM((8, 8, wide), F32),
        ],
        spaces=([VMEM] * 5, [VMEM] * 3),
        name="last_sums",
    )


def head_rows(matrix, head):
    row = lax.broadcasted_iota(jnp.int32, matrix.shape, 0)
    keep = (row >= 64 * head) & (row < 64 * head + 64)
    return jnp.where(keep, matrix, jnp.zeros_like(matrix))


def head_cols(matrix, head):
    col = lax.broadcasted_iota(jnp.int32, matrix.shape, 1)
    keep = (col >= 64 * head) & (col < 64 * head + 64)
    return jnp.where(keep, matrix, jnp.zeros_like(matrix))


def place(index):
    return (index // 128) * 256 + index % 128


def dot(a, b):
    return jnp.dot(a, b, preferred_element_type=F32)


def attend(query, kv_all):
    def kernel(q_ref, kv_ref, h_ref, ot_ref, lse_ref, qt, m_ref, l_ref):
        y, z, k, x = coords()
        q_t = q_ref[...].T
        for head in range(3):
            qt[head] = head_rows(q_t, head)
        m_ref[...] = jnp.full_like(m_ref, -1e30)
        l_ref[...] = jnp.zeros_like(l_ref)
        ot_ref[...] = jnp.zeros_like(ot_ref)

        def block(by, bk, masked):
            keys = kv_ref[by, bk, :, :192]
            values_t = kv_ref[by, bk, :, 192:].T
            if masked:
                key_at = place(lax.broadcasted_iota(jnp.int32, (512, 512), 0)) + 128 * bk
                query_at = place(lax.broadcasted_iota(jnp.int32, (512, 512), 1)) + 128 * k
                visible = query_at >= key_at
            for head in range(3):
                s = dot(keys, qt[head])
                if masked:
                    s = jnp.where(visible, s, -1e9)
                old = m_ref[head : head + 1]
                new = jnp.maximum(old, jnp.max(s, 0, keepdims=True))
                e = jnp.exp(s - new)
                scale = jnp.exp(old - new)
                m_ref[head : head + 1] = new
                l_ref[head : head + 1] = l_ref[head : head + 1] * scale + jnp.sum(
                    e, 0, keepdims=True
                )
                rows = slice(64 * head, 64 * head + 64)
                ot_ref[rows] = ot_ref[rows] * scale + dot(values_t[rows], e.astype(BF))

        def step(j, carry):
            block(j // 2, j % 2, False)
            return carry

        lax.fori_loop(0, 2 * y, step, 0)
        block(y, 0, True)
        block(y, 1, True)
        for head in range(3):
            rows = slice(64 * head, 64 * head + 64)
            total = l_ref[head : head + 1]
            ot_ref[rows] = ot_ref[rows] / total
            lse_ref[head : head + 1] = m_ref[head : head + 1] + jnp.log(total)
        h_ref[...] = ot_ref[...].T.astype(BF)

    return pl.pallas_call(
        kernel,
        out_shape=[
            jax.ShapeDtypeStruct((512, 192), BF),
            jax.ShapeDtypeStruct((192, 512), F32),
            jax.ShapeDtypeStruct((8, 512), F32),
        ],
        in_specs=[VMEM] * 2,
        out_specs=[VMEM] * 3,
        scratch_shapes=[
            pltpu.VMEM((3, 192, 512), BF),
            pltpu.VMEM((8, 512), F32),
            pltpu.VMEM((8, 512), F32),
        ],
        compiler_params=pltpu.CompilerParams(vmem_limit_bytes=LIMIT),
        name="attend",
    )(query, kv_all)


def attend_back(query, grad_heads, kv_all, out_t, lse):
    def kernel(q_ref, g_ref, kv_ref, ot_ref, lse_ref, dq_ref, dkv_ref, qt, gt, qm, gm, delta, dqt):
        y, z, k, x = coords()
        query_blk, grad_blk = q_ref[...], g_ref[...]
        q_t, g_t = query_blk.T, grad_blk.T
        for head in range(3):
            rows = slice(64 * head, 64 * head + 64)
            qt[head] = head_rows(q_t, head)
            gt[head] = head_rows(g_t, head)
            qm[head] = head_cols(query_blk, head)
            gm[head] = head_cols(grad_blk, head)
            delta[head : head + 1] = jnp.sum(
                g_t[rows].astype(F32) * ot_ref[rows], 0, keepdims=True
            )
        dqt[...] = jnp.zeros_like(dqt)

        def block(by, bk, masked):
            keys = kv_ref[by, bk, :, :192]
            values = kv_ref[by, bk, :, 192:]
            keys_t = keys.T
            if masked:
                key_at = place(lax.broadcasted_iota(jnp.int32, (512, 512), 0)) + 128 * bk
                query_at = place(lax.broadcasted_iota(jnp.int32, (512, 512), 1)) + 128 * k
                visible = query_at >= key_at
            dk = dv = None
            for head in range(3):
                s = dot(keys, qt[head])
                p = jnp.exp(s - lse_ref[head : head + 1])
                if masked:
                    p = jnp.where(visible, p, 0.0)
                dp = dot(values, gt[head])
                ds = (p * (dp - delta[head : head + 1])).astype(BF)
                pv = dot(p.astype(BF), gm[head])
                pk = dot(ds, qm[head])
                dv = pv if dv is None else dv + pv
                dk = pk if dk is None else dk + pk
                rows = slice(64 * head, 64 * head + 64)
                dqt[rows] += dot(keys_t[rows], ds)
            dkv_ref[by, bk, :, :192] = dk.astype(BF)
            dkv_ref[by, bk, :, 192:] = dv.astype(BF)

        def step(j, carry):
            block(j // 2, j % 2, False)
            return carry

        def clear(j, carry):
            dkv_ref[j // 2, j % 2] = jnp.zeros((512, 384), BF)
            return carry

        lax.fori_loop(0, 2 * y, step, 0)
        block(y, 0, True)
        block(y, 1, True)
        lax.fori_loop(2 * y + 2, 8, clear, 0)
        dq_ref[...] = (dqt[...].T * 0.125).astype(BF)

    return pl.pallas_call(
        kernel,
        out_shape=[
            jax.ShapeDtypeStruct((512, 192), BF),
            jax.ShapeDtypeStruct((4, 2, 512, 384), BF),
        ],
        in_specs=[VMEM] * 5,
        out_specs=[VMEM] * 2,
        scratch_shapes=[
            pltpu.VMEM((3, 192, 512), BF),
            pltpu.VMEM((3, 192, 512), BF),
            pltpu.VMEM((3, 512, 192), BF),
            pltpu.VMEM((3, 512, 192), BF),
            pltpu.VMEM((8, 512), F32),
            pltpu.VMEM((192, 512), F32),
        ],
        compiler_params=pltpu.CompilerParams(vmem_limit_bytes=LIMIT),
        name="attend_back",
    )(query, grad_heads, kv_all, out_t, lse)


def normalize(rows):
    centered = rows - jnp.mean(rows, -1, keepdims=True)
    inverse = lax.rsqrt(jnp.mean(centered * centered, -1, keepdims=True) + EPSILON)
    return centered * inverse, inverse


def normalize_back(normed, inverse, gain, grad):
    scaled = grad * gain
    return inverse * (
        scaled
        - jnp.mean(scaled, -1, keepdims=True)
        - normed * jnp.mean(scaled * normed, -1, keepdims=True)
    )


def gelu_tanh(values):
    return (
        0.5
        * values
        * (1.0 + jnp.tanh(0.7978845608028654 * (values + 0.044715 * values * values * values)))
    )


def adam_update(weight, moment_one, moment_two, gradient, rate, decay):
    new_one = BETA_ONE * moment_one + (1.0 - BETA_ONE) * gradient
    new_two = BETA_TWO * moment_two + (1.0 - BETA_TWO) * gradient * gradient
    fix_one = 1.0 - BETA_ONE**STEP
    fix_two = 1.0 - BETA_TWO**STEP
    direction = new_one / fix_one / (jnp.sqrt(new_two / fix_two) + ADAM_EPSILON)
    return (weight - rate * (direction + decay * weight), new_one, new_two)


def shards(
    tokens,
    cotangent,
    w_qkv,
    qkv_m,
    qkv_v,
    w_out,
    out_m,
    out_v,
    w_fc,
    fc_m,
    fc_v,
    w_proj,
    proj_m,
    proj_v,
    vectors,
    vec_m,
    vec_v,
):
    y, z, k, x = coords()
    wq, fc_part, out_part, proj_part, x_group = first_gather(
        w_qkv, w_fc, w_out, w_proj, vectors, tokens[0]
    )
    wq = wq.reshape(768, 640)
    vec = wq[:, 576:588].astype(F32)
    wq = wq[:, :576]
    gain_one, shift_one, q_bias, v_bias = vec[:, 0], vec[:, 1], vec[:, 2], vec[:, 3]
    out_bias, gain_two, shift_two, proj_bias = vec[:, 4], vec[:, 5], vec[:, 6], vec[:, 7]
    fc_bias = lax.dynamic_slice(vec[:, 8:].T.reshape(-1), ((2 * z + k) * 384,), (384,))
    bias = jnp.concatenate(
        [
            lax.dynamic_slice(q_bias, (192 * z,), (192,)),
            jnp.zeros((192,), F32),
            lax.dynamic_slice(v_bias, (192 * z,), (192,)),
        ]
    )
    x_core = lax.dynamic_index_in_dim(x_group, k, 0, False).reshape(512, 768).astype(F32)
    normed_core, _ = normalize(x_core)
    act_one = (normed_core * gain_one + shift_one).astype(BF)
    mixed = (dot(act_one, wq) + bias).astype(BF)
    query = mixed[:, :192] * jnp.asarray(0.125, BF)
    kv_all, dy_group, wf, wo, wp = kv_gather(
        mixed[:, 192:], cotangent[0], fc_part, out_part, proj_part
    )
    wf = wf.reshape(768, 384)
    wo = jnp.concatenate([wo[0].reshape(768, 384), wo[1].reshape(768, 384)], 1)
    wp = wp.reshape(384, 768)
    heads, out_t, lse = attend(query, kv_all)
    heads_all = heads_gather(heads)
    heads_all = jnp.concatenate([heads_all[i].reshape(1024, 192) for i in range(4)], 1)
    x_two = x_group.reshape(1024, 768).astype(F32) + dot(heads_all, wo) + out_bias
    normed_two, inverse_two = normalize(x_two)
    act_two = (normed_two * gain_two + shift_two).astype(BF)
    hidden = dot(act_two, wf) + fc_bias
    gelu_out, gelu_back = jax.vjp(gelu_tanh, hidden)
    act_three = gelu_out.astype(BF)
    dy = dy_group.reshape(1024, 768)
    result_part = dot(act_three, wp).astype(BF)
    grad_w_proj = dot(act_three.T, dy)
    grad_hidden = gelu_back(dot(dy, wp.T))[0].astype(BF)
    grad_w_fc = dot(act_two.T, grad_hidden)
    grad_fc_bias = jnp.sum(grad_hidden.astype(F32), 0)
    norm_part = dot(grad_hidden, wf.T).astype(BF)
    sums = group_sum(
        jnp.stack([norm_part, result_part]).reshape(2, 2, 4, 128, 768), 8, "ffn_sum"
    )

    def own(group):
        return lax.dynamic_slice(group, ((k * 4 + z) * 128, 0), (128, group.shape[1]))

    own_x_two = own(x_two)
    output = own_x_two + sums[1] + proj_bias
    own_normed, own_inverse = normalize(own_x_two)
    grad_output = cotangent[0].astype(F32)
    grad_norm_two = sums[0]
    grad_x_two = grad_output + normalize_back(own_normed, own_inverse, gain_two, grad_norm_two)
    grad_branch = grad_x_two.astype(BF)
    branch_core = z_gather(grad_branch).reshape(512, 768)
    wo_rows = lax.dynamic_slice(wo, (192 * z, 0), (192, 768))
    grad_heads = dot(branch_core, wo_rows.T).astype(BF)
    grad_query, kv_parts = attend_back(query, grad_heads, kv_all, out_t, lse)
    grad_kv, fc_sum, proj_sum = kv_sum(
        kv_parts,
        grad_w_fc.astype(BF).reshape(4, 4, 48, 384),
        grad_w_proj.astype(BF).reshape(2, 4, 48, 768),
    )
    grad_mixed = jnp.concatenate([grad_query, grad_kv.astype(BF)], 1)
    branch_cols = lax.dynamic_slice(branch_core, (0, 192 * z), (512, 192))
    heads_core = lax.dynamic_index_in_dim(heads_all.reshape(2, 512, 768), k, 0, False)
    left = jnp.concatenate([act_one, heads_core], 0)
    gap = jnp.zeros((512, 96), BF)
    room = jnp.zeros((512, 288), BF)
    right = jnp.concatenate(
        [
            jnp.concatenate([grad_mixed[:, :288], gap, grad_mixed[:, 288:], gap], 1),
            jnp.concatenate([room, branch_cols[:, :96], room, branch_cols[:, 96:]], 1),
        ],
        0,
    )
    grad_mix = dot(left.T, right).astype(BF)
    one_part = dot(grad_mixed, wq.T)

    def spread(piece, at, size):
        return lax.dynamic_update_slice(jnp.zeros((size,), F32), piece, (at,))

    mixed_sums = jnp.sum(grad_mixed.astype(F32), 0)
    columns = jnp.stack(
        [
            jnp.sum(one_part * normed_core, 0),
            jnp.sum(one_part, 0),
            spread(mixed_sums[:192], 192 * z, 768),
            spread(mixed_sums[384:], 192 * z, 768),
            jnp.sum(grad_branch.astype(F32), 0),
            jnp.sum(grad_norm_two * own_normed, 0),
            jnp.sum(grad_norm_two, 0),
            jnp.sum(grad_output, 0),
        ]
        + list(spread(grad_fc_bias, (2 * z + k) * 384, 3072).reshape(4, 768)),
        1,
    )
    grad_vec = jnp.pad(columns, ((0, 0), (0, 116))).astype(BF)
    grad_norm_one, last_rows, sum_proj = last_sums(
        one_part.astype(BF).reshape(4, 128, 768),
        grad_mix.reshape(4, 4, 48, 768),
        grad_vec.reshape(4, 4, 48, 128),
        fc_sum,
        proj_sum,
    )
    normed_one, inverse_one = normalize(tokens[0].astype(F32))
    grad_inputs = grad_x_two + normalize_back(normed_one, inverse_one, gain_one, grad_norm_one)
    last_rows = last_rows[:, :6]
    mix_rows = last_rows[:, :, :1536].reshape(2, 6, 4, 384)
    sum_qkv = (
        mix_rows[..., :288]
        .transpose(1, 2, 0, 3)
        .reshape(6, 4, 3, 192)
        .transpose(0, 2, 1, 3)
        .reshape(6, 2304)
    )
    sum_out = mix_rows[..., 288:].transpose(1, 2, 0, 3).reshape(6, 768)
    sum_fc = last_rows[:, :, 1536:3072].reshape(2, 6, 4, 384).transpose(1, 2, 0, 3).reshape(6, 3072)
    sum_vec = last_rows[0, :, 3072:3084] + last_rows[1, :, 3072:3084]
    new_qkv = adam_update(w_qkv, qkv_m, qkv_v, sum_qkv, 0.1, 0.1)
    new_out = adam_update(w_out, out_m, out_v, sum_out, 0.3, 0.1)
    new_fc = adam_update(w_fc, fc_m, fc_v, sum_fc, 0.05, 0.1)
    new_proj = adam_update(w_proj, proj_m, proj_v, sum_proj, 0.03, 0.1)
    new_vec = adam_update(vectors, vec_m, vec_v, sum_vec, 0.5, 0.0)
    return (output[None], grad_inputs[None], *new_qkv, *new_out, *new_fc, *new_proj, *new_vec)


def solution(mesh):
    split = P("fsdp", "ctx", None)
    rows = P(("ctx", "fsdp"), None)
    return jax.shard_map(
        shards,
        mesh=mesh,
        in_specs=(split, split) + (rows,) * 15,
        out_specs=(split, split) + (rows,) * 15,
        check_vma=False,
    )
```

time: 1740 us -> 314 us (0.18); the launches traced: 1710 us -> 314 us
  waiting for transfers between devices: 629 us -> 0 us
  blocking collectives: 480 us -> 0 us
  Pallas kernels: 0 us -> 252 us
  starting transfers between devices: 227 us -> 0 us
  local copies, waits for them, and re-layouts: 162 us -> 14.8 us
  matrix products: 124 us -> 19.8 us
  other arithmetic: 67 us -> 25.7 us
    unnamed x2 -> x0, blocking collectives: 421 us -> none
    all_gather x6 -> x0, waiting for transfers between devices: 272 us -> none  [the longest x1 68 us: shards(): lax.all_gather(low_proj, ('ctx', 'fsdp'), axis=0, tiled=True)]
    pallas_call x0 -> x9, Pallas kernels: none -> 252 us  [the longest x7 213 us: comm(): pl.pallas_call(kernel, out_shape=outs, in_specs=[ANY] * len(args) if spac...]
    unnamed x97 -> x0, starting transfers between devices: 227 us -> none
    reduce_scatter x1 -> x0, waiting for transfers between devices: 212 us -> none  [shards(): lax.psum_scatter(grad_w_proj, ('ctx', 'fsdp'), scatter_dimension=0, tiled...]
    unnamed x105 -> x0, waiting for transfers between devices: 145 us -> none
    unnamed x278 -> x104, local copies, waits for them, and re-layouts: 132 us -> 2.01 us
    dot_general x33 -> x11, matrix products: 124 us -> 19.8 us  [dot(): return jnp.dot(a, b, preferred_element_type=F32)]
  transfers between devices with their start and end apart: 104 -> 0, of which waited for: 26 -> 0; matrix products, arithmetic and copies ran while one was open for 7% -> 0% of each run, Pallas kernels for 0% -> 0%
where the time goes in v1:
time: 314 us
  Pallas kernels  252 us (80%)
  other arithmetic  25.7 us (8%)
  matrix products  19.8 us (6%)
  local copies, waits for them, and re-layouts  14.8 us (5%)
    pallas_call x7, Pallas kernels, comm(): pl.pallas_call(kernel, out_shape=outs, in_specs=[ANY] * len(args) if spac...  213 us
    pallas_call x1, Pallas kernels, attend_back(): pl.pallas_call(kernel, out_shape=[jax.ShapeDtypeStruct((512, 192), BF), j...  21.9 us
    dot_general x11, matrix products, dot(): return jnp.dot(a, b, preferred_element_type=F32)  19.8 us
    pallas_call x1, Pallas kernels, attend(): pl.pallas_call(kernel, out_shape=[jax.ShapeDtypeStruct((512, 192), BF), j...  16.9 us

profile of v1, /device:TPU:29, one launch (start us, length us, event | category | flops | bytes accessed | tf_op | source)
XLA Modules:
  0.0 313.7 jit_solution(3889090817397308059)
XLA Ops:
  5.0 36.9 %first_gather.1 = (bf16[16,48,640]{2,1,0:T(8,128)(2,1)}, bf16[16,48,384]{2,1,0:T(8,128)(2,1)}, bf16[16,48,384]{2,1,0:T(8,128)(2,1)}, bf16[2,192,768]{2,1,0:T(8,128)(2,1)}, bf16[2,4,128,768]{3,2,1,0:T(8,128)(2,1)}) custom-call(f32[6,2304]{1,0:T(8,128)} %wq_ref.1, f32[6,3072]{1,0:T(8,128)} %wf_ref.1, f32[6,768]{1,0:T(8,128)} %wo_ref.1, f32[24,768]{1,0:T(8,128)} %wp_ref.1, ...), custom_call_target="tpu_custom_call" | custom-call | tf_op jit(solution)/shard_map/first_gather/pallas_call | solution.py:48
  43.4 1.6 multiply_reduce_fusion.2
  49.5 44.9 %kv_gather.1 = (bf16[4,2,512,384]{3,2,1,0:T(8,128)(2,1)}, bf16[2,4,128,768]{3,2,1,0:T(8,128)(2,1)}, bf16[16,48,384]{2,1,0:T(8,128)(2,1)}, bf16[2,16,48,384]{3,2,1,0:T(8,128)(2,1)}, bf16[2,192,768]{2,1,0:T(8,128)(2,1)}) custom-call(bf16[512,384]{1,0:T(8,128)(2,1)} %slice.152.v_ref, bf16[128,768]{1,0:T(8,128)(2,1)} %bitcast.114, ...), custom_call_target="tpu_custom_call" | custom-call | tf_op jit(solution)/shard_map/kv_gather/pallas_call | solution.py:48
  95.8 16.9 %attend.1 = (bf16[512,192]{1,0:T(8,128)(2,1)}, f32[192,512]{1,0:T(8,128)}, f32[8,512]{1,0:T(8,128)}) custom-call(bf16[512,192]{1,0:T(8,128)(2,1)} %slice_multiply_fusion.q_ref, bf16[4,2,512,384]{3,2,1,0:T(8,128)(2,1)} %get-tuple-element.43.kv_ref), custom_call_target="tpu_custom_call" | custom-call | tf_op jit(solution)/shard_map/attend/pallas_call | solution.py:1002
  112.7 18.1 %heads_gather.1 = bf16[4,2,512,192]{3,2,1,0:T(8,128)(2,1)} custom-call(bf16[512,192]{1,0:T(8,128)(2,1)} %get-tuple-element.44.h_ref), custom_call_target="tpu_custom_call" | custom-call | tf_op jit(solution)/shard_map/heads_gather/pallas_call | solution.py:48
  130.8 1.9 slice_bitcast_fusion.3
  134.4 1.7 fusion.90
  139.4 1.8 convolution_convert_fusion.2
  141.3 2.0 convert_reduce_fusion
  143.3 2.4 convolution_convert_fusion
  145.7 1.9 convolution_convert_fusion.3
  149.5 2.3 convolution_convert_fusion.1
  151.8 2.0 pad_maximum_fusion.p_ref
  153.8 25.5 %ffn_sum.1 = f32[2,128,768]{2,1,0:T(8,128)} custom-call(bf16[2,2,4,128,768]{4,3,2,1,0:T(8,128)(2,1)} %pad_maximum_fusion.p_ref), custom_call_target="tpu_custom_call" | custom-call | tf_op jit(solution)/shard_map/ffn_sum/pallas_call | solution.py:48
  181.0 2.0 fusion.58
  183.1 1.7 fusion.84
  184.7 12.0 %z_gather.1 = bf16[4,128,768]{2,1,0:T(8,128)(2,1)} custom-call(bf16[128,768]{1,0:T(8,128)(2,1)} %get-tuple-element.90.r_ref), custom_call_target="tpu_custom_call" | custom-call | tf_op jit(solution)/shard_map/z_gather/pallas_call | solution.py:48
  196.8 1.5 convolution_convert_fusion.4
  200.4 21.9 %attend_back.1 = (bf16[512,192]{1,0:T(8,128)(2,1)}, bf16[4,2,512,384]{3,2,1,0:T(8,128)(2,1)}) custom-call(bf16[512,192]{1,0:T(8,128)(2,1)} %slice_multiply_fusion.q_ref, bf16[512,192]{1,0:T(8,128)(2,1)} %copy.61.g_ref, bf16[4,2,512,384]{3,2,1,0:T(8,128)(2,1)} %get-tuple-element.43.kv_ref, f32[192,512]{1,0:T(8,128)} %get-tuple-element.49.ot_ref, ...), custom_call_target="tpu_custom_call" | custom-call | tf_op jit(solution)/shard_map/attend_back/pallas_call | solution.py:1076
  222.2 27.4 %kv_sum.1 = (f32[512,384]{1,0:T(8,128)}, bf16[4,48,384]{2,1,0:T(8,128)(2,1)}, bf16[2,48,768]{2,1,0:T(8,128)(2,1)}) custom-call(bf16[4,2,512,384]{3,2,1,0:T(8,128)(2,1)} %get-tuple-element.52.p_ref, bf16[4,4,48,384]{3,2,1,0:T(8,128)(2,1)} %bitcast.121, bf16[2,4,48,768]{3,2,1,0:T(8,128)(2,1)} %bitcast.120), custom_call_target="tpu_custom_call" | custom-call | tf_op jit(solution)/shard_map/kv_sum/pallas_call | solution.py:48
  251.0 1.8 fusion.76
  254.2 2.6 fusion.34
  257.7 48.1 %last_sums.1 = (f32[128,768]{1,0:T(8,128)}, f32[2,8,3200]{2,1,0:T(8,128)}, f32[24,768]{1,0:T(8,128)}) custom-call(bf16[4,128,768]{2,1,0:T(8,128)(2,1)} %bitcast.119, bf16[4,4,48,768]{3,2,1,0:T(8,128)(2,1)} %bitcast.117, bf16[4,4,48,128]{3,2,1,0:T(8,128)(2,1)} %bitcast.118, bf16[4,48,384]{2,1,0:T(8,128)(2,1)} %get-tuple-element.54.fc_ref, ...), custom_call_target="tpu_custom_call" | custom-call | tf_op jit(solution)/shard_map/last_sums/pallas_call | solution.py:48
  307.3 2.0 fusion.55
  (188 shorter events, 31.2 us)
Async XLA Ops:
  41.9 4.6 %copy-start.2 = (bf16[2,4,128,768]{3,2,1,0:T(8,128)(2,1)S(1)}, bf16[2,4,128,768]{3,2,1,0:T(8,128)(2,1)}, u32[]{:S(2)}) copy-start(bf16[2,4,128,768]{3,2,1,0:T(8,128)(2,1)} %get-tuple-element.38) | copy-start | bytes 4718596
  43.4 3.5 %copy-start.37 = (f32[512]{0:T(512)}, f32[512]{0:T(512)S(1)}, u32[]{:S(2)}) copy-start(f32[512]{0:T(512)S(1)} %get-tuple-element.118) | copy-start | bytes 6148
  43.4 3.5 %copy-start.27 = (bf16[16,48,640]{2,1,0:T(8,128)(2,1)S(1)}, bf16[16,48,640]{2,1,0:T(8,128)(2,1)}, u32[]{:S(2)}) copy-start(bf16[16,48,640]{2,1,0:T(8,128)(2,1)} %get-tuple-element.39) | copy-start | bytes 2949124
  95.8 38.1 %copy-start.5 = (bf16[1,16,48,384]{3,2,1,0:T(8,128)(2,1)}, bf16[1,16,48,384]{3,2,1,0:T(8,128)(2,1)S(1)}, u32[]{:S(2)}) copy-start(bf16[1,16,48,384]{3,2,1,0:T(8,128)(2,1)S(1)} %get-tuple-element.102) | copy-start | bytes 1769476
  95.8 38.1 %copy-start.7 = (bf16[1,16,48,384]{3,2,1,0:T(8,128)(2,1)}, bf16[1,16,48,384]{3,2,1,0:T(8,128)(2,1)S(1)}, u32[]{:S(2)}) copy-start(bf16[1,16,48,384]{3,2,1,0:T(8,128)(2,1)S(1)} %get-tuple-element.103) | copy-start | bytes 1769476
  136.4 44.6 %copy-start.46 = (f32[128]{0:T(128)}, f32[128]{0:T(128)S(1)}, u32[]{:S(2)}) copy-start(f32[128]{0:T(128)S(1)} %add_rsqrt_fusion.2) | copy-start | bytes 1540
  147.8 4.1 %copy-start.10 = (bf16[1024,768]{1,0:T(8,128)(2,1)S(1)}, bf16[1024,768]{1,0:T(8,128)(2,1)}, u32[]{:S(2)}) copy-start(bf16[1024,768]{1,0:T(8,128)(2,1)} %convolution_convert_fusion) | copy-start | bytes 4718596
  179.3 3.8 %copy-start = (f32[2,128,768]{2,1,0:T(8,128)S(1)}, f32[2,128,768]{2,1,0:T(8,128)}, u32[]{:S(2)}) copy-start(f32[2,128,768]{2,1,0:T(8,128)} %ffn_sum.1) | copy-start | bytes 2359300
  179.3 3.8 %copy-start.9 = (bf16[1,128,768]{2,1,0:T(8,128)(2,1)S(1)}, bf16[1,128,768]{2,1,0:T(8,128)(2,1)}, u32[]{:S(2)}) copy-start(bf16[1,128,768]{2,1,0:T(8,128)(2,1)} %param.18) | copy-start | bytes 589828
  183.0 13.7 %copy-start.6 = (bf16[1,16,48,384]{3,2,1,0:T(8,128)(2,1)S(1)}, bf16[1,16,48,384]{3,2,1,0:T(8,128)(2,1)}, u32[]{:S(2)}) copy-start(bf16[1,16,48,384]{3,2,1,0:T(8,128)(2,1)} %copy-done.5) | copy-start | bytes 1769476
  183.0 13.7 %copy-start.8 = (bf16[1,16,48,384]{3,2,1,0:T(8,128)(2,1)S(1)}, bf16[1,16,48,384]{3,2,1,0:T(8,128)(2,1)}, u32[]{:S(2)}) copy-start(bf16[1,16,48,384]{3,2,1,0:T(8,128)(2,1)} %copy-done.7) | copy-start | bytes 1769476
  222.2 28.6 %copy-start.4 = (bf16[2,4,128,768]{3,2,1,0:T(8,128)(2,1)S(1)}, bf16[2,4,128,768]{3,2,1,0:T(8,128)(2,1)}, u32[]{:S(2)}) copy-start(bf16[2,4,128,768]{3,2,1,0:T(8,128)(2,1)} %get-tuple-element.38) | copy-start | bytes 4718596
  222.2 28.6 %copy-start.11 = (bf16[512,192]{1,0:T(8,128)(2,1)S(1)}, bf16[512,192]{1,0:T(8,128)(2,1)}, u32[]{:S(2)}) copy-start(bf16[512,192]{1,0:T(8,128)(2,1)} %get-tuple-element.51) | copy-start | bytes 589828
  222.2 28.7 %copy-start.28 = (bf16[16,48,640]{2,1,0:T(8,128)(2,1)S(1)}, bf16[16,48,640]{2,1,0:T(8,128)(2,1)}, u32[]{:S(2)}) copy-start(bf16[16,48,640]{2,1,0:T(8,128)(2,1)} %get-tuple-element.39) | copy-start | bytes 2949124
  222.2 28.7 %copy-start.38 = (f32[512]{0:T(512)S(1)}, f32[512]{0:T(512)}, u32[]{:S(2)}) copy-start(f32[512]{0:T(512)} %copy-done.37) | copy-start | bytes 6148
  222.2 28.7 %copy-start.40 = (f32[512]{0:T(512)S(1)}, f32[512]{0:T(512)}, u32[]{:S(2)}) copy-start(f32[512]{0:T(512)} %copy-done.39) | copy-start | bytes 6148
  256.8 49.1 %copy-start.1 = (bf16[1,128,768]{2,1,0:T(8,128)(2,1)S(1)}, bf16[1,128,768]{2,1,0:T(8,128)(2,1)}, u32[]{:S(2)}) copy-start(bf16[1,128,768]{2,1,0:T(8,128)(2,1)} %param.17) | copy-start | bytes 589828
  256.8 49.1 %copy-start.42 = (f32[128]{0:T(128)S(1)}, f32[128]{0:T(128)}, u32[]{:S(2)}) copy-start(f32[128]{0:T(128)} %copy-done.41) | copy-start | bytes 1540
  256.8 49.1 %copy-start.45 = (f32[128]{0:T(128)S(1)}, f32[128]{0:T(128)}, u32[]{:S(2)}) copy-start(f32[128]{0:T(128)} %add_rsqrt_fusion.1) | copy-start | bytes 1540
  307.3 3.5 %copy-start.19 = (f32[6,768]{1,0:T(8,128)S(1)}, f32[6,768]{1,0:T(8,128)}, u32[]{:S(2)}) copy-start(f32[6,768]{1,0:T(8,128)} %wo_ref.1) | copy-start | bytes 55300
  307.3 3.5 %copy-start.29 = (f32[6,768]{1,0:T(8,128)S(1)}, f32[6,768]{1,0:T(8,128)}, u32[]{:S(2)}) copy-start(f32[6,768]{1,0:T(8,128)} %param.23) | copy-start | bytes 55300
  307.3 4.1 %copy-start.16 = (f32[6,2304]{1,0:T(8,128)S(1)}, f32[6,2304]{1,0:T(8,128)}, u32[]{:S(2)}) copy-start(f32[6,2304]{1,0:T(8,128)} %wq_ref.1) | copy-start | bytes 165892
  307.3 4.1 %copy-start.22 = (f32[6,2304]{1,0:T(8,128)S(1)}, f32[6,2304]{1,0:T(8,128)}, u32[]{:S(2)}) copy-start(f32[6,2304]{1,0:T(8,128)} %param.20) | copy-start | bytes 165892
  307.3 4.1 %copy-start.23 = (f32[6,2304]{1,0:T(8,128)S(1)}, f32[6,2304]{1,0:T(8,128)}, u32[]{:S(2)}) copy-start(f32[6,2304]{1,0:T(8,128)} %param.21) | copy-start | bytes 165892
  (27 other events, 67.3 us)

commit v2 on v1

--- a/solution.py
+++ b/solution.py
@@ -324,176 +324,6 @@
         spaces=([VMEM] * 5 + [ANY], [ANY] * 5),
         name="first_gather",
     )
-
-
-def kv_gather(kv, rows, fc, out, proj):
-    def kernel(
-        v_ref, r_ref, f_ref, o_ref, p_ref, vo_ref, ro_ref, fo_ref, oo_ref, po_ref,
-        vs, vr, rs, rr, cs, cr, ds, dr, ws, wr, os, orr, loc,
-    ):
-        y, z, k, x = coords()
-        sib = device(y, z, 1 - k, x)
-        ys = [(d, ring(y, d)) for d in (1, 2, 3)]
-        zs = [(d, ring(z, d)) for d in (1, 2, 3)]
-        greet(
-            [sib]
-            + [device(b, z, k, x) for _, b in ys]
-            + [device(y, b, k, x) for _, b in zs]
-            + [device(y, z, k, ring(x, d)) for d in (1, 2, 3)]
-        )
-        own = [
-            pltpu.make_async_copy(v_ref, vo_ref.at[y, k], loc.at[0]),
-            pltpu.make_async_copy(r_ref, ro_ref.at[k, z], loc.at[1]),
-        ]
-        for c in own:
-            c.start()
-        kv_copies, row_copies, forward = [], [], []
-        for d, b in ys:
-            c = remote(v_ref, vo_ref.at[y, k], vs.at[d], vr.at[d], device(b, z, k, x))
-            c.start()
-            kv_copies.append(c)
-        for d, b in zs:
-            c = remote(r_ref, ro_ref.at[k, z], rs.at[d], rr.at[d], device(y, b, k, x))
-            c.start()
-            row_copies.append(c)
-
-        weights = ((1, f_ref, fo_ref), (2, o_ref, oo_ref.at[k]), (3, p_ref, po_ref))
-
-        def weight_copy(a, d):
-            _, src, dst = weights[a - 1]
-            return remote(src, dst, ws.at[d], wr.at[a], device(y, z, k, ring(x, d)))
-
-        for a in (1, 2, 3):
-
-            @pl.when(x == a)
-            def _():
-                for d in (1, 2, 3):
-                    weight_copy(a, d).start()
-                _, src, dst = weights[a - 1]
-                c = pltpu.make_async_copy(src, dst, loc.at[2])
-                c.start()
-                c.wait()
-
-        c = remote(v_ref, vo_ref.at[y, k], cs.at[0], cr.at[0], sib)
-        c.start()
-        forward.append(c)
-        c = remote(r_ref, ro_ref.at[k, z], ds.at[0], dr.at[0], sib)
-        c.start()
-        forward.append(c)
-        for c, (d, b) in zip(row_copies, zs):
-            c.wait_recv()
-            src = ring(z, 4 - d)
-            f = remote(ro_ref.at[k, src], ro_ref.at[k, src], ds.at[d], dr.at[d], sib)
-            f.start()
-            forward.append(f)
-        for c, (d, b) in zip(kv_copies, ys):
-            c.wait_recv()
-            src = ring(y, 4 - d)
-            f = remote(vo_ref.at[src, k], vo_ref.at[src, k], cs.at[d], cr.at[d], sib)
-            f.start()
-            forward.append(f)
-        for a in (2, 1, 3):
-
-            @pl.when(x != a)
-            def _():
-                weight_copy(a, 1).wait_recv()
-
-            if a == 2:
-                c = remote(oo_ref.at[k], oo_ref.at[k], os.at[0], orr.at[0], sib)
-                c.start()
-                forward.append(c)
-        for a in (1, 2, 3):
-
-            @pl.when(x == a)
-            def _():
-                for d in (1, 2, 3):
-                    weight_copy(a, d).wait_send()
-
-        for c in kv_copies + row_copies:
-            c.wait_send()
-        for c in forward:
-            c.wait()
-        for c in own:
-            c.wait()
-
-    return comm(
-        kernel,
-        [
-            jax.ShapeDtypeStruct((4, 2) + kv.shape, BF),
-            jax.ShapeDtypeStruct((2, 4) + rows.shape, BF),
-            jax.ShapeDtypeStruct((16, 48, 384), BF),
-            jax.ShapeDtypeStruct((2, 16, 48, 384), BF),
-            jax.ShapeDtypeStruct((2, 192, 768), BF),
-        ],
-        2,
-        (4, 4, 4, 4, 4, 4, 4, 4, 4, 4, 1, 1, 3),
-        (kv, rows, fc, out, proj),
-        name="kv_gather",
-    )
-
-
-def heads_gather(heads):
-    def kernel(h_ref, ho_ref, hs, hr, cs, cr, loc):
-        y, z, k, x = coords()
-        sib = device(y, z, 1 - k, x)
-        zs = [(d, ring(z, d)) for d in (1, 2, 3)]
-        greet([sib] + [device(y, b, k, x) for _, b in zs])
-        own = pltpu.make_async_copy(h_ref, ho_ref.at[z, k], loc.at[0])
-        own.start()
-        copies = []
-        for d, b in zs:
-            c = remote(h_ref, ho_ref.at[z, k], hs.at[d], hr.at[d], device(y, b, k, x))
-            c.start()
-            copies.append(c)
-        c = remote(h_ref, ho_ref.at[z, k], cs.at[0], cr.at[0], sib)
-        c.start()
-        forward = [c]
-        for c, (d, b) in zip(copies, zs):
-            c.wait_recv()
-            src = ring(z, 4 - d)
-            f = remote(ho_ref.at[src, k], ho_ref.at[src, k], cs.at[d], cr.at[d], sib)
-            f.start()
-            forward.append(f)
-        for c in copies:
-            c.wait_send()
-        for c in forward:
-            c.wait()
-        own.wait()
-
-    return comm(
-        kernel,
-        [jax.ShapeDtypeStruct((4, 2) + heads.shape, BF)],
-        3,
-        (4, 4, 4, 4, 1),
-        (heads,),
-        name="heads_gather",
-    )[0]
-
-
-def z_gather(rows):
-    def kernel(r_ref, ro_ref, rs, rr, loc):
-        y, z, k, x = coords()
-        zs = [(d, ring(z, d)) for d in (1, 2, 3)]
-        greet([device(y, b, k, x) for _, b in zs])
-        own = pltpu.make_async_copy(r_ref, ro_ref.at[z], loc.at[0])
-        own.start()
-        copies = []
-        for d, b in zs:
-            c = remote(r_ref, ro_ref.at[z], rs.at[d], rr.at[d], device(y, b, k, x))
-            c.start()
-            copies.append(c)
-        for c in copies:
-            c.wait()
-        own.wait()
-
-    return comm(
-        kernel,
-        [jax.ShapeDtypeStruct((4,) + rows.shape, BF)],
-        4,
-        (4, 4, 1),
-        (rows,),
-        name="z_gather",
-    )[0]
 
 
 def group_sum(parts, cid, name):
@@ -559,98 +389,6 @@
     )[0]
 
 
-def kv_sum(parts, fc, proj):
-    rows, cols = parts.shape[2:]
-
-    def kernel(
-        p_ref, f_ref, w_ref, o_ref, fo_ref, wo_ref, got, mine, far, f_far, w_far,
-        cs, cr, ys, yr, fs, fr, ws, wr,
-    ):
-        y, z, k, x = coords()
-        sib = device(y, z, 1 - k, x)
-        ring_y = [(d, ring(y, d)) for d in (1, 2, 3)]
-        greet(
-            [sib]
-            + [device(b, z, k, x) for _, b in ring_y]
-            + [device(y, z, k, ring(x, d)) for d in (1, 2, 3)]
-        )
-        order = ring_y + [(0, y)]
-        pairs = []
-        for d, b in order:
-            c = remote(p_ref.at[b, 1 - k], got.at[b], cs.at[d], cr.at[b], sib)
-            c.start()
-            pairs.append(c)
-        weights = []
-        for d in (1, 2, 3):
-            b = ring(x, d)
-            to = device(y, z, k, b)
-            weights.append(
-                remote(f_ref.at[:, b], f_far.at[d - 1], fs.at[d - 1], fr.at[d - 1], to)
-            )
-            weights.append(
-                remote(w_ref.at[:, b], w_far.at[d - 1], ws.at[d - 1], wr.at[d - 1], to)
-            )
-        for c in weights:
-            c.start()
-        copies = []
-        for i, (d, b) in enumerate(order):
-            pairs[i].wait_recv()
-            total = p_ref[b, k].astype(F32) + got[b].astype(F32)
-            if d == 0:
-                o_ref[...] = total
-            else:
-                mine[d - 1] = total.astype(BF)
-                c = remote(
-                    mine.at[d - 1], far.at[d - 1], ys.at[d - 1], yr.at[d - 1], device(b, z, k, x)
-                )
-                c.start()
-                copies.append(c)
-        for c in weights:
-            c.wait()
-        fo_ref[...] = (
-            f_ref[:, x].astype(F32)
-            + f_far[0].astype(F32)
-            + f_far[1].astype(F32)
-            + f_far[2].astype(F32)
-        ).astype(BF)
-        wo_ref[...] = (
-            w_ref[:, x].astype(F32)
-            + w_far[0].astype(F32)
-            + w_far[1].astype(F32)
-            + w_far[2].astype(F32)
-        ).astype(BF)
-        for c in copies:
-            c.wait_recv()
-        o_ref[...] = (
-            o_ref[...] + far[0].astype(F32) + far[1].astype(F32) + far[2].astype(F32)
-        )
-        for c in copies:
-            c.wait_send()
-        for c in pairs:
-            c.wait_send()
-
-    return comm(
-        kernel,
-        [
-            jax.ShapeDtypeStruct((rows, cols), F32),
-            jax.ShapeDtypeStruct((4, 48, 384), BF),
-            jax.ShapeDtypeStruct((2, 48, 768), BF),
-        ],
-        5,
-        (4, 4, 3, 3, 3, 3, 3, 3),
-        (parts, fc, proj),
-        scratch=[
-            pltpu.VMEM((4, rows, cols), BF),
-            pltpu.VMEM((3, rows, cols), BF),
-            pltpu.VMEM((3, rows, cols), BF),
-            pltpu.VMEM((3, 4, 48, 384), BF),
-            pltpu.VMEM((3, 2, 48, 768), BF),
-        ],
-        spaces=([VMEM] * 3, [VMEM] * 3),
-        name="kv_sum",
-    )
-
-
 def last_sums(one, mix, vec, fc, proj):
     wide = 3200
 
@@ -953,9 +691,67 @@
     return jnp.dot(a, b, preferred_element_type=F32)
 
 
-def attend(query, kv_all):
-    def kernel(q_ref, kv_ref, h_ref, ot_ref, lse_ref, qt, m_ref, l_ref):
+def attend(query, kv, rows, fc, out, proj):
+    def kernel(
+        q_ref, v_ref, r_ref, f_ref, o_ref, p_ref,
+        ho_ref, ot_ref, lse_ref, vo_ref, ro_ref, fo_ref, oo_ref, po_ref,
+        qt, m_ref, l_ref, h_buf,
+        vs, vr, rs, rr, cs, cr, ds, dr, ws, wr, os, orr, hs, hr, gs, gr, loc,
+    ):
         y, z, k, x = coords()
+        sib = device(y, z, 1 - k, x)
+        steps = (1, 2, 3)
+        greet(
+            [sib]
+            + [device(ring(y, d), z, k, x) for d in steps]
+            + [device(y, ring(z, d), k, x) for d in steps]
+            + [device(y, z, k, ring(x, d)) for d in steps]
+        )
+
+        def kv_copy(d):
+            return remote(
+                v_ref, vo_ref.at[y, k], vs.at[d], vr.at[d], device(ring(y, d), z, k, x)
+            )
+
+        for d in steps:
+
+            @pl.when(y + d < 4)
+            def _():
+                kv_copy(d).start()
+
+        swap = remote(v_ref, vo_ref.at[y, k], cs.at[0], cr.at[0], sib)
+        swap.start()
+        vo_ref[y, k] = v_ref[...]
+        own_r = pltpu.make_async_copy(r_ref, ro_ref.at[k, z], loc.at[0])
+        own_r.start()
+        row_copies = []
+        for d in steps:
+            c = remote(
+                r_ref, ro_ref.at[k, z], rs.at[d], rr.at[d], device(y, ring(z, d), k, x)
+            )
+            c.start()
+            row_copies.append(c)
+        row_first = remote(r_ref, ro_ref.at[k, z], ds.at[0], dr.at[0], sib)
+        row_first.start()
+
+        weights = ((1, f_ref, fo_ref), (2, o_ref, oo_ref.at[k]), (3, p_ref, po_ref))
+
+        def weight_copy(a, d):
+            _, src, dst = weights[a - 1]
+            return remote(src, dst, ws.at[d], wr.at[a], device(y, z, k, ring(x, d)))
+
+        def weight_own(a):
+            _, src, dst = weights[a - 1]
+            return pltpu.make_async_copy(src, dst, loc.at[1])
+
+        for a in steps:
+
+            @pl.when(x == a)
+            def _():
+                for d in steps:
+                    weight_copy(a, d).start()
+                weight_own(a).start()
+
         q_t = q_ref[...].T
         for head in range(3):
             qt[head] = head_rows(q_t, head)
@@ -964,8 +760,8 @@
         ot_ref[...] = jnp.zeros_like(ot_ref)
 
         def block(by, bk, masked):
-            keys = kv_ref[by, bk, :, :192]
-            values_t = kv_ref[by, bk, :, 192:].T
+            keys = vo_ref[by, bk, :, :192]
+            values_t = vo_ref[by, bk, :, 192:].T
             if masked:
                 key_at = place(lax.broadcasted_iota(jnp.int32, (512, 512), 0)) + 128 * bk
                 query_at = place(lax.broadcasted_iota(jnp.int32, (512, 512), 1)) + 128 * k
@@ -982,59 +778,192 @@
                 l_ref[head : head + 1] = l_ref[head : head + 1] * scale + jnp.sum(
                     e, 0, keepdims=True
                 )
-                rows = slice(64 * head, 64 * head + 64)
-                ot_ref[rows] = ot_ref[rows] * scale + dot(values_t[rows], e.astype(BF))
-
-        def step(j, carry):
-            block(j // 2, j % 2, False)
+                at = slice(64 * head, 64 * head + 64)
+                ot_ref[at] = ot_ref[at] * scale + dot(values_t[at], e.astype(BF))
+
+        def diagonal(j, carry):
+            @pl.when(j == 1)
+            def _():
+                remote(v_ref, vo_ref.at[y, 1 - k], cs.at[0], cr.at[0], sib).wait_recv()
+
+            block(y, lax.rem(k + j, 2), True)
             return carry
 
-        lax.fori_loop(0, 2 * y, step, 0)
-        block(y, 0, True)
-        block(y, 1, True)
+        lax.fori_loop(0, 2, diagonal, 0)
+
+        def pass_on(d):
+            return remote(
+                vo_ref.at[y - d, k], vo_ref.at[y - d, k], cs.at[d], cr.at[d], sib
+            )
+
+        def earlier(i, carry):
+            d, j = i // 2 + 1, i % 2
+
+            @pl.when(j == 0)
+            def _():
+                remote(v_ref, vo_ref.at[y - d, k], vs.at[d], vr.at[d], sib).wait_recv()
+                pass_on(d).start()
+
+            @pl.when(j == 1)
+            def _():
+                remote(v_ref, vo_ref.at[y - d, 1 - k], cs.at[d], cr.at[d], sib).wait_recv()
+
+            block(y - d, lax.rem(k + j, 2), False)
+            return carry
+
+        lax.fori_loop(0, 2 * y, earlier, 0)
         for head in range(3):
-            rows = slice(64 * head, 64 * head + 64)
+            at = slice(64 * head, 64 * head + 64)
             total = l_ref[head : head + 1]
-            ot_ref[rows] = ot_ref[rows] / total
+            ot_ref[at] = ot_ref[at] / total
             lse_ref[head : head + 1] = m_ref[head : head + 1] + jnp.log(total)
-        h_ref[...] = ot_ref[...].T.astype(BF)
-
-    return pl.pallas_call(
+        h_buf[...] = ot_ref[...].T.astype(BF)
+        heads_copies = []
+        for d in steps:
+            c = remote(
+                h_buf, ho_ref.at[z, k], hs.at[d], hr.at[d], device(y, ring(z, d), k, x)
+            )
+            c.start()
+            heads_copies.append(c)
+        c = remote(h_buf, ho_ref.at[z, k], gs.at[0], gr.at[0], sib)
+        c.start()
+        forward = [c, row_first]
+        own_h = pltpu.make_async_copy(h_buf, ho_ref.at[z, k], loc.at[2])
+        own_h.start()
+        for d in steps:
+            row_copies[d - 1].wait_recv()
+            src = ring(z, 4 - d)
+            c = remote(ro_ref.at[k, src], ro_ref.at[k, src], ds.at[d], dr.at[d], sib)
+            c.start()
+            forward.append(c)
+        for a in steps:
+
+            @pl.when(x == a)
+            def _():
+                weight_own(a).wait()
+
+            @pl.when(x != a)
+            def _():
+                weight_copy(a, 1).wait_recv()
+
+        c = remote(oo_ref.at[k], oo_ref.at[k], os.at[0], orr.at[0], sib)
+        c.start()
+        forward.append(c)
+        for d in steps:
+            heads_copies[d - 1].wait_recv()
+            src = ring(z, 4 - d)
+            c = remote(ho_ref.at[src, k], ho_ref.at[src, k], gs.at[d], gr.at[d], sib)
+            c.start()
+            forward.append(c)
+        for c in forward:
+            c.wait()
+        for c in row_copies + heads_copies + [swap]:
+            c.wait_send()
+        for d in steps:
+
+            @pl.when(y + d < 4)
+            def _():
+                kv_copy(d).wait_send()
+
+            @pl.when(y >= d)
+            def _():
+                pass_on(d).wait_send()
+
+        for a in steps:
+
+            @pl.when(x == a)
+            def _():
+                for d in steps:
+                    weight_copy(a, d).wait_send()
+
+        own_r.wait()
+        own_h.wait()
+
+    return comm(
         kernel,
-        out_shape=[
-            jax.ShapeDtypeStruct((512, 192), BF),
+        [
+            jax.ShapeDtypeStruct((4, 2, 512, 192), BF),
             jax.ShapeDtypeStruct((192, 512), F32),
             jax.ShapeDtypeStruct((8, 512), F32),
+            jax.ShapeDtypeStruct((4, 2, 512, 384), BF),
+            jax.ShapeDtypeStruct((2, 4, 128, 768), BF),
+            jax.ShapeDtypeStruct((16, 48, 384), BF),
+            jax.ShapeDtypeStruct((2, 16, 48, 384), BF),
+            jax.ShapeDtypeStruct((2, 192, 768), BF),
         ],
-        in_specs=[VMEM] * 2,
-        out_specs=[VMEM] * 3,
-        scratch_shapes=[
+        2,
+        (4, 4, 4, 4, 4, 4, 4, 4, 4, 4, 1, 1, 4, 4, 4, 4, 3),
+        (query, kv, rows, fc, out, proj),
+        scratch=[
             pltpu.VMEM((3, 192, 512), BF),
             pltpu.VMEM((8, 512), F32),
             pltpu.VMEM((8, 512), F32),
+            pltpu.VMEM((512, 192), BF),
         ],
-        compiler_params=pltpu.CompilerParams(vmem_limit_bytes=LIMIT),
+        spaces=(
+            [VMEM, VMEM, ANY, ANY, ANY, ANY],
+            [ANY, VMEM, VMEM, VMEM, ANY, ANY, ANY, ANY],
+        ),
         name="attend",
-    )(query, kv_all)
-
-
-def attend_back(query, grad_heads, kv_all, out_t, lse):
-    def kernel(q_ref, g_ref, kv_ref, ot_ref, lse_ref, dq_ref, dkv_ref, qt, gt, qm, gm, delta, dqt):
+    )
+
+
+def attend_back(query, branch, wo_rows, kv_all, out_t, lse, fc, proj):
+    def kernel(
+        q_ref, b_ref, w_ref, kv_ref, ot_ref, lse_ref, f_ref, p_ref,
+        dq_ref, dkv_ref, bo_ref, fo_ref, po_ref,
+        qt, gt, qm, gm, delta, dqt, out_buf, keep, got, far, f_far, p_far,
+        bs, br, cs, cr, ys, yr, fs, fr, ps, pr,
+    ):
         y, z, k, x = coords()
-        query_blk, grad_blk = q_ref[...], g_ref[...]
-        q_t, g_t = query_blk.T, grad_blk.T
+        sib = device(y, z, 1 - k, x)
+        steps = (1, 2, 3)
+        greet(
+            [sib]
+            + [device(ring(y, d), z, k, x) for d in steps]
+            + [device(y, ring(z, d), k, x) for d in steps]
+            + [device(y, z, k, ring(x, d)) for d in steps]
+        )
+        branches = []
+        for d in steps:
+            c = remote(b_ref, bo_ref.at[z], bs.at[d], br.at[d], device(y, ring(z, d), k, x))
+            c.start()
+            branches.append(c)
+        weights = []
+        for d in steps:
+            b = ring(x, d)
+            to = device(y, z, k, b)
+            weights.append(
+                remote(f_ref.at[:, b], f_far.at[d - 1], fs.at[d - 1], fr.at[d - 1], to)
+            )
+            weights.append(
+                remote(p_ref.at[:, b], p_far.at[d - 1], ps.at[d - 1], pr.at[d - 1], to)
+            )
+        for c in weights:
+            c.start()
+        bo_ref[z] = b_ref[...]
+        query_blk = q_ref[...]
+        q_t = query_blk.T
         for head in range(3):
-            rows = slice(64 * head, 64 * head + 64)
             qt[head] = head_rows(q_t, head)
+            qm[head] = head_cols(query_blk, head)
+        dqt[...] = jnp.zeros_like(dqt)
+        for c in branches:
+            c.wait_recv()
+        grad_blk = lax.dot_general(
+            bo_ref[...].reshape(512, 768),
+            w_ref[...],
+            (((1,), (1,)), ((), ())),
+            preferred_element_type=F32,
+        ).astype(BF)
+        g_t = grad_blk.T
+        for head in range(3):
+            at = slice(64 * head, 64 * head + 64)
             gt[head] = head_rows(g_t, head)
-            qm[head] = head_cols(query_blk, head)
             gm[head] = head_cols(grad_blk, head)
-            delta[head : head + 1] = jnp.sum(
-                g_t[rows].astype(F32) * ot_ref[rows], 0, keepdims=True
-            )
-        dqt[...] = jnp.zeros_like(dqt)
-
-        def block(by, bk, masked):
+            delta[head : head + 1] = jnp.sum(g_t[at].astype(F32) * ot_ref[at], 0, keepdims=True)
+
+        def block(by, bk, masked, to_ref, to):
             keys = kv_ref[by, bk, :, :192]
             values = kv_ref[by, bk, :, 192:]
             keys_t = keys.T
@@ -1054,44 +983,94 @@
                 pk = dot(ds, qm[head])
                 dv = pv if dv is None else dv + pv
                 dk = pk if dk is None else dk + pk
-                rows = slice(64 * head, 64 * head + 64)
-                dqt[rows] += dot(keys_t[rows], ds)
-            dkv_ref[by, bk, :, :192] = dk.astype(BF)
-            dkv_ref[by, bk, :, 192:] = dv.astype(BF)
-
-        def step(j, carry):
-            block(j // 2, j % 2, False)
+                at = slice(64 * head, 64 * head + 64)
+                dqt[at] += dot(keys_t[at], ds)
+            to_ref[to, :, :192] = dk.astype(BF)
+            to_ref[to, :, 192:] = dv.astype(BF)
+
+        def cross(d):
+            return remote(out_buf.at[d], got.at[d], cs.at[d], cr.at[d], sib)
+
+        def up(d):
+            return remote(keep.at[d], far.at[d], ys.at[d], yr.at[d], device(y - d, z, k, x))
+
+        def earlier(i, carry):
+            d = y - i
+            block(y - d, 1 - k, False, out_buf, d)
+            cross(d).start()
+            block(y - d, k, False, keep, d)
+            cross(d).wait_recv()
+            keep[d] = (keep[d].astype(F32) + got[d].astype(F32)).astype(BF)
+            up(d).start()
             return carry
 
-        def clear(j, carry):
-            dkv_ref[j // 2, j % 2] = jnp.zeros((512, 384), BF)
-            return carry
-
-        lax.fori_loop(0, 2 * y, step, 0)
-        block(y, 0, True)
-        block(y, 1, True)
-        lax.fori_loop(2 * y + 2, 8, clear, 0)
+        lax.fori_loop(0, y, earlier, 0)
+        block(y, 1 - k, True, out_buf, 0)
+        cross(0).start()
+        block(y, k, True, keep, 0)
         dq_ref[...] = (dqt[...].T * 0.125).astype(BF)
-
-    return pl.pallas_call(
+        cross(0).wait_recv()
+        for c in weights:
+            c.wait()
+        fo_ref[...] = (
+            f_ref[:, x].astype(F32)
+            + f_far[0].astype(F32)
+            + f_far[1].astype(F32)
+            + f_far[2].astype(F32)
+        ).astype(BF)
+        po_ref[...] = (
+            p_ref[:, x].astype(F32)
+            + p_far[0].astype(F32)
+            + p_far[1].astype(F32)
+            + p_far[2].astype(F32)
+        ).astype(BF)
+        dkv_ref[...] = keep[0].astype(F32) + got[0].astype(F32)
+        for d in (1, 2, 3):
+
+            @pl.when(y + d < 4)
+            def _():
+                remote(keep.at[d], far.at[d], ys.at[d], yr.at[d], sib).wait_recv()
+                dkv_ref[...] += far[d].astype(F32)
+
+        for c in branches:
+            c.wait_send()
+        cross(0).wait_send()
+        for d in (1, 2, 3):
+
+            @pl.when(y >= d)
+            def _():
+                cross(d).wait_send()
+                up(d).wait_send()
+
+    return comm(
         kernel,
-        out_shape=[
+        [
             jax.ShapeDtypeStruct((512, 192), BF),
-            jax.ShapeDtypeStruct((4, 2, 512, 384), BF),
+            jax.ShapeDtypeStruct((512, 384), F32),
+            jax.ShapeDtypeStruct((4, 128, 768), BF),
+            jax.ShapeDtypeStruct((4, 48, 384), BF),
+            jax.ShapeDtypeStruct((2, 48, 768), BF),
         ],
-        in_specs=[VMEM] * 5,
-        out_specs=[VMEM] * 2,
-        scratch_shapes=[
+        5,
+        (4, 4, 4, 4, 4, 4, 3, 3, 3, 3),
+        (query, branch, wo_rows, kv_all, out_t, lse, fc, proj),
+        scratch=[
             pltpu.VMEM((3, 192, 512), BF),
             pltpu.VMEM((3, 192, 512), BF),
             pltpu.VMEM((3, 512, 192), BF),
             pltpu.VMEM((3, 512, 192), BF),
             pltpu.VMEM((8, 512), F32),
             pltpu.VMEM((192, 512), F32),
+            pltpu.VMEM((4, 512, 384), BF),
+            pltpu.VMEM((4, 512, 384), BF),
+            pltpu.VMEM((4, 512, 384), BF),
+            pltpu.VMEM((4, 512, 384), BF),
+            pltpu.VMEM((3, 4, 48, 384), BF),
+            pltpu.VMEM((3, 2, 48, 768), BF),
         ],
-        compiler_params=pltpu.CompilerParams(vmem_limit_bytes=LIMIT),
+        spaces=([VMEM] * 8, [VMEM] * 5),
         name="attend_back",
-    )(query, grad_heads, kv_all, out_t, lse)
+    )
 
 
 def normalize(rows):
@@ -1167,14 +1146,12 @@
     act_one = (normed_core * gain_one + shift_one).astype(BF)
     mixed = (dot(act_one, wq) + bias).astype(BF)
     query = mixed[:, :192] * jnp.asarray(0.125, BF)
-    kv_all, dy_group, wf, wo, wp = kv_gather(
-        mixed[:, 192:], cotangent[0], fc_part, out_part, proj_part
+    heads_all, out_t, lse, kv_all, dy_group, wf, wo, wp = attend(
+        query, mixed[:, 192:], cotangent[0], fc_part, out_part, proj_part
     )
     wf = wf.reshape(768, 384)
     wo = jnp.concatenate([wo[0].reshape(768, 384), wo[1].reshape(768, 384)], 1)
     wp = wp.reshape(384, 768)
-    heads, out_t, lse = attend(query, kv_all)
-    heads_all = heads_gather(heads)
     heads_all = jnp.concatenate([heads_all[i].reshape(1024, 192) for i in range(4)], 1)
     x_two = x_group.reshape(1024, 768).astype(F32) + dot(heads_all, wo) + out_bias
     normed_two, inverse_two = normalize(x_two)
@@ -1203,15 +1180,18 @@
     grad_norm_two = sums[0]
     grad_x_two = grad_output + normalize_back(own_normed, own_inverse, gain_two, grad_norm_two)
     grad_branch = grad_x_two.astype(BF)
-    branch_core = z_gather(grad_branch).reshape(512, 768)
     wo_rows = lax.dynamic_slice(wo, (192 * z, 0), (192, 768))
-    grad_heads = dot(branch_core, wo_rows.T).astype(BF)
-    grad_query, kv_parts = attend_back(query, grad_heads, kv_all, out_t, lse)
-    grad_kv, fc_sum, proj_sum = kv_sum(
-        kv_parts,
+    grad_query, grad_kv, branch_core, fc_sum, proj_sum = attend_back(
+        query,
+        grad_branch,
+        wo_rows,
+        kv_all,
+        out_t,
+        lse,
         grad_w_fc.astype(BF).reshape(4, 4, 48, 384),
         grad_w_proj.astype(BF).reshape(2, 4, 48, 768),
     )
+    branch_core = branch_core.reshape(512, 768)
     grad_mixed = jnp.concatenate([grad_query, grad_kv.astype(BF)], 1)
     branch_cols = lax.dynamic_slice(branch_core, (0, 192 * z), (512, 192))
     heads_core = lax.dynamic_index_in_dim(heads_all.reshape(2, 512, 768), k, 0, False)

time: 314 us -> 263 us (0.84)
  Pallas kernels: 252 us -> 201 us
    pallas_call x2 -> x0, Pallas kernels: 38.8 us -> none  [the longest x1 21.9 us: attend_back(): pl.pallas_call(kernel, out_shape=[jax.ShapeDtypeStruct((512, 192), BF), j...]
    pallas_call x7 -> x5, Pallas kernels: 213 us -> 201 us  [comm(): pl.pallas_call(kernel, out_shape=outs, in_specs=[ANY] * len(args) if spac...]
    dot_general x11 -> x10, matrix products: 19.8 us -> 19.4 us  [dot(): return jnp.dot(a, b, preferred_element_type=F32)]
where the time goes in v2:
time: 263 us
  Pallas kernels  201 us (76%)
  other arithmetic  26.3 us (10%)
  matrix products  19.4 us (7%)
  local copies, waits for them, and re-layouts  14.8 us (6%)
    pallas_call x5, Pallas kernels, comm(): pl.pallas_call(kernel, out_shape=outs, in_specs=[ANY] * len(args) if spac...  201 us
    dot_general x10, matrix products, dot(): return jnp.dot(a, b, preferred_element_type=F32)  19.4 us

profile of v2, /device:TPU:29, one launch (start us, length us, event | category | flops | bytes accessed | tf_op | source)
XLA Modules:
  0.0 262.6 jit_solution(4438842965270170044)
XLA Ops:
  4.4 37.0 %first_gather.1 = (bf16[16,48,640]{2,1,0:T(8,128)(2,1)}, bf16[16,48,384]{2,1,0:T(8,128)(2,1)}, bf16[16,48,384]{2,1,0:T(8,128)(2,1)}, bf16[2,192,768]{2,1,0:T(8,128)(2,1)}, bf16[2,4,128,768]{3,2,1,0:T(8,128)(2,1)}) custom-call(f32[6,2304]{1,0:T(8,128)} %wq_ref.1, f32[6,3072]{1,0:T(8,128)} %wf_ref.1, f32[6,768]{1,0:T(8,128)} %wo_ref.1, f32[24,768]{1,0:T(8,128)} %wp_ref.1, ...), custom_call_target="tpu_custom_call" | custom-call | tf_op jit(solution)/shard_map/first_gather/pallas_call | solution.py:48
  41.4 1.4 convert_reduce_fusion.1
  42.9 1.6 multiply_reduce_fusion.2
  49.5 45.0 %attend.1 = (bf16[4,2,512,192]{3,2,1,0:T(8,128)(2,1)}, f32[192,512]{1,0:T(8,128)}, f32[8,512]{1,0:T(8,128)}, bf16[4,2,512,384]{3,2,1,0:T(8,128)(2,1)}, bf16[2,4,...) custom-call(bf16[512,192]{1,0:T(8,128)(2,1)} %slice_multiply_fusion., ...), custom_call_target="tpu_custom_call" | custom-call | tf_op jit(solution)/shard_map/attend/pallas_call | solution.py:48
  94.6 1.5 fusion.82
  97.3 1.2 fusion.46
  99.0 1.7 fusion.87
  104.0 1.8 convolution_convert_fusion.2
  105.8 2.0 convert_reduce_fusion
  107.9 2.4 convolution_convert_fusion
  110.3 1.9 convolution_convert_fusion.3
  114.1 2.3 convolution_convert_fusion.1
  116.4 2.0 pad_maximum_fusion.p_ref
  118.4 25.5 %ffn_sum.1 = f32[2,128,768]{2,1,0:T(8,128)} custom-call(bf16[2,2,4,128,768]{4,3,2,1,0:T(8,128)(2,1)} %pad_maximum_fusion.p_ref), custom_call_target="tpu_custom_call" | custom-call | tf_op jit(solution)/shard_map/ffn_sum/pallas_call | solution.py:48
  145.6 2.0 fusion.58
  147.7 1.6 fusion.81
  149.2 42.2 %attend_back.1 = (bf16[512,192]{1,0:T(8,128)(2,1)}, f32[512,384]{1,0:T(8,128)}, bf16[4,128,768]{2,1,0:T(8,128)(2,1)}, bf16[4,48,384]{2,1,0:T(8,128)(2,1)}, bf16[2,48,768]{2,1,0:T(8,128)(2,1)}) custom-call(bf16[512,192]{1,0:T(8,128)(2,1)} %slice_multiply_fusion.q_ref, bf16[128,768]{1,0:T(8,128)(2,1)} %get-tuple-element.90.b_ref, ...), custom_call_target="tpu_custom_call" | custom-call | tf_op jit(solution)/shard_map/attend_back/pallas_call | solution.py:48
  192.7 2.9 %fusion.73 = (bf16[768]{0:T(1024)(128)(2,1)S(1)}, bf16[768]{0:T(1024)(128)(2,1)S(1)}, bf16[512,768]{1,0:T(8,128)(2,1)}) fusion(f32[512]{0:T(512)S(1)} %copy-done.39, f32[512]{0:T(512)S(1)} %copy-done.37, bf16[2,4,128,768]{3,2,1,0:T(8,128)(2,1)S(1)} %copy-done.4, s32[]{:T(128)S(6)} %select_n.37, bf16[768,640]{1,0:T(8,128)(2,1)S(1)} %bitcast.128, ...), kind=kOutput, calls=%fused_computation.160 | convolution fusion | flops 456915456 | bytes 3152900 | tf_op jit(solution)/shard_map/dot_general | solution.py:691
  195.6 1.9 constant_dynamic-slice_fusion.1
  198.2 1.3 stack.57
  200.5 2.6 fusion.34
  204.0 50.8 %last_sums.1 = (f32[128,768]{1,0:T(8,128)}, f32[2,8,3200]{2,1,0:T(8,128)}, f32[24,768]{1,0:T(8,128)}) custom-call(bf16[4,128,768]{2,1,0:T(8,128)(2,1)} %bitcast.116, bf16[4,4,48,768]{3,2,1,0:T(8,128)(2,1)} %bitcast.114, bf16[4,4,48,128]{3,2,1,0:T(8,128)(2,1)} %bitcast.115, bf16[4,48,384]{2,1,0:T(8,128)(2,1)} %get-tuple-element.54.fc_ref, ...), custom_call_target="tpu_custom_call" | custom-call | tf_op jit(solution)/shard_map/last_sums/pallas_call | solution.py:48
  254.9 1.3 multiply_reduce_fusion.5
  256.3 2.0 fusion.55
  (185 shorter events, 25.2 us)
Async XLA Ops:
  41.4 5.2 %copy-start.2 = (bf16[2,4,128,768]{3,2,1,0:T(8,128)(2,1)S(1)}, bf16[2,4,128,768]{3,2,1,0:T(8,128)(2,1)}, u32[]{:S(2)}) copy-start(bf16[2,4,128,768]{3,2,1,0:T(8,128)(2,1)} %get-tuple-element.38) | copy-start | bytes 4718596
  42.9 4.1 %copy-start.36 = (f32[512]{0:T(512)}, f32[512]{0:T(512)S(1)}, u32[]{:S(2)}) copy-start(f32[512]{0:T(512)S(1)} %get-tuple-element.118) | copy-start | bytes 6148
  42.9 4.1 %copy-start.27 = (bf16[16,48,640]{2,1,0:T(8,128)(2,1)S(1)}, bf16[16,48,640]{2,1,0:T(8,128)(2,1)}, u32[]{:S(2)}) copy-start(bf16[16,48,640]{2,1,0:T(8,128)(2,1)} %get-tuple-element.39) | copy-start | bytes 2949124
  100.8 44.8 %copy-start.42 = (f32[128]{0:T(128)}, f32[128]{0:T(128)S(1)}, u32[]{:S(2)}) copy-start(f32[128]{0:T(128)S(1)} %broadcast_multiply_fusion.7) | copy-start | bytes 1540
  101.0 44.6 %copy-start.47 = (f32[128]{0:T(128)}, f32[128]{0:T(128)S(1)}, u32[]{:S(2)}) copy-start(f32[128]{0:T(128)S(1)} %add_rsqrt_fusion.2) | copy-start | bytes 1540
  112.4 4.1 %copy-start.7 = (bf16[1024,768]{1,0:T(8,128)(2,1)S(1)}, bf16[1024,768]{1,0:T(8,128)(2,1)}, u32[]{:S(2)}) copy-start(bf16[1024,768]{1,0:T(8,128)(2,1)} %convolution_convert_fusion) | copy-start | bytes 4718596
  143.9 3.8 %copy-start = (f32[2,128,768]{2,1,0:T(8,128)S(1)}, f32[2,128,768]{2,1,0:T(8,128)}, u32[]{:S(2)}) copy-start(f32[2,128,768]{2,1,0:T(8,128)} %ffn_sum.1) | copy-start | bytes 2359300
  143.9 3.8 %copy-start.6 = (bf16[1,128,768]{2,1,0:T(8,128)(2,1)S(1)}, bf16[1,128,768]{2,1,0:T(8,128)(2,1)}, u32[]{:S(2)}) copy-start(bf16[1,128,768]{2,1,0:T(8,128)(2,1)} %param.18) | copy-start | bytes 589828
  149.2 43.4 %copy-start.4 = (bf16[2,4,128,768]{3,2,1,0:T(8,128)(2,1)S(1)}, bf16[2,4,128,768]{3,2,1,0:T(8,128)(2,1)}, u32[]{:S(2)}) copy-start(bf16[2,4,128,768]{3,2,1,0:T(8,128)(2,1)} %get-tuple-element.38) | copy-start | bytes 4718596
  149.2 43.4 %copy-start.28 = (bf16[16,48,640]{2,1,0:T(8,128)(2,1)S(1)}, bf16[16,48,640]{2,1,0:T(8,128)(2,1)}, u32[]{:S(2)}) copy-start(bf16[16,48,640]{2,1,0:T(8,128)(2,1)} %get-tuple-element.39) | copy-start | bytes 2949124
  149.2 43.4 %copy-start.37 = (f32[512]{0:T(512)S(1)}, f32[512]{0:T(512)}, u32[]{:S(2)}) copy-start(f32[512]{0:T(512)} %copy-done.36) | copy-start | bytes 6148
  149.2 43.4 %copy-start.39 = (f32[512]{0:T(512)S(1)}, f32[512]{0:T(512)}, u32[]{:S(2)}) copy-start(f32[512]{0:T(512)} %copy-done.38) | copy-start | bytes 6148
  192.7 4.9 %copy-start.8 = (bf16[512,192]{1,0:T(8,128)(2,1)S(1)}, bf16[512,192]{1,0:T(8,128)(2,1)}, u32[]{:S(2)}) copy-start(bf16[512,192]{1,0:T(8,128)(2,1)} %get-tuple-element.51) | copy-start | bytes 589828
  192.7 5.5 %copy-start.32 = (bf16[768,1]{0,1:T(2,128)(2,1)S(1)}, bf16[768,1]{0,1:T(2,128)(2,1)}, u32[]{:S(2)}) copy-start(bf16[768,1]{0,1:T(2,128)(2,1)} %stack_unstack.18) | copy-start | bytes 4612
  192.7 5.5 %copy-start.33 = (bf16[768,1]{0,1:T(2,128)(2,1)S(1)}, bf16[768,1]{0,1:T(2,128)(2,1)}, u32[]{:S(2)}) copy-start(bf16[768,1]{0,1:T(2,128)(2,1)} %stack_unstack.17) | copy-start | bytes 4612
  192.7 5.5 %copy-start.34 = (bf16[768,1]{0,1:T(2,128)(2,1)S(1)}, bf16[768,1]{0,1:T(2,128)(2,1)}, u32[]{:S(2)}) copy-start(bf16[768,1]{0,1:T(2,128)(2,1)} %stack_unstack.16) | copy-start | bytes 4612
  192.7 5.5 %copy-start.35 = (bf16[768,1]{0,1:T(2,128)(2,1)S(1)}, bf16[768,1]{0,1:T(2,128)(2,1)}, u32[]{:S(2)}) copy-start(bf16[768,1]{0,1:T(2,128)(2,1)} %stack.55) | copy-start | bytes 4612
  203.1 51.8 %copy-start.1 = (bf16[1,128,768]{2,1,0:T(8,128)(2,1)S(1)}, bf16[1,128,768]{2,1,0:T(8,128)(2,1)}, u32[]{:S(2)}) copy-start(bf16[1,128,768]{2,1,0:T(8,128)(2,1)} %param.17) | copy-start | bytes 589828
  203.1 51.8 %copy-start.41 = (f32[128]{0:T(128)S(1)}, f32[128]{0:T(128)}, u32[]{:S(2)}) copy-start(f32[128]{0:T(128)} %copy-done.40) | copy-start | bytes 1540
  203.1 51.8 %copy-start.46 = (f32[128]{0:T(128)S(1)}, f32[128]{0:T(128)}, u32[]{:S(2)}) copy-start(f32[128]{0:T(128)} %add_rsqrt_fusion.1) | copy-start | bytes 1540
  256.2 3.5 %copy-start.18 = (f32[6,768]{1,0:T(8,128)S(1)}, f32[6,768]{1,0:T(8,128)}, u32[]{:S(2)}) copy-start(f32[6,768]{1,0:T(8,128)} %wo_ref.1) | copy-start | bytes 55300
  256.3 4.2 %copy-start.13 = (f32[6,2304]{1,0:T(8,128)S(1)}, f32[6,2304]{1,0:T(8,128)}, u32[]{:S(2)}) copy-start(f32[6,2304]{1,0:T(8,128)} %wq_ref.1) | copy-start | bytes 165892
  256.3 4.1 %copy-start.22 = (f32[6,2304]{1,0:T(8,128)S(1)}, f32[6,2304]{1,0:T(8,128)}, u32[]{:S(2)}) copy-start(f32[6,2304]{1,0:T(8,128)} %param.20) | copy-start | bytes 165892
  256.3 4.1 %copy-start.23 = (f32[6,2304]{1,0:T(8,128)S(1)}, f32[6,2304]{1,0:T(8,128)}, u32[]{:S(2)}) copy-start(f32[6,2304]{1,0:T(8,128)} %param.21) | copy-start | bytes 165892
  (28 other events, 67.7 us)

commit v3 on v2

--- a/solution.py
+++ b/solution.py
@@ -326,69 +326,6 @@
     )
 
 
-def group_sum(parts, cid, name):
-    n = parts.shape[0]
-    rows, cols = parts.shape[3:]
-
-    def kernel(p_ref, o_ref, got, mine, far, cs, cr, zs, zr):
-        y, z, k, x = coords()
-        sib = device(y, z, 1 - k, x)
-        ring_z = [(d, ring(z, d)) for d in (1, 2, 3)]
-        greet([sib] + [device(y, b, k, x) for _, b in ring_z])
-        order = ring_z + [(0, z)]
-        pairs = []
-        for i in range(n):
-            for d, b in order:
-                c = remote(
-                    p_ref.at[i, 1 - k, b], got.at[i, b], cs.at[4 * i + d], cr.at[4 * i + d], sib
-                )
-                c.start()
-                pairs.append(c)
-        copies = []
-        for i in range(n):
-            for d, b in order:
-                pairs[4 * i + (d - 1) % 4].wait_recv()
-                total = p_ref[i, k, b].astype(F32) + got[i, b].astype(F32)
-                if d == 0:
-                    o_ref[i] = total
-                else:
-                    mine[i, d - 1] = total.astype(BF)
-                    c = remote(
-                        mine.at[i, d - 1],
-                        far.at[i, d - 1],
-                        zs.at[3 * i + d - 1],
-                        zr.at[3 * i + d - 1],
-                        device(y, b, k, x),
-                    )
-                    c.start()
-                    copies.append(c)
-        for i in range(n):
-            for d in range(3):
-                copies[3 * i + d].wait_recv()
-            o_ref[i] = (
-                o_ref[i] + far[i, 0].astype(F32) + far[i, 1].astype(F32) + far[i, 2].astype(F32)
-            )
-        for c in copies:
-            c.wait_send()
-        for c in pairs:
-            c.wait_send()
-
-    return comm(
-        kernel,
-        [jax.ShapeDtypeStruct((n, rows, cols), F32)],
-        cid,
-        (4 * n, 4 * n, 3 * n, 3 * n),
-        (parts,),
-        scratch=[
-            pltpu.VMEM((n, 4, rows, cols), BF),
-            pltpu.VMEM((n, 3, rows, cols), BF),
-            pltpu.VMEM((n, 3, rows, cols), BF),
-        ],
-        spaces=([VMEM], [VMEM]),
-        name=name,
-    )[0]
-
-
 def last_sums(one, mix, vec, fc, proj):
     wide = 3200
 
@@ -691,11 +628,11 @@
     return jnp.dot(a, b, preferred_element_type=F32)
 
 
-def attend(query, kv, rows, fc, out, proj):
+def attend(tokens, wq, bias, rows768, rows, fc, out, proj):
     def kernel(
-        q_ref, v_ref, r_ref, f_ref, o_ref, p_ref,
-        ho_ref, ot_ref, lse_ref, vo_ref, ro_ref, fo_ref, oo_ref, po_ref,
-        qt, m_ref, l_ref, h_buf,
+        x_ref, wq_ref, b_ref, g_ref, r_ref, f_ref, o_ref, p_ref,
+        ho_ref, ot_ref, lse_ref, vo_ref, ro_ref, fo_ref, oo_ref, po_ref, q_ref, a_ref, n_ref,
+        qt, m_ref, l_ref, h_buf, v_ref,
         vs, vr, rs, rr, cs, cr, ds, dr, ws, wr, os, orr, hs, hr, gs, gr, loc,
     ):
         y, z, k, x = coords()
@@ -708,20 +645,6 @@
             + [device(y, z, k, ring(x, d)) for d in steps]
         )
 
-        def kv_copy(d):
-            return remote(
-                v_ref, vo_ref.at[y, k], vs.at[d], vr.at[d], device(ring(y, d), z, k, x)
-            )
-
-        for d in steps:
-
-            @pl.when(y + d < 4)
-            def _():
-                kv_copy(d).start()
-
-        swap = remote(v_ref, vo_ref.at[y, k], cs.at[0], cr.at[0], sib)
-        swap.start()
-        vo_ref[y, k] = v_ref[...]
         own_r = pltpu.make_async_copy(r_ref, ro_ref.at[k, z], loc.at[0])
         own_r.start()
         row_copies = []
@@ -752,7 +675,30 @@
                     weight_copy(a, d).start()
                 weight_own(a).start()
 
-        q_t = q_ref[...].T
+        normed, _ = normalize(x_ref[k].reshape(512, 768).astype(F32))
+        n_ref[...] = normed.astype(BF)
+        act = (normed * g_ref[0:1] + g_ref[1:2]).astype(BF)
+        a_ref[...] = act
+        mixed = dot(act, wq_ref[...]) + b_ref[...]
+        v_ref[...] = mixed[:, 192:576].astype(BF)
+
+        def kv_copy(d):
+            return remote(
+                v_ref, vo_ref.at[y, k], vs.at[d], vr.at[d], device(ring(y, d), z, k, x)
+            )
+
+        for d in steps:
+
+            @pl.when(y + d < 4)
+            def _():
+                kv_copy(d).start()
+
+        swap = remote(v_ref, vo_ref.at[y, k], cs.at[0], cr.at[0], sib)
+        swap.start()
+        vo_ref[y, k] = v_ref[...]
+        query = mixed[:, :192].astype(BF) * jnp.asarray(0.125, BF)
+        q_ref[...] = query
+        q_t = query.T
         for head in range(3):
             qt[head] = head_rows(q_t, head)
         m_ref[...] = jnp.full_like(m_ref, -1e30)
@@ -890,30 +836,34 @@
             jax.ShapeDtypeStruct((16, 48, 384), BF),
             jax.ShapeDtypeStruct((2, 16, 48, 384), BF),
             jax.ShapeDtypeStruct((2, 192, 768), BF),
+            jax.ShapeDtypeStruct((512, 192), BF),
+            jax.ShapeDtypeStruct((512, 768), BF),
+            jax.ShapeDtypeStruct((512, 768), BF),
         ],
         2,
         (4, 4, 4, 4, 4, 4, 4, 4, 4, 4, 1, 1, 4, 4, 4, 4, 3),
-        (query, kv, rows, fc, out, proj),
+        (tokens, wq, bias, rows768, rows, fc, out, proj),
         scratch=[
             pltpu.VMEM((3, 192, 512), BF),
             pltpu.VMEM((8, 512), F32),
             pltpu.VMEM((8, 512), F32),
             pltpu.VMEM((512, 192), BF),
+            pltpu.VMEM((512, 384), BF),
         ],
         spaces=(
-            [VMEM, VMEM, ANY, ANY, ANY, ANY],
-            [ANY, VMEM, VMEM, VMEM, ANY, ANY, ANY, ANY],
+            [VMEM, VMEM, VMEM, VMEM, ANY, ANY, ANY, ANY],
+            [ANY, VMEM, VMEM, VMEM, ANY, ANY, ANY, ANY, VMEM, VMEM, VMEM],
         ),
         name="attend",
     )
 
 
-def attend_back(query, branch, wo_rows, kv_all, out_t, lse, fc, proj):
+def attend_back(query, branch, wo, kv_all, out_t, lse, fc, proj):
     def kernel(
         q_ref, b_ref, w_ref, kv_ref, ot_ref, lse_ref, f_ref, p_ref,
-        dq_ref, dkv_ref, bo_ref, fo_ref, po_ref,
+        dq_ref, dkv_ref, fo_ref, po_ref,
         qt, gt, qm, gm, delta, dqt, out_buf, keep, got, far, f_far, p_far,
-        bs, br, cs, cr, ys, yr, fs, fr, ps, pr,
+        cs, cr, ys, yr, fs, fr, ps, pr,
     ):
         y, z, k, x = coords()
         sib = device(y, z, 1 - k, x)
@@ -921,14 +871,8 @@
         greet(
             [sib]
             + [device(ring(y, d), z, k, x) for d in steps]
-            + [device(y, ring(z, d), k, x) for d in steps]
             + [device(y, z, k, ring(x, d)) for d in steps]
         )
-        branches = []
-        for d in steps:
-            c = remote(b_ref, bo_ref.at[z], bs.at[d], br.at[d], device(y, ring(z, d), k, x))
-            c.start()
-            branches.append(c)
         weights = []
         for d in steps:
             b = ring(x, d)
@@ -941,21 +885,21 @@
             )
         for c in weights:
             c.start()
-        bo_ref[z] = b_ref[...]
         query_blk = q_ref[...]
         q_t = query_blk.T
         for head in range(3):
             qt[head] = head_rows(q_t, head)
             qm[head] = head_cols(query_blk, head)
         dqt[...] = jnp.zeros_like(dqt)
-        for c in branches:
-            c.wait_recv()
+        nt = (((1,), (1,)), ((), ()))
+        own_heads = pl.ds(pl.multiple_of(192 * z, 64), 192)
         grad_blk = lax.dot_general(
-            bo_ref[...].reshape(512, 768),
-            w_ref[...],
-            (((1,), (1,)), ((), ())),
-            preferred_element_type=F32,
-        ).astype(BF)
+            b_ref[:, :384], w_ref[0, own_heads], nt, preferred_element_type=F32
+        )
+        grad_blk += lax.dot_general(
+            b_ref[:, 384:], w_ref[1, own_heads], nt, preferred_element_type=F32
+        )
+        grad_blk = grad_blk.astype(BF)
         g_t = grad_blk.T
         for head in range(3):
             at = slice(64 * head, 64 * head + 64)
@@ -1032,8 +976,6 @@
                 remote(keep.at[d], far.at[d], ys.at[d], yr.at[d], sib).wait_recv()
                 dkv_ref[...] += far[d].astype(F32)
 
-        for c in branches:
-            c.wait_send()
         cross(0).wait_send()
         for d in (1, 2, 3):
 
@@ -1047,13 +989,12 @@
         [
             jax.ShapeDtypeStruct((512, 192), BF),
             jax.ShapeDtypeStruct((512, 384), F32),
-            jax.ShapeDtypeStruct((4, 128, 768), BF),
             jax.ShapeDtypeStruct((4, 48, 384), BF),
             jax.ShapeDtypeStruct((2, 48, 768), BF),
         ],
         5,
-        (4, 4, 4, 4, 4, 4, 3, 3, 3, 3),
-        (query, branch, wo_rows, kv_all, out_t, lse, fc, proj),
+        (4, 4, 4, 4, 3, 3, 3, 3),
+        (query, branch, wo, kv_all, out_t, lse, fc, proj),
         scratch=[
             pltpu.VMEM((3, 192, 512), BF),
             pltpu.VMEM((3, 192, 512), BF),
@@ -1068,7 +1009,7 @@
             pltpu.VMEM((3, 4, 48, 384), BF),
             pltpu.VMEM((3, 2, 48, 768), BF),
         ],
-        spaces=([VMEM] * 8, [VMEM] * 5),
+        spaces=([VMEM] * 8, [VMEM] * 4),
         name="attend_back",
     )
 
@@ -1088,11 +1029,166 @@
     )
 
 
-def gelu_tanh(values):
-    return (
-        0.5
-        * values
-        * (1.0 + jnp.tanh(0.7978845608028654 * (values + 0.044715 * values * values * values)))
+def feed_forward(heads_all, x_group, dy_group, wo, wf, wp, rows768, fc_bias):
+    def kernel(
+        h_ref, x_ref, dy_ref, wo_ref, wf_ref, wp_ref, v_ref, fb_ref,
+        out_ref, gx_ref, bo_ref, gwf_ref, gwp_ref, gfb_ref, gv_ref,
+        a2, act, df, x_two, normed, inverse, norm_other, norm_mine, res_other, res_mine,
+        norm_got, res_got, norm_far, res_far, branch,
+        cs, cr, es, er, zs, zr, ws, wr, bs, br,
+    ):
+        y, z, k, x = coords()
+        sib = device(y, z, 1 - k, x)
+        steps = (1, 2, 3)
+        greet([sib] + [device(y, ring(z, d), k, x) for d in steps])
+        out_bias, gain, shift, proj_bias = (v_ref[i : i + 1] for i in range(4))
+
+        def half(kk, norm_ref, res_ref):
+            two = x_ref[kk].reshape(512, 768).astype(F32) + out_bias
+            for g in range(4):
+                h = h_ref[g, kk]
+                at = slice(192 * g, 192 * g + 192)
+                part = jnp.concatenate([dot(h, wo_ref[0, at]), dot(h, wo_ref[1, at])], 1)
+                two = two + part
+            x_two[...] = two
+            n, inv = normalize(two)
+            normed[...] = n
+            inverse[...] = jnp.broadcast_to(inv, (512, 128))
+            a = (n * gain + shift).astype(BF)
+            a2[kk] = a
+            hidden = dot(a, wf_ref[...]) + fb_ref[...]
+            square = hidden * hidden
+            t = jnp.tanh(0.7978845608028654 * (hidden + 0.044715 * square * hidden))
+            act_blk = (0.5 * hidden * (1.0 + t)).astype(BF)
+            act[kk] = act_blk
+            slope = 0.5 * (1.0 + t) + 0.5 * hidden * (1.0 - t * t) * (
+                0.7978845608028654 * (1.0 + 3 * 0.044715 * square)
+            )
+            dy = dy_ref[kk].reshape(512, 768)
+            back = lax.dot_general(
+                dy, wp_ref[...], (((1,), (1,)), ((), ())), preferred_element_type=F32
+            )
+            df_blk = (back * slope).astype(BF)
+            df[kk] = df_blk
+            norm_part = lax.dot_general(
+                df_blk, wf_ref[...], (((1,), (1,)), ((), ())), preferred_element_type=F32
+            )
+            norm_ref[...] = norm_part.astype(BF).reshape(4, 128, 768)
+            res_ref[...] = dot(act_blk, wp_ref[...]).astype(BF).reshape(4, 128, 768)
+
+        half(1 - k, norm_other, res_other)
+        swaps = []
+        for d in (1, 2, 3, 0):
+            b = ring(z, d)
+            c = remote(norm_other.at[b], norm_got.at[b], cs.at[d], cr.at[d], sib)
+            c.start()
+            swaps.append(c)
+        for d in (1, 2, 3, 0):
+            b = ring(z, d)
+            c = remote(res_other.at[b], res_got.at[b], es.at[d], er.at[d], sib)
+            c.start()
+            swaps.append(c)
+        half(k, norm_mine, res_mine)
+        sends = []
+        for i, (mine, got, far, s, r) in enumerate(
+            ((norm_mine, norm_got, norm_far, zs, zr), (res_mine, res_got, res_far, ws, wr))
+        ):
+            for d in steps:
+                b = ring(z, d)
+                swaps[4 * i + d - 1].wait_recv()
+                mine[b] = (mine[b].astype(F32) + got[b].astype(F32)).astype(BF)
+                c = remote(
+                    mine.at[b], far.at[d - 1], s.at[d - 1], r.at[d - 1], device(y, b, k, x)
+                )
+                c.start()
+                sends.append(c)
+        tn = (((0,), (0,)), ((), ()))
+        gwf = lax.dot_general(a2[0], df[0], tn, preferred_element_type=F32)
+        gwf += lax.dot_general(a2[1], df[1], tn, preferred_element_type=F32)
+        gwf_ref[...] = gwf.astype(BF)
+        own_rows = pl.ds(pl.multiple_of(128 * z, 128), 128)
+        swaps[3].wait_recv()
+        for c in sends[:3]:
+            c.wait_recv()
+        da = (
+            norm_mine[z].astype(F32)
+            + norm_got[z].astype(F32)
+            + norm_far[0].astype(F32)
+            + norm_far[1].astype(F32)
+            + norm_far[2].astype(F32)
+        )
+        n = normed[own_rows]
+        dy = dy_ref[k, z].astype(F32)
+        gx = dy + normalize_back(n, inverse[own_rows, 0:1], gain, da)
+        gx_ref[...] = gx
+        low = gx.astype(BF)
+        branch[...] = low
+        bo_ref[z] = low
+        branches = []
+        for d in steps:
+            c = remote(
+                branch, bo_ref.at[z], bs.at[d - 1], br.at[d - 1], device(y, ring(z, d), k, x)
+            )
+            c.start()
+            branches.append(c)
+        gwp = lax.dot_general(
+            act[0], dy_ref[0].reshape(512, 768), tn, preferred_element_type=F32
+        )
+        gwp += lax.dot_general(
+            act[1], dy_ref[1].reshape(512, 768), tn, preferred_element_type=F32
+        )
+        gwp_ref[...] = gwp.astype(BF)
+        gfb_ref[...] = jnp.sum(df[0].astype(F32), 0, keepdims=True) + jnp.sum(
+            df[1].astype(F32), 0, keepdims=True
+        )
+        gv_ref[0:1] = jnp.sum(low.astype(F32), 0, keepdims=True)
+        gv_ref[1:2] = jnp.sum(da * n, 0, keepdims=True)
+        gv_ref[2:3] = jnp.sum(da, 0, keepdims=True)
+        gv_ref[3:4] = jnp.sum(dy, 0, keepdims=True)
+        swaps[7].wait_recv()
+        for c in sends[3:]:
+            c.wait_recv()
+        out_ref[...] = (
+            x_two[own_rows]
+            + proj_bias
+            + res_mine[z].astype(F32)
+            + res_got[z].astype(F32)
+            + res_far[0].astype(F32)
+            + res_far[1].astype(F32)
+            + res_far[2].astype(F32)
+        )
+        for c in branches:
+            c.wait()
+        for c in swaps + sends:
+            c.wait_send()
+
+    return comm(
+        kernel,
+        [
+            jax.ShapeDtypeStruct((128, 768), F32),
+            jax.ShapeDtypeStruct((128, 768), F32),
+            jax.ShapeDtypeStruct((4, 128, 768), BF),
+            jax.ShapeDtypeStruct((768, 384), BF),
+            jax.ShapeDtypeStruct((384, 768), BF),
+            jax.ShapeDtypeStruct((1, 384), F32),
+            jax.ShapeDtypeStruct((4, 768), F32),
+        ],
+        3,
+        (4, 4, 4, 4, 3, 3, 3, 3, 3, 3),
+        (heads_all, x_group, dy_group, wo, wf, wp, rows768, fc_bias),
+        scratch=[
+            pltpu.VMEM((2, 512, 768), BF),
+            pltpu.VMEM((2, 512, 384), BF),
+            pltpu.VMEM((2, 512, 384), BF),
+            pltpu.VMEM((512, 768), F32),
+            pltpu.VMEM((512, 768), F32),
+            pltpu.VMEM((512, 128), F32),
+        ]
+        + [pltpu.VMEM((4, 128, 768), BF)] * 6
+        + [pltpu.VMEM((3, 128, 768), BF)] * 2
+        + [pltpu.VMEM((128, 768), BF)],
+        spaces=([VMEM] * 8, [VMEM] * 7),
+        name="feed_forward",
     )
 
 
@@ -1129,72 +1225,47 @@
         w_qkv, w_fc, w_out, w_proj, vectors, tokens[0]
     )
     wq = wq.reshape(768, 640)
-    vec = wq[:, 576:588].astype(F32)
-    wq = wq[:, :576]
-    gain_one, shift_one, q_bias, v_bias = vec[:, 0], vec[:, 1], vec[:, 2], vec[:, 3]
-    out_bias, gain_two, shift_two, proj_bias = vec[:, 4], vec[:, 5], vec[:, 6], vec[:, 7]
-    fc_bias = lax.dynamic_slice(vec[:, 8:].T.reshape(-1), ((2 * z + k) * 384,), (384,))
+    vec_rows = wq[:, 576:592].astype(F32).T
+    gain_one = vec_rows[0]
     bias = jnp.concatenate(
         [
-            lax.dynamic_slice(q_bias, (192 * z,), (192,)),
-            jnp.zeros((192,), F32),
-            lax.dynamic_slice(v_bias, (192 * z,), (192,)),
-        ]
-    )
-    x_core = lax.dynamic_index_in_dim(x_group, k, 0, False).reshape(512, 768).astype(F32)
-    normed_core, _ = normalize(x_core)
-    act_one = (normed_core * gain_one + shift_one).astype(BF)
-    mixed = (dot(act_one, wq) + bias).astype(BF)
-    query = mixed[:, :192] * jnp.asarray(0.125, BF)
-    heads_all, out_t, lse, kv_all, dy_group, wf, wo, wp = attend(
-        query, mixed[:, 192:], cotangent[0], fc_part, out_part, proj_part
-    )
-    wf = wf.reshape(768, 384)
-    wo = jnp.concatenate([wo[0].reshape(768, 384), wo[1].reshape(768, 384)], 1)
-    wp = wp.reshape(384, 768)
-    heads_all = jnp.concatenate([heads_all[i].reshape(1024, 192) for i in range(4)], 1)
-    x_two = x_group.reshape(1024, 768).astype(F32) + dot(heads_all, wo) + out_bias
-    normed_two, inverse_two = normalize(x_two)
-    act_two = (normed_two * gain_two + shift_two).astype(BF)
-    hidden = dot(act_two, wf) + fc_bias
-    gelu_out, gelu_back = jax.vjp(gelu_tanh, hidden)
-    act_three = gelu_out.astype(BF)
-    dy = dy_group.reshape(1024, 768)
-    result_part = dot(act_three, wp).astype(BF)
-    grad_w_proj = dot(act_three.T, dy)
-    grad_hidden = gelu_back(dot(dy, wp.T))[0].astype(BF)
-    grad_w_fc = dot(act_two.T, grad_hidden)
-    grad_fc_bias = jnp.sum(grad_hidden.astype(F32), 0)
-    norm_part = dot(grad_hidden, wf.T).astype(BF)
-    sums = group_sum(
-        jnp.stack([norm_part, result_part]).reshape(2, 2, 4, 128, 768), 8, "ffn_sum"
-    )
-
-    def own(group):
-        return lax.dynamic_slice(group, ((k * 4 + z) * 128, 0), (128, group.shape[1]))
-
-    own_x_two = own(x_two)
-    output = own_x_two + sums[1] + proj_bias
-    own_normed, own_inverse = normalize(own_x_two)
-    grad_output = cotangent[0].astype(F32)
-    grad_norm_two = sums[0]
-    grad_x_two = grad_output + normalize_back(own_normed, own_inverse, gain_two, grad_norm_two)
-    grad_branch = grad_x_two.astype(BF)
-    wo_rows = lax.dynamic_slice(wo, (192 * z, 0), (192, 768))
-    grad_query, grad_kv, branch_core, fc_sum, proj_sum = attend_back(
+            lax.dynamic_slice(vec_rows, (2, 192 * z), (1, 192)),
+            jnp.zeros((1, 192), F32),
+            lax.dynamic_slice(vec_rows, (3, 192 * z), (1, 192)),
+            jnp.zeros((1, 64), F32),
+        ],
+        1,
+    )
+    fc_bias = lax.dynamic_slice(vec_rows[8:12].reshape(1, 3072), (0, (2 * z + k) * 384), (1, 384))
+    heads_all, out_t, lse, kv_all, dy_group, wf, wo, wp, query, act_one, normed_core = attend(
+        x_group, wq, bias, vec_rows[0:2], cotangent[0], fc_part, out_part, proj_part
+    )
+    wo = wo.reshape(2, 768, 384)
+    output, grad_x_two, branch_core, grad_w_fc, grad_w_proj, grad_fc_bias, vec_sums = feed_forward(
+        heads_all,
+        x_group,
+        dy_group,
+        wo,
+        wf.reshape(768, 384),
+        wp.reshape(384, 768),
+        vec_rows[4:8],
+        fc_bias,
+    )
+    branch_core = branch_core.reshape(512, 768)
+    grad_query, grad_kv, fc_sum, proj_sum = attend_back(
         query,
-        grad_branch,
-        wo_rows,
+        branch_core,
+        wo,
         kv_all,
         out_t,
         lse,
-        grad_w_fc.astype(BF).reshape(4, 4, 48, 384),
-        grad_w_proj.astype(BF).reshape(2, 4, 48, 768),
-    )
-    branch_core = branch_core.reshape(512, 768)
+        grad_w_fc.reshape(4, 4, 48, 384),
+        grad_w_proj.reshape(2, 4, 48, 768),
+    )
     grad_mixed = jnp.concatenate([grad_query, grad_kv.astype(BF)], 1)
     branch_cols = lax.dynamic_slice(branch_core, (0, 192 * z), (512, 192))
-    heads_core = lax.dynamic_index_in_dim(heads_all.reshape(2, 512, 768), k, 0, False)
+    heads_core = lax.dynamic_index_in_dim(heads_all, k, 1, False)
+    heads_core = jnp.concatenate([heads_core[i] for i in range(4)], 1)
     left = jnp.concatenate([act_one, heads_core], 0)
     gap = jnp.zeros((512, 96), BF)
     room = jnp.zeros((512, 288), BF)
@@ -1206,7 +1277,7 @@
         0,
     )
     grad_mix = dot(left.T, right).astype(BF)
-    one_part = dot(grad_mixed, wq.T)
+    one_part = dot(grad_mixed, wq[:, :576].T)
 
     def spread(piece, at, size):
         return lax.dynamic_update_slice(jnp.zeros((size,), F32), piece, (at,))
@@ -1214,16 +1285,16 @@
     mixed_sums = jnp.sum(grad_mixed.astype(F32), 0)
     columns = jnp.stack(
         [
-            jnp.sum(one_part * normed_core, 0),
+            jnp.sum(one_part * normed_core.astype(F32), 0),
             jnp.sum(one_part, 0),
             spread(mixed_sums[:192], 192 * z, 768),
             spread(mixed_sums[384:], 192 * z, 768),
-            jnp.sum(grad_branch.astype(F32), 0),
-            jnp.sum(grad_norm_two * own_normed, 0),
-            jnp.sum(grad_norm_two, 0),
-            jnp.sum(grad_output, 0),
+            vec_sums[0],
+            vec_sums[1],
+            vec_sums[2],
+            vec_sums[3],
         ]
-        + list(spread(grad_fc_bias, (2 * z + k) * 384, 3072).reshape(4, 768)),
+        + list(spread(grad_fc_bias[0], (2 * z + k) * 384, 3072).reshape(4, 768)),
         1,
     )
     grad_vec = jnp.pad(columns, ((0, 0), (0, 116))).astype(BF)

time: 263 us -> 234 us (0.89)
  other arithmetic: 26.3 us -> 9.04 us
  matrix products: 19.4 us -> 4.36 us
  Pallas kernels: 201 us -> 208 us
  local copies, waits for them, and re-layouts: 14.8 us -> 10.6 us
    dot_general x10 -> x2, matrix products: 19.4 us -> 4.36 us  [dot(): return jnp.dot(a, b, preferred_element_type=F32)]
    pallas_call x5, Pallas kernels: 201 us -> 208 us  [comm(): pl.pallas_call(kernel, out_shape=outs, in_specs=[ANY] * len(args) if spac...]
    reduce_sum x4 -> x0, other arithmetic: 5.67 us -> none  [the longest x1 2.02 us: shards(): jnp.sum(grad_norm_two * own_normed, 0)]
    another operation x14 -> x11, local copies, waits for them, and re-layouts: 3.66 us -> 0.15 us  [the longest x10 0.14 us: shards(): jnp.stack([jnp.sum(one_part * normed_core.astype(F32), 0), jnp.sum(one_pa...]
    reduce_sum x4 -> x1, other arithmetic: 3.37 us -> 0.2 us  [normalize(): jnp.mean(centered * centered, -1, keepdims=True) + EPSILON]
where the time goes in v3:
time: 234 us; the launch traced here: 233 us
  Pallas kernels  208 us (89%)
  local copies, waits for them, and re-layouts  10.6 us (5%)
  other arithmetic  9.04 us (4%)
  matrix products  4.36 us (2%)
    pallas_call x5, Pallas kernels, comm(): pl.pallas_call(kernel, out_shape=outs, in_specs=[ANY] * len(args) if spac...  208 us

profile of v3, /device:TPU:29, one launch (start us, length us, event | category | flops | bytes accessed | tf_op | source)
XLA Modules:
  0.0 233.4 jit_solution(15937421807379886614)
XLA Ops:
  0.7 37.0 %first_gather.1 = (bf16[16,48,640]{2,1,0:T(8,128)(2,1)}, bf16[16,48,384]{2,1,0:T(8,128)(2,1)}, bf16[16,48,384]{2,1,0:T(8,128)(2,1)}, bf16[2,192,768]{2,1,0:T(8,128)(2,1)}, bf16[2,4,128,768]{3,2,1,0:T(8,128)(2,1)}) custom-call(f32[6,2304]{1,0:T(8,128)} %wq_ref.1, f32[6,3072]{1,0:T(8,128)} %wf_ref.1, f32[6,768]{1,0:T(8,128)} %wo_ref.1, f32[24,768]{1,0:T(8,128)} %wp_ref.1, ...), custom_call_target="tpu_custom_call" | custom-call | tf_op jit(solution)/shard_map/first_gather/pallas_call | solution.py:48
  37.7 1.0 slice.125
  39.7 0.6 slice.126.g_ref
  40.3 47.5 %attend.1 = (bf16[4,2,512,192]{3,2,1,0:T(8,128)(2,1)}, f32[192,512]{1,0:T(8,128)}, f32[8,512]{1,0:T(8,128)}, bf16[4,2,512,384]{3,2,1,0:T(8,128)(2,1)}, bf16[2,4,...) custom-call(bf16[2,4,128,768]{3,2,1,0:T(8,128)(2,1)} %get-tuple-elem, ...), custom_call_target="tpu_custom_call" | custom-call | tf_op jit(solution)/shard_map/attend/pallas_call | solution.py:48
  87.9 0.6 slice_bitcast_fusion.2
  89.1 40.9 %feed_forward.1 = (f32[128,768]{1,0:T(8,128)}, f32[128,768]{1,0:T(8,128)}, bf16[4,128,768]{2,1,0:T(8,128)(2,1)}, bf16[768,384]{1,0:T(8,128)(2,1)}, bf16[384,768]...) custom-call(bf16[4,2,512,192]{3,2,1,0:T(8,128)(2,1)} %get-tuple-element.52.h_ref, ...), custom_call_target="tpu_custom_call" | custom-call | tf_op jit(solution)/shard_map/feed_forward/pallas_call | solution.py:48
  130.0 31.8 %attend_back.1 = (bf16[512,192]{1,0:T(8,128)(2,1)}, f32[512,384]{1,0:T(8,128)}, bf16[4,48,384]{2,1,0:T(8,128)(2,1)}, bf16[2,48,768]{2,1,0:T(8,128)(2,1)}) custom-call(bf16[512,192]{1,0:T(8,128)(2,1)} %get-tuple-element.59.q_ref, bf16[512,768]{1,0:T(8,128)(2,1)} %bitcast.69, bf16[2,768,384]{2,1,0:T(8,128)(2,1)} %bitcast.65, ...), custom_call_target="tpu_custom_call" | custom-call | tf_op jit(solution)/shard_map/attend_back/pallas_call | solution.py:48
  161.8 1.3 convert_element_type.26
  163.1 1.2 convert_reduce_fusion
  165.1 1.7 fusion.52
  167.2 0.7 pad.5.clone
  168.2 1.3 constant_dynamic-slice_fusion
  169.7 1.0 copy-done.26
  170.6 2.6 %fusion.25 = bf16[768,768]{1,0:T(8,128)(2,1)} fusion(bf16[512,96]{1,0:T(8,128)(2,1)S(1)} %get-tuple-element.102, bf16[512,288]{1,0:T(8,128)(2,1)S(1)} %broadcast_in_dim.29, bf16[512,96]{1,0:T(8,128)(2,1)S(1)} %get-tuple-element.101, bf16[512,96]{1,0:T(8,128)(2,1)S(1)} %broadcast_in_dim.28, bf16[512,288]{1,0:T(8,128)(2,1)S(1)} %get-tuple-element.104, ...), kind=kOutput, calls=%fused_computation.26 | convolution fusion | flops 1228996608 | bytes 3932160 | tf_op jit(solution)/shard_map/dot_general | solution.py:628
  173.3 50.9 %last_sums.1 = (f32[128,768]{1,0:T(8,128)}, f32[2,8,3200]{2,1,0:T(8,128)}, f32[24,768]{1,0:T(8,128)}) custom-call(bf16[4,128,768]{2,1,0:T(8,128)(2,1)} %bitcast.73, bf16[4,4,48,768]{3,2,1,0:T(8,128)(2,1)} %bitcast.71, bf16[4,4,48,128]{3,2,1,0:T(8,128)(2,1)} %bitcast.72, bf16[4,48,384]{2,1,0:T(8,128)(2,1)} %get-tuple-element.72.fc_ref, ...), custom_call_target="tpu_custom_call" | custom-call | tf_op jit(solution)/shard_map/last_sums/pallas_call | solution.py:48
  224.2 1.1 fusion.59
  225.7 0.7 multiply_subtract_fusion.2
  226.7 0.8 multiply_subtract_fusion
  227.7 0.6 multiply_subtract_fusion.3
  228.3 0.8 slice_reduce_fusion
  229.7 0.9 fusion.40
  230.6 0.7 multiply_subtract_fusion.1
  231.3 1.3 multiply_subtract_fusion.4
  232.7 0.7 copy.65
  (106 shorter events, 4.3 us)
Async XLA Ops:
  38.9 49.0 %copy-start.10 = (f32[16,768]{1,0:T(8,128)}, f32[16,768]{1,0:T(8,128)S(1)}, u32[]{:S(2)}) copy-start(f32[16,768]{1,0:T(8,128)S(1)} %get-tuple-element.111) | copy-start | bytes 147460
  130.0 35.1 %copy-start.27 = (bf16[512,768]{1,0:T(8,128)(2,1)S(1)}, bf16[512,768]{1,0:T(8,128)(2,1)}, u32[]{:S(2)}) copy-start(bf16[512,768]{1,0:T(8,128)(2,1)} %get-tuple-element.69) | copy-start | bytes 2359300
  161.8 2.9 %copy-start.25 = (f32[1,384]{1,0:T(1,128)S(1)}, f32[1,384]{1,0:T(1,128)}, u32[]{:S(2)}) copy-start(f32[1,384]{1,0:T(1,128)} %get-tuple-element.71) | copy-start | bytes 4612
  161.8 3.3 %copy-start.3 = (bf16[16,48,640]{2,1,0:T(8,128)(2,1)S(1)}, bf16[16,48,640]{2,1,0:T(8,128)(2,1)}, u32[]{:S(2)}) copy-start(bf16[16,48,640]{2,1,0:T(8,128)(2,1)} %get-tuple-element.48) | copy-start | bytes 2949124
  161.8 3.3 %copy-start.4 = (bf16[512,192]{1,0:T(8,128)(2,1)S(1)}, bf16[512,192]{1,0:T(8,128)(2,1)}, u32[]{:S(2)}) copy-start(bf16[512,192]{1,0:T(8,128)(2,1)} %get-tuple-element.66) | copy-start | bytes 589828
  166.8 2.7 %copy-start.1 = (bf16[4,2,512,192]{3,2,1,0:T(8,128)(2,1)S(1)}, bf16[4,2,512,192]{3,2,1,0:T(8,128)(2,1)}, u32[]{:S(2)}) copy-start(bf16[4,2,512,192]{3,2,1,0:T(8,128)(2,1)} %get-tuple-element.52.h_ref) | copy-start | bytes 4718596
  173.3 52.4 %copy-start.8 = (f32[6,2304]{1,0:T(8,128)S(1)}, f32[6,2304]{1,0:T(8,128)}, u32[]{:S(2)}) copy-start(f32[6,2304]{1,0:T(8,128)} %wq_ref.1) | copy-start | bytes 165892
  173.3 52.4 %copy-start.14 = (f32[6,2304]{1,0:T(8,128)S(1)}, f32[6,2304]{1,0:T(8,128)}, u32[]{:S(2)}) copy-start(f32[6,2304]{1,0:T(8,128)} %param.20) | copy-start | bytes 165892
  173.3 52.5 %copy-start.15 = (f32[6,2304]{1,0:T(8,128)S(1)}, f32[6,2304]{1,0:T(8,128)}, u32[]{:S(2)}) copy-start(f32[6,2304]{1,0:T(8,128)} %param.21) | copy-start | bytes 165892
  224.1 2.5 %copy-start.7 = (f32[6,3072]{1,0:T(8,128)S(1)}, f32[6,3072]{1,0:T(8,128)}, u32[]{:S(2)}) copy-start(f32[6,3072]{1,0:T(8,128)} %wf_ref.1) | copy-start | bytes 221188
  224.2 3.5 %copy-start.11 = (f32[6,768]{1,0:T(8,128)S(1)}, f32[6,768]{1,0:T(8,128)}, u32[]{:S(2)}) copy-start(f32[6,768]{1,0:T(8,128)} %wo_ref.1) | copy-start | bytes 55300
  224.2 3.5 %copy-start.19 = (f32[6,768]{1,0:T(8,128)S(1)}, f32[6,768]{1,0:T(8,128)}, u32[]{:S(2)}) copy-start(f32[6,768]{1,0:T(8,128)} %param.23) | copy-start | bytes 55300
  224.2 3.5 %copy-start.20 = (f32[6,768]{1,0:T(8,128)S(1)}, f32[6,768]{1,0:T(8,128)}, u32[]{:S(2)}) copy-start(f32[6,768]{1,0:T(8,128)} %param.24) | copy-start | bytes 55300
  225.3 3.8 %copy-start = (bf16[1,128,768]{2,1,0:T(8,128)(2,1)S(1)}, bf16[1,128,768]{2,1,0:T(8,128)(2,1)}, u32[]{:S(2)}) copy-start(bf16[1,128,768]{2,1,0:T(8,128)(2,1)} %param.17) | copy-start | bytes 589828
  225.4 4.1 %copy-start.2 = (f32[128,768]{1,0:T(8,128)S(1)}, f32[128,768]{1,0:T(8,128)}, u32[]{:S(2)}) copy-start(f32[128,768]{1,0:T(8,128)} %get-tuple-element.74) | copy-start | bytes 1179652
  225.6 4.1 %copy-start.6 = (f32[128,768]{1,0:T(8,128)S(1)}, f32[128,768]{1,0:T(8,128)}, u32[]{:S(2)}) copy-start(f32[128,768]{1,0:T(8,128)} %get-tuple-element.58) | copy-start | bytes 1179652
  226.6 4.0 %copy-start.9 = (f32[24,768]{1,0:T(8,128)S(1)}, f32[24,768]{1,0:T(8,128)}, u32[]{:S(2)}) copy-start(f32[24,768]{1,0:T(8,128)} %wp_ref.1) | copy-start | bytes 221188
  226.6 4.0 %copy-start.16 = (f32[24,768]{1,0:T(8,128)S(1)}, f32[24,768]{1,0:T(8,128)}, u32[]{:S(2)}) copy-start(f32[24,768]{1,0:T(8,128)} %param.29) | copy-start | bytes 221188
  226.7 4.0 %copy-start.17 = (f32[24,768]{1,0:T(8,128)S(1)}, f32[24,768]{1,0:T(8,128)}, u32[]{:S(2)}) copy-start(f32[24,768]{1,0:T(8,128)} %param.30) | copy-start | bytes 221188
  226.7 4.0 %copy-start.18 = (f32[24,768]{1,0:T(8,128)S(1)}, f32[24,768]{1,0:T(8,128)}, u32[]{:S(2)}) copy-start(f32[24,768]{1,0:T(8,128)} %get-tuple-element.76) | copy-start | bytes 221188
  227.5 3.8 %copy-start.21 = (f32[6,12]{1,0:T(8,128)S(1)}, f32[6,12]{1,0:T(8,128)}, u32[]{:S(2)}) copy-start(f32[6,12]{1,0:T(8,128)} %wv_ref.1) | copy-start | bytes 868
  227.5 3.8 %copy-start.23 = (f32[6,12]{1,0:T(8,128)S(1)}, f32[6,12]{1,0:T(8,128)}, u32[]{:S(2)}) copy-start(f32[6,12]{1,0:T(8,128)} %param.32) | copy-start | bytes 868
  227.5 3.8 %copy-start.24 = (f32[6,12]{1,0:T(8,128)S(1)}, f32[6,12]{1,0:T(8,128)}, u32[]{:S(2)}) copy-start(f32[6,12]{1,0:T(8,128)} %param.33) | copy-start | bytes 868
  227.7 5.0 %copy-start.5 = (f32[128,768]{1,0:T(8,128)S(1)}, f32[128,768]{1,0:T(8,128)}, u32[]{:S(2)}) copy-start(f32[128,768]{1,0:T(8,128)} %get-tuple-element.57) | copy-start | bytes 1179652
  (4 other events, 7.8 us)

commit v4 on v3

--- a/solution.py
+++ b/solution.py
@@ -326,15 +326,26 @@
     )
 
 
-def last_sums(one, mix, vec, fc, proj):
+def last_sums(pieces, fc, proj, state):
     wide = 3200
 
-    def kernel(
-        one_ref, mix_ref, vec_ref, fc_ref, proj_ref, one_out, rows_out, proj_out,
-        one_far, mix_got, mix_sum, mix_far, vec_far, mix_mine, vec_mine,
-        mix_all, fc_all, vec_all, proj_all, proj_sum, out_send,
+    def kernel(*refs):
+        (
+            act_ref, n_ref, h_ref, gq_ref, gkv_ref, br_ref, wq_ref, vs_ref, fb_ref,
+            tok_ref, gx_ref, gain_ref, fc_ref, proj_ref,
+        ) = refs[:14]
+        state_ref = refs[14:29]
+        gin_ref = refs[29]
+        new_ref = refs[30:45]
+        (
+            one_far, mix_got, mix_sum, mix_far, vec_far, mix_mine, vec_mine,
+            mix_all, fc_all, vec_all, proj_all, proj_sum, out_send,
+            one_ref, mix_other, mix_ref, vec_ref, rows_out, proj_out,
+            act_t, heads, heads_t, d_ref, right_one, right_two, vec_rows, g_qkv, g_out, g_fc,
+        ) = refs[45:74]
+        (
         zs, zr, cs, cr, s1, r1, s2, r2, s3, r3, s4, r4, s5, r5, s6, r6, s7, r7, s8, r8, loc,
-    ):
+        ) = refs[74:]
         y, z, k, x = coords()
         me = y * 4 + z
         sib = device(y, z, 1 - k, x)
@@ -349,26 +360,61 @@
                 if (a, b) != (0, 0)
             ]
         )
-        mine_at = pl.ds(pl.multiple_of(384 * k, 128), 384)
-        other_at = pl.ds(pl.multiple_of(384 * (1 - k), 128), 384)
+        d_ref[:, 0:192] = gq_ref[...]
+        d_ref[:, 192:576] = gkv_ref[...].astype(BF)
+        d_ref[:, 576:640] = jnp.zeros((512, 64), BF)
+        right_one[...] = jnp.zeros_like(right_one)
+        right_one[:, 0:288] = d_ref[:, 0:288]
+        right_one[:, 384:672] = d_ref[:, 288:576]
+        right_two[...] = jnp.zeros_like(right_two)
+        vec_rows[...] = jnp.zeros_like(vec_rows)
+        sums = jnp.sum(d_ref[...].astype(F32), 0, keepdims=True)
+        at_half = pl.ds(pl.multiple_of(384 * k, 128), 384)
+        for b in range(4):
+            heads[:, 192 * b : 192 * b + 192] = h_ref[b, k]
+
+            @pl.when(z == b)
+            def _():
+                right_two[:, 288:384] = br_ref[:, 192 * b : 192 * b + 96]
+                right_two[:, 672:768] = br_ref[:, 192 * b + 96 : 192 * b + 192]
+                vec_rows[2:3, 192 * b : 192 * b + 192] = sums[:, 0:192]
+                vec_rows[3:4, 192 * b : 192 * b + 192] = sums[:, 384:576]
+                vec_rows[8 + b : 9 + b, at_half] = fb_ref[...]
+
+        vec_rows[4:8] = vs_ref[...]
+        act_t[...] = act_ref[...].T
+        heads_t[...] = heads[...].T
+
+        def product(h):
+            at = pl.ds(pl.multiple_of(384 * h, 128), 384)
+            total = dot(act_t[...], right_one[:, at]) + dot(heads_t[...], right_two[:, at])
+            return total.reshape(4, 4, 48, 384)
+
+        mix_other[...] = product(1 - k).astype(BF)
         swap = []
         for d in (1, 2, 3, 0):
             b = ring(x, d)
-            c = remote(mix_ref.at[:, b, :, other_at], mix_got.at[b], cs.at[d], cr.at[d], sib)
+            c = remote(mix_other.at[:, b], mix_got.at[b], cs.at[d], cr.at[d], sib)
             c.start()
             swap.append(c)
+        mix_ref[...] = product(k).astype(BF)
+        one = lax.dot_general(
+            d_ref[...], wq_ref[...], (((1,), (1,)), ((), ())), preferred_element_type=F32
+        )
+        one_ref[...] = one.astype(BF).reshape(4, 128, 768)
+        vec_rows[0:1] = jnp.sum(one * n_ref[...].astype(F32), 0, keepdims=True)
+        vec_rows[1:2] = jnp.sum(one, 0, keepdims=True)
+        vec_ref[...] = vec_rows[...].T.astype(BF).reshape(4, 4, 48, 128)
         along = []
         for d in steps:
             b = ring(x, d)
             to = device(y, z, k, b)
+            swap[d - 1].wait_recv()
+            mix_sum[d] = (mix_ref[:, b].astype(F32) + mix_got[b].astype(F32)).astype(BF)
+            c = remote(mix_sum.at[d], mix_far.at[d - 1], s1.at[d - 1], r1.at[d - 1], to)
+            c.start()
+            along.append(c)
             c = remote(vec_ref.at[:, b], vec_far.at[d - 1], s2.at[d - 1], r2.at[d - 1], to)
-            c.start()
-            along.append(c)
-            swap[d - 1].wait_recv()
-            mix_sum[d] = (
-                mix_ref[:, b, :, mine_at].astype(F32) + mix_got[b].astype(F32)
-            ).astype(BF)
-            c = remote(mix_sum.at[d], mix_far.at[d - 1], s1.at[d - 1], r1.at[d - 1], to)
             c.start()
             along.append(c)
         ones = []
@@ -438,7 +484,7 @@
         for c in along:
             c.wait_recv()
         mix_mine[...] = (
-            mix_ref[:, x, :, mine_at].astype(F32)
+            mix_ref[:, x].astype(F32)
             + mix_got[x].astype(F32)
             + mix_far[0].astype(F32)
             + mix_far[1].astype(F32)
@@ -454,12 +500,14 @@
         all_start(vec_mine, vec_all, s5, r5)
         for c in ones:
             c.wait_recv()
-        one_out[...] = (
+        grad = (
             one_ref[z].astype(F32)
             + one_far[0].astype(F32)
             + one_far[1].astype(F32)
             + one_far[2].astype(F32)
         )
+        normed, inverse = normalize(tok_ref[...].astype(F32))
+        gin_ref[...] = gx_ref[...] + normalize_back(normed, inverse, gain_ref[...], grad)
 
         def proj_last(i):
             return remote(
@@ -552,6 +600,34 @@
         def _():
             remote(proj_sum.at[0], proj_out, s8.at[0], r8.at[0], sib).wait_recv()
 
+        for b in range(4):
+            one_half = rows_out[0, 0:6, 384 * b : 384 * b + 384]
+            two_half = rows_out[1, 0:6, 384 * b : 384 * b + 384]
+            q = 192 * b
+            g_qkv[:, q : q + 192] = one_half[:, 0:192]
+            g_qkv[:, 768 + q : 864 + q] = one_half[:, 192:288]
+            g_qkv[:, 864 + q : 960 + q] = two_half[:, 0:96]
+            g_qkv[:, 1536 + q : 1728 + q] = two_half[:, 96:288]
+            g_out[:, q : q + 96] = one_half[:, 288:384]
+            g_out[:, q + 96 : q + 192] = two_half[:, 288:384]
+            for j in range(2):
+                at = 384 * (2 * b + j)
+                g_fc[:, at : at + 384] = rows_out[j, 0:6, 1536 + 384 * b : 1920 + 384 * b]
+        g_vec = rows_out[0, 0:6, 3072:3084] + rows_out[1, 0:6, 3072:3084]
+        for i, (gradient, rate, decay) in enumerate(
+            (
+                (g_qkv[...], 0.1, 0.1),
+                (g_out[...], 0.3, 0.1),
+                (g_fc[...], 0.05, 0.1),
+                (proj_out[...], 0.03, 0.1),
+                (g_vec, 0.5, 0.0),
+            )
+        ):
+            w, m, v = state_ref[3 * i : 3 * i + 3]
+            results = adam_update(w[...], m[...], v[...], gradient, rate, decay)
+            for j in range(3):
+                new_ref[3 * i + j][...] = results[j]
+
         @pl.when(z == x)
         def _():
             for i in range(8):
@@ -582,12 +658,11 @@
         kernel,
         [
             jax.ShapeDtypeStruct((128, 768), F32),
-            jax.ShapeDtypeStruct((2, 8, wide), F32),
-            jax.ShapeDtypeStruct((24, 768), F32),
-        ],
+        ]
+        + [jax.ShapeDtypeStruct(one.shape, F32) for one in state],
         6,
         (3, 3, 4, 4, 3, 3, 3, 3, 4, 16, 4, 16, 4, 16, 2, 4, 8, 2, 2, 1, 4),
-        (one, mix, vec, fc, proj),
+        (*pieces, fc, proj, *state),
         scratch=[
             pltpu.VMEM((3, 128, 768), BF),
             pltpu.VMEM((4, 4, 48, 384), BF),
@@ -602,8 +677,24 @@
             pltpu.VMEM((4, 48, 768), BF),
             pltpu.VMEM((2, 24, 768), F32),
             pltpu.VMEM((8, 8, wide), F32),
+            pltpu.VMEM((4, 128, 768), BF),
+            pltpu.VMEM((4, 4, 48, 384), BF),
+            pltpu.VMEM((4, 4, 48, 384), BF),
+            pltpu.VMEM((4, 4, 48, 128), BF),
+            pltpu.VMEM((2, 8, wide), F32),
+            pltpu.VMEM((24, 768), F32),
+            pltpu.VMEM((768, 512), BF),
+            pltpu.VMEM((512, 768), BF),
+            pltpu.VMEM((768, 512), BF),
+            pltpu.VMEM((512, 640), BF),
+            pltpu.VMEM((512, 768), BF),
+            pltpu.VMEM((512, 768), BF),
+            pltpu.VMEM((128, 768), F32),
+            pltpu.VMEM((6, 2304), F32),
+            pltpu.VMEM((6, 768), F32),
+            pltpu.VMEM((6, 3072), F32),
         ],
-        spaces=([VMEM] * 5, [VMEM] * 3),
+        spaces=([VMEM] * 29, [VMEM] * 16),
         name="last_sums",
     )
 
@@ -1221,12 +1312,15 @@
     vec_v,
 ):
     y, z, k, x = coords()
+    state = (
+        w_qkv, qkv_m, qkv_v, w_out, out_m, out_v, w_fc, fc_m, fc_v, w_proj, proj_m, proj_v,
+        vectors, vec_m, vec_v,
+    )
     wq, fc_part, out_part, proj_part, x_group = first_gather(
         w_qkv, w_fc, w_out, w_proj, vectors, tokens[0]
     )
     wq = wq.reshape(768, 640)
     vec_rows = wq[:, 576:592].astype(F32).T
-    gain_one = vec_rows[0]
     bias = jnp.concatenate(
         [
             lax.dynamic_slice(vec_rows, (2, 192 * z), (1, 192)),
@@ -1262,69 +1356,26 @@
         grad_w_fc.reshape(4, 4, 48, 384),
         grad_w_proj.reshape(2, 4, 48, 768),
     )
-    grad_mixed = jnp.concatenate([grad_query, grad_kv.astype(BF)], 1)
-    branch_cols = lax.dynamic_slice(branch_core, (0, 192 * z), (512, 192))
-    heads_core = lax.dynamic_index_in_dim(heads_all, k, 1, False)
-    heads_core = jnp.concatenate([heads_core[i] for i in range(4)], 1)
-    left = jnp.concatenate([act_one, heads_core], 0)
-    gap = jnp.zeros((512, 96), BF)
-    room = jnp.zeros((512, 288), BF)
-    right = jnp.concatenate(
-        [
-            jnp.concatenate([grad_mixed[:, :288], gap, grad_mixed[:, 288:], gap], 1),
-            jnp.concatenate([room, branch_cols[:, :96], room, branch_cols[:, 96:]], 1),
-        ],
-        0,
-    )
-    grad_mix = dot(left.T, right).astype(BF)
-    one_part = dot(grad_mixed, wq[:, :576].T)
-
-    def spread(piece, at, size):
-        return lax.dynamic_update_slice(jnp.zeros((size,), F32), piece, (at,))
-
-    mixed_sums = jnp.sum(grad_mixed.astype(F32), 0)
-    columns = jnp.stack(
-        [
-            jnp.sum(one_part * normed_core.astype(F32), 0),
-            jnp.sum(one_part, 0),
-            spread(mixed_sums[:192], 192 * z, 768),
-            spread(mixed_sums[384:], 192 * z, 768),
-            vec_sums[0],
-            vec_sums[1],
-            vec_sums[2],
-            vec_sums[3],
-        ]
-        + list(spread(grad_fc_bias[0], (2 * z + k) * 384, 3072).reshape(4, 768)),
-        1,
-    )
-    grad_vec = jnp.pad(columns, ((0, 0), (0, 116))).astype(BF)
-    grad_norm_one, last_rows, sum_proj = last_sums(
-        one_part.astype(BF).reshape(4, 128, 768),
-        grad_mix.reshape(4, 4, 48, 768),
-        grad_vec.reshape(4, 4, 48, 128),
+    grad_inputs, *new_state = last_sums(
+        (
+            act_one,
+            normed_core,
+            heads_all,
+            grad_query,
+            grad_kv,
+            branch_core,
+            wq,
+            vec_sums,
+            grad_fc_bias,
+            tokens[0],
+            grad_x_two,
+            vec_rows[0:1],
+        ),
         fc_sum,
         proj_sum,
-    )
-    normed_one, inverse_one = normalize(tokens[0].astype(F32))
-    grad_inputs = grad_x_two + normalize_back(normed_one, inverse_one, gain_one, grad_norm_one)
-    last_rows = last_rows[:, :6]
-    mix_rows = last_rows[:, :, :1536].reshape(2, 6, 4, 384)
-    sum_qkv = (
-        mix_rows[..., :288]
-        .transpose(1, 2, 0, 3)
-        .reshape(6, 4, 3, 192)
-        .transpose(0, 2, 1, 3)
-        .reshape(6, 2304)
-    )
-    sum_out = mix_rows[..., 288:].transpose(1, 2, 0, 3).reshape(6, 768)
-    sum_fc = last_rows[:, :, 1536:3072].reshape(2, 6, 4, 384).transpose(1, 2, 0, 3).reshape(6, 3072)
-    sum_vec = last_rows[0, :, 3072:3084] + last_rows[1, :, 3072:3084]
-    new_qkv = adam_update(w_qkv, qkv_m, qkv_v, sum_qkv, 0.1, 0.1)
-    new_out = adam_update(w_out, out_m, out_v, sum_out, 0.3, 0.1)
-    new_fc = adam_update(w_fc, fc_m, fc_v, sum_fc, 0.05, 0.1)
-    new_proj = adam_update(w_proj, proj_m, proj_v, sum_proj, 0.03, 0.1)
-    new_vec = adam_update(vectors, vec_m, vec_v, sum_vec, 0.5, 0.0)
-    return (output[None], grad_inputs[None], *new_qkv, *new_out, *new_fc, *new_proj, *new_vec)
+        state,
+    )
+    return (output[None], grad_inputs[None], *new_state)
 
 
 def solution(mesh):

time: 234 us -> 230 us (0.983)
  other arithmetic: 9.04 us -> 0.61 us
  Pallas kernels: 208 us -> 213 us
  local copies, waits for them, and re-layouts: 10.6 us -> 15.6 us
  matrix products: 4.36 us -> 0 us
    unnamed x61 -> x52, local copies, waits for them, and re-layouts: 2.76 us -> 12.6 us
    pallas_call x5, Pallas kernels: 208 us -> 213 us  [comm(): pl.pallas_call(kernel, out_shape=outs, in_specs=[ANY] * len(args) if spac...]
    dot_general x2 -> x0, matrix products: 4.36 us -> none  [dot(): return jnp.dot(a, b, preferred_element_type=F32)]
    sub x5 -> x0, other arithmetic: 4.12 us -> none  [adam_update(): return (weight - rate * (direction + decay * weight), new_one, new_two)]
    slice x4 -> x1, local copies, waits for them, and re-layouts: 3.1 us -> 0.58 us  [shards(): vec_rows[0:1]]
where the time goes in v4:
time: 230 us
  Pallas kernels  213 us (93%)
  local copies, waits for them, and re-layouts  15.6 us (7%)
    pallas_call x5, Pallas kernels, comm(): pl.pallas_call(kernel, out_shape=outs, in_specs=[ANY] * len(args) if spac...  213 us
    unnamed x52, local copies, waits for them, and re-layouts  12.6 us

profile of v4, /device:TPU:29, one launch (start us, length us, event | category | flops | bytes accessed | tf_op | source)
XLA Modules:
  0.0 229.8 jit_solution(7318573155346196481)
XLA Ops:
  0.9 36.9 %first_gather.1 = (bf16[16,48,640]{2,1,0:T(8,128)(2,1)}, bf16[16,48,384]{2,1,0:T(8,128)(2,1)}, bf16[16,48,384]{2,1,0:T(8,128)(2,1)}, bf16[2,192,768]{2,1,0:T(8,128)(2,1)}, bf16[2,4,128,768]{3,2,1,0:T(8,128)(2,1)}) custom-call(f32[6,2304]{1,0:T(8,128)} %refs_14_.1, f32[6,3072]{1,0:T(8,128)} %refs_20_.1, f32[6,768]{1,0:T(8,128)} %refs_17_.1, ...), custom_call_target="tpu_custom_call" | custom-call | tf_op jit(solution)/shard_map/first_gather/pallas_call | solution.py:48
  37.8 1.0 slice.20
  40.2 0.6 slice.21.g_ref
  40.8 0.6 slice_bitcast_fusion
  42.0 47.5 %attend.1 = (bf16[4,2,512,192]{3,2,1,0:T(8,128)(2,1)}, f32[192,512]{1,0:T(8,128)}, f32[8,512]{1,0:T(8,128)}, bf16[4,2,512,384]{3,2,1,0:T(8,128)(2,1)}, bf16[2,4,...) custom-call(bf16[2,4,128,768]{3,2,1,0:T(8,128)(2,1)} %get-tuple-elem, ...), custom_call_target="tpu_custom_call" | custom-call | tf_op jit(solution)/shard_map/attend/pallas_call | solution.py:48
  89.6 40.9 %feed_forward.1 = (f32[128,768]{1,0:T(8,128)}, f32[128,768]{1,0:T(8,128)}, bf16[4,128,768]{2,1,0:T(8,128)(2,1)}, bf16[768,384]{1,0:T(8,128)(2,1)}, bf16[384,768]...) custom-call(bf16[4,2,512,192]{3,2,1,0:T(8,128)(2,1)} %get-tuple-element.65.h_ref.refs_2_, ...), custom_call_target="tpu_custom_call" | custom-call | tf_op jit(solution)/shard_map/feed_forward/pallas_call | solution.py:48
  130.5 31.6 %attend_back.1 = (bf16[512,192]{1,0:T(8,128)(2,1)}, f32[512,384]{1,0:T(8,128)}, bf16[4,48,384]{2,1,0:T(8,128)(2,1)}, bf16[2,48,768]{2,1,0:T(8,128)(2,1)}) custom-call(bf16[512,192]{1,0:T(8,128)(2,1)} %get-tuple-element.73.q_ref, bf16[512,768]{1,0:T(8,128)(2,1)} %bitcast.26, bf16[2,768,384]{2,1,0:T(8,128)(2,1)} %bitcast.25, ...), custom_call_target="tpu_custom_call" | custom-call | tf_op jit(solution)/shard_map/attend_back/pallas_call | solution.py:48
  162.2 55.5 %last_sums.1 = (f32[128,768]{1,0:T(8,128)}, f32[6,2304]{1,0:T(8,128)}, f32[6,2304]{1,0:T(8,128)}, f32[6,2304]{1,0:T(8,128)}, f32[6,768]{1,0:T(8,128)}, /*index=5...) custom-call(bf16[512,768]{1,0:T(8,128)(2,1)} %get-tuple-element.71.r, ...), custom_call_target="tpu_custom_call" | custom-call | tf_op jit(solution)/shard_map/last_sums/pallas_call | solution.py:48
  217.9 0.7 copy.57
  218.6 1.8 copy.58
  220.4 0.6 copy.59
  221.0 0.6 copy.60
  221.7 0.6 copy.61
  222.3 0.6 copy.62
  222.9 0.6 copy.63
  223.5 0.6 copy.64
  224.1 0.6 copy.65
  224.8 0.6 copy.66
  225.4 0.6 copy.67
  226.1 0.6 copy.68
  226.7 0.6 copy.69
  227.3 0.6 copy.70
  228.0 0.6 copy.71
  228.6 0.6 copy.72
  (44 shorter events, 2.8 us)
Async XLA Ops:
  162.2 55.7 %copy-start = (f32[128,768]{1,0:T(8,128)S(1)}, f32[128,768]{1,0:T(8,128)}, u32[]{:S(2)}) copy-start(f32[128,768]{1,0:T(8,128)} %get-tuple-element.70) | copy-start | bytes 1179652
  217.7 2.7 %copy-start.9 = (f32[6,2304]{1,0:T(8,128)S(1)}, f32[6,2304]{1,0:T(8,128)}, u32[]{:S(2)}) copy-start(f32[6,2304]{1,0:T(8,128)} %get-tuple-element.128) | copy-start | bytes 165892
  217.7 3.3 %copy-start.8 = (f32[6,2304]{1,0:T(8,128)S(1)}, f32[6,2304]{1,0:T(8,128)}, u32[]{:S(2)}) copy-start(f32[6,2304]{1,0:T(8,128)} %get-tuple-element.129) | copy-start | bytes 165892
  217.7 3.9 %copy-start.7 = (f32[6,2304]{1,0:T(8,128)S(1)}, f32[6,2304]{1,0:T(8,128)}, u32[]{:S(2)}) copy-start(f32[6,2304]{1,0:T(8,128)} %get-tuple-element.130) | copy-start | bytes 165892
  217.8 4.6 %copy-start.12 = (f32[6,768]{1,0:T(8,128)S(1)}, f32[6,768]{1,0:T(8,128)}, u32[]{:S(2)}) copy-start(f32[6,768]{1,0:T(8,128)} %get-tuple-element.131) | copy-start | bytes 55300
  217.8 5.2 %copy-start.11 = (f32[6,768]{1,0:T(8,128)S(1)}, f32[6,768]{1,0:T(8,128)}, u32[]{:S(2)}) copy-start(f32[6,768]{1,0:T(8,128)} %get-tuple-element.132) | copy-start | bytes 55300
  217.8 5.8 %copy-start.10 = (f32[6,768]{1,0:T(8,128)S(1)}, f32[6,768]{1,0:T(8,128)}, u32[]{:S(2)}) copy-start(f32[6,768]{1,0:T(8,128)} %get-tuple-element.133) | copy-start | bytes 55300
  217.8 6.4 %copy-start.3 = (f32[6,3072]{1,0:T(8,128)S(1)}, f32[6,3072]{1,0:T(8,128)}, u32[]{:S(2)}) copy-start(f32[6,3072]{1,0:T(8,128)} %get-tuple-element.134) | copy-start | bytes 221188
  217.8 7.0 %copy-start.2 = (f32[6,3072]{1,0:T(8,128)S(1)}, f32[6,3072]{1,0:T(8,128)}, u32[]{:S(2)}) copy-start(f32[6,3072]{1,0:T(8,128)} %get-tuple-element.135) | copy-start | bytes 221188
  217.8 7.6 %copy-start.1 = (f32[6,3072]{1,0:T(8,128)S(1)}, f32[6,3072]{1,0:T(8,128)}, u32[]{:S(2)}) copy-start(f32[6,3072]{1,0:T(8,128)} %get-tuple-element.136) | copy-start | bytes 221188
  217.8 8.3 %copy-start.6 = (f32[24,768]{1,0:T(8,128)S(1)}, f32[24,768]{1,0:T(8,128)}, u32[]{:S(2)}) copy-start(f32[24,768]{1,0:T(8,128)} %get-tuple-element.137) | copy-start | bytes 221188
  217.8 8.9 %copy-start.5 = (f32[24,768]{1,0:T(8,128)S(1)}, f32[24,768]{1,0:T(8,128)}, u32[]{:S(2)}) copy-start(f32[24,768]{1,0:T(8,128)} %get-tuple-element.138) | copy-start | bytes 221188
  217.8 9.5 %copy-start.4 = (f32[24,768]{1,0:T(8,128)S(1)}, f32[24,768]{1,0:T(8,128)}, u32[]{:S(2)}) copy-start(f32[24,768]{1,0:T(8,128)} %get-tuple-element.139) | copy-start | bytes 221188
  217.9 10.1 %copy-start.15 = (f32[6,12]{1,0:T(8,128)S(1)}, f32[6,12]{1,0:T(8,128)}, u32[]{:S(2)}) copy-start(f32[6,12]{1,0:T(8,128)} %get-tuple-element.140) | copy-start | bytes 868
  217.9 10.7 %copy-start.14 = (f32[6,12]{1,0:T(8,128)S(1)}, f32[6,12]{1,0:T(8,128)}, u32[]{:S(2)}) copy-start(f32[6,12]{1,0:T(8,128)} %get-tuple-element.141) | copy-start | bytes 868
  217.9 11.3 %copy-start.13 = (f32[6,12]{1,0:T(8,128)S(1)}, f32[6,12]{1,0:T(8,128)}, u32[]{:S(2)}) copy-start(f32[6,12]{1,0:T(8,128)} %get-tuple-element.142) | copy-start | bytes 868

commit v5 on v4

--- a/solution.py
+++ b/solution.py
@@ -58,294 +58,24 @@
     )(*args)
 
 
-def first_gather(w_qkv, w_fc, w_out, w_proj, vectors, rows):
-    width = 4736
-
-    def kernel(
-        wq_ref, wf_ref, wo_ref, wp_ref, wv_ref, r_ref,
-        q_out, f_out, o_out, p_out, ro_ref,
-        wide, packed, got, fc48, qkv48, out48, proj_wide, q_send, f_send, o_send, p_send,
-        ms, mr, fs, fr, s1, r1, s2, r2, ps, pr, xs_s, xs_r, xf_s, xf_r, rs, rr, cs, cr, loc,
-    ):
-        y, z, k, x = coords()
-        me = y * 4 + z
-        sib = device(y, z, 1 - k, x)
-        steps = (1, 2, 3)
-        greet(
-            [sib]
-            + [device(y, z, k, ring(x, d)) for d in steps]
-            + [
-                device(ring(y, a), ring(z, b), k, x)
-                for a in range(4)
-                for b in range(4)
-                if (a, b) != (0, 0)
-            ]
-        )
-        own_r = pltpu.make_async_copy(r_ref, ro_ref.at[k, z], loc.at[0])
-        own_r.start()
-        row_copies = []
-        for d in steps:
-            c = remote(
-                r_ref, ro_ref.at[k, z], rs.at[d], rr.at[d], device(y, ring(z, d), k, x)
-            )
-            row_copies.append(c)
-        wide[...] = jnp.zeros_like(wide)
-        wide[0:6, 0:3072] = wf_ref[...]
-        wide[6:12, 0:2304] = wq_ref[...]
-        wide[6:12, 2304:3072] = wo_ref[...]
-        wide[0:12, 3072:3840] = wp_ref[0:12]
-        wide[0:12, 3840:4608] = wp_ref[12:24]
-        wide[0:6, 4608:4620] = wv_ref[...]
-        t = k * 4 + x
-        packed[...] = wide[...].astype(BF)
-        got[t] = packed[...]
-        message = []
-        for d in steps:
-            c = remote(packed, got.at[t], ms.at[d], mr.at[d], device(y, z, k, ring(x, d)))
-            c.start()
-            message.append(c)
-        c = remote(packed, got.at[t], fs.at[0], fr.at[0], sib)
-        c.start()
-        forward = [c]
-        for c in row_copies:
-            c.start()
-        c = remote(r_ref, ro_ref.at[k, z], cs.at[0], cr.at[0], sib)
-        c.start()
-        row_forward = [c]
-        for d in steps:
-            message[d - 1].wait_recv()
-            src = k * 4 + ring(x, 4 - d)
-            f = remote(got.at[src], got.at[src], fs.at[d], fr.at[d], sib)
-            f.start()
-            forward.append(f)
-        for f in forward:
-            f.wait_recv()
-        for i in range(8):
-            piece = got[i].astype(F32)
-            at = slice(6 * i, 6 * i + 6)
-            fc48[at] = piece[0:6, 0:3072]
-            qkv48[at] = piece[6:12, 0:2304]
-            out48[at, 0:768] = piece[6:12, 2304:3072]
-            out48[at, 768:896] = piece[0:6, 4608:4736]
-            proj_wide[24 * i : 24 * i + 12] = piece[0:12, 3072:3840]
-            proj_wide[24 * i + 12 : 24 * i + 24] = piece[0:12, 3840:4608]
-        for j in range(4):
-            q_send[j, :, 0:192] = qkv48[:, 192 * j : 192 * j + 192].astype(BF)
-            q_send[j, :, 192:384] = qkv48[:, 768 + 192 * j : 960 + 192 * j].astype(BF)
-            q_send[j, :, 384:576] = qkv48[:, 1536 + 192 * j : 1728 + 192 * j].astype(BF)
-            q_send[j, :, 576:640] = out48[:, 768:832].astype(BF)
-        for j in range(8):
-            f_send[j] = fc48[:, 384 * j : 384 * j + 384].astype(BF)
-        o_send[0] = out48[:, 0:384].astype(BF)
-        o_send[1] = out48[:, 384:768].astype(BF)
-        p_send[...] = proj_wide[...].astype(BF)
-
-        group = pl.ds(pl.multiple_of(16 * jnp.minimum(x, 2), 16), 16)
-
-        def to_of(m):
-            return ring(y, m // 4), ring(z, m % 4)
-
-        def q_copy(m):
-            ty, tz = to_of(m)
-            return remote(
-                q_send.at[tz, group], q_out.at[me, group], s1.at[m], r1.at[m],
-                device(ty, tz, k, x),
-            )
-
-        def f_copy(m):
-            ty, tz = to_of(m)
-            return remote(
-                f_send.at[tz * 2 + k], f_out.at[me], s2.at[m], r2.at[m], device(ty, tz, k, x)
-            )
-
-        def o_copy(m):
-            ty, tz = to_of(m)
-            return remote(o_send.at[k], o_out.at[me], s2.at[m], r2.at[m], device(ty, tz, k, x))
-
-        def p_copy(a):
-            return remote(
-                p_send, p_out.at[z % 2], ps.at[a], pr.at[z % 2], device(ring(y, a), y, k, x)
-            )
-
-        def each(copy, what):
-            def step(m, carry):
-                what(copy(m))
-                return carry
-
-            lax.fori_loop(1, 16, step, 0)
-
-        start = lambda c: c.start()
-        finish = lambda c: c.wait()
-
-        @pl.when(x < 3)
-        def _():
-            each(q_copy, start)
-            c = pltpu.make_async_copy(q_send.at[z, group], q_out.at[me, group], loc.at[1])
-            c.start()
-            c.wait()
-
-        @pl.when(x == 1)
-        def _():
-            each(f_copy, start)
-            c = pltpu.make_async_copy(f_send.at[z * 2 + k], f_out.at[me], loc.at[2])
-            c.start()
-            c.wait()
-
-        @pl.when(x == 2)
-        def _():
-            each(o_copy, start)
-            c = pltpu.make_async_copy(o_send.at[k], o_out.at[me], loc.at[2])
-            c.start()
-            c.wait()
-
-        @pl.when((x == 3) & (k == z // 2))
-        def _():
-            for a in range(1, 4):
-                p_copy(a).start()
-
-            @pl.when(z != y)
-            def _():
-                p_copy(0).start()
-
-            @pl.when(z == y)
-            def _():
-                c = pltpu.make_async_copy(p_send, p_out.at[z % 2], loc.at[2])
-                c.start()
-                c.wait()
-
-        half = pl.ds(8 * k, 8)
-        other_half = pl.ds(8 * (1 - k), 8)
-
-        def rows_of(plane):
-            return pl.ds(pl.multiple_of(16 * plane, 16), 16)
-
-        @pl.when(x < 3)
-        def _():
-            each(q_copy, finish)
-            for d in steps:
-                remote(
-                    q_out.at[half, group], q_out.at[half, group], xs_s.at[d], xs_r.at[x],
-                    device(y, z, k, ring(x, d)),
-                ).start()
-
-        def pass_on(a):
-            return remote(
-                q_out.at[half, rows_of(a)], q_out.at[half, rows_of(a)], xf_s.at[a], xf_r.at[a], sib
-            )
-
-        for a in range(3):
-
-            @pl.when(x != a)
-            def _():
-                remote(
-                    q_out.at[half, rows_of(a)], q_out.at[half, rows_of(a)], xs_s.at[0],
-                    xs_r.at[a], sib,
-                ).wait_recv()
-                pass_on(a).start()
-
-        for d in steps:
-            row_copies[d - 1].wait_recv()
-            src = ring(z, 4 - d)
-            f = remote(ro_ref.at[k, src], ro_ref.at[k, src], cs.at[d], cr.at[d], sib)
-            f.start()
-            row_forward.append(f)
-
-        @pl.when(x == 1)
-        def _():
-            each(f_copy, finish)
-
-        @pl.when(x == 2)
-        def _():
-            each(o_copy, finish)
-
-        @pl.when((x == 3) & (k == z // 2))
-        def _():
-            for a in range(1, 4):
-                p_copy(a).wait_send()
-
-            @pl.when(z != y)
-            def _():
-                p_copy(0).wait_send()
-
-        for j in range(2):
-            @pl.when((x == 3) & jnp.logical_not((y == z) & (z == 2 * k + j)))
-            def _():
-                remote(p_send, p_out.at[j], ps.at[0], pr.at[j], sib).wait_recv()
-
-        @pl.when(x < 3)
-        def _():
-            for d in steps:
-                remote(
-                    q_out.at[half, group], q_out.at[half, group], xs_s.at[d], xs_r.at[x],
-                    device(y, z, k, ring(x, d)),
-                ).wait_send()
-
-        for a in range(3):
-
-            @pl.when(x != a)
-            def _():
-                pass_on(a).wait_send()
-                remote(
-                    q_out.at[other_half, rows_of(a)], q_out.at[other_half, rows_of(a)],
-                    xf_s.at[a], xf_r.at[a], sib,
-                ).wait_recv()
-
-        for c in message + row_copies + forward:
-            c.wait_send()
-        for c in row_forward:
-            c.wait()
-        own_r.wait()
-
-    return comm(
-        kernel,
-        [
-            jax.ShapeDtypeStruct((16, 48, 640), BF),
-            jax.ShapeDtypeStruct((16, 48, 384), BF),
-            jax.ShapeDtypeStruct((16, 48, 384), BF),
-            jax.ShapeDtypeStruct((2, 192, 768), BF),
-            jax.ShapeDtypeStruct((2, 4) + rows.shape, BF),
-        ],
-        0,
-        (4, 4, 4, 4, 16, 16, 16, 16, 4, 2, 4, 4, 4, 4, 4, 4, 4, 4, 3),
-        (w_qkv, w_fc, w_out, w_proj, vectors, rows),
-        scratch=[
-            pltpu.VMEM((16, width), F32),
-            pltpu.VMEM((16, width), BF),
-            pltpu.VMEM((8, 16, width), BF),
-            pltpu.VMEM((48, 3072), F32),
-            pltpu.VMEM((48, 2304), F32),
-            pltpu.VMEM((48, 896), F32),
-            pltpu.VMEM((192, 768), F32),
-            pltpu.VMEM((4, 48, 640), BF),
-            pltpu.VMEM((8, 48, 384), BF),
-            pltpu.VMEM((2, 48, 384), BF),
-            pltpu.VMEM((192, 768), BF),
-        ],
-        spaces=([VMEM] * 5 + [ANY], [ANY] * 5),
-        name="first_gather",
-    )
-
-
-def last_sums(pieces, fc, proj, state):
+def last_sums(pieces, fc, proj):
     wide = 3200
 
     def kernel(*refs):
         (
             act_ref, n_ref, h_ref, gq_ref, gkv_ref, br_ref, wq_ref, vs_ref, fb_ref,
-            tok_ref, gx_ref, gain_ref, fc_ref, proj_ref,
-        ) = refs[:14]
-        state_ref = refs[14:29]
-        gin_ref = refs[29]
-        new_ref = refs[30:45]
+            fc_ref, proj_ref,
+        ) = refs[:11]
+        one_out, rows_out, proj_out = refs[11:14]
         (
             one_far, mix_got, mix_sum, mix_far, vec_far, mix_mine, vec_mine,
             mix_all, fc_all, vec_all, proj_all, proj_sum, out_send,
-            one_ref, mix_other, mix_ref, vec_ref, rows_out, proj_out,
-            act_t, heads, heads_t, d_ref, right_one, right_two, vec_rows, g_qkv, g_out, g_fc,
-        ) = refs[45:74]
+            one_ref, mix_other, mix_ref, vec_ref,
+            act_t, heads, heads_t, d_ref, right_one, right_two, vec_rows,
+        ) = refs[14:38]
         (
         zs, zr, cs, cr, s1, r1, s2, r2, s3, r3, s4, r4, s5, r5, s6, r6, s7, r7, s8, r8, loc,
-        ) = refs[74:]
+        ) = refs[38:]
         y, z, k, x = coords()
         me = y * 4 + z
         sib = device(y, z, 1 - k, x)
@@ -500,14 +230,12 @@
         all_start(vec_mine, vec_all, s5, r5)
         for c in ones:
             c.wait_recv()
-        grad = (
+        one_out[...] = (
             one_ref[z].astype(F32)
             + one_far[0].astype(F32)
             + one_far[1].astype(F32)
             + one_far[2].astype(F32)
         )
-        normed, inverse = normalize(tok_ref[...].astype(F32))
-        gin_ref[...] = gx_ref[...] + normalize_back(normed, inverse, gain_ref[...], grad)
 
         def proj_last(i):
             return remote(
@@ -600,34 +328,6 @@
         def _():
             remote(proj_sum.at[0], proj_out, s8.at[0], r8.at[0], sib).wait_recv()
 
-        for b in range(4):
-            one_half = rows_out[0, 0:6, 384 * b : 384 * b + 384]
-            two_half = rows_out[1, 0:6, 384 * b : 384 * b + 384]
-            q = 192 * b
-            g_qkv[:, q : q + 192] = one_half[:, 0:192]
-            g_qkv[:, 768 + q : 864 + q] = one_half[:, 192:288]
-            g_qkv[:, 864 + q : 960 + q] = two_half[:, 0:96]
-            g_qkv[:, 1536 + q : 1728 + q] = two_half[:, 96:288]
-            g_out[:, q : q + 96] = one_half[:, 288:384]
-            g_out[:, q + 96 : q + 192] = two_half[:, 288:384]
-            for j in range(2):
-                at = 384 * (2 * b + j)
-                g_fc[:, at : at + 384] = rows_out[j, 0:6, 1536 + 384 * b : 1920 + 384 * b]
-        g_vec = rows_out[0, 0:6, 3072:3084] + rows_out[1, 0:6, 3072:3084]
-        for i, (gradient, rate, decay) in enumerate(
-            (
-                (g_qkv[...], 0.1, 0.1),
-                (g_out[...], 0.3, 0.1),
-                (g_fc[...], 0.05, 0.1),
-                (proj_out[...], 0.03, 0.1),
-                (g_vec, 0.5, 0.0),
-            )
-        ):
-            w, m, v = state_ref[3 * i : 3 * i + 3]
-            results = adam_update(w[...], m[...], v[...], gradient, rate, decay)
-            for j in range(3):
-                new_ref[3 * i + j][...] = results[j]
-
         @pl.when(z == x)
         def _():
             for i in range(8):
@@ -658,11 +358,12 @@
         kernel,
         [
             jax.ShapeDtypeStruct((128, 768), F32),
-        ]
-        + [jax.ShapeDtypeStruct(one.shape, F32) for one in state],
+            jax.ShapeDtypeStruct((2, 8, wide), F32),
+            jax.ShapeDtypeStruct((24, 768), F32),
+        ],
         6,
         (3, 3, 4, 4, 3, 3, 3, 3, 4, 16, 4, 16, 4, 16, 2, 4, 8, 2, 2, 1, 4),
-        (*pieces, fc, proj, *state),
+        (*pieces, fc, proj),
         scratch=[
             pltpu.VMEM((3, 128, 768), BF),
             pltpu.VMEM((4, 4, 48, 384), BF),
@@ -681,8 +382,6 @@
             pltpu.VMEM((4, 4, 48, 384), BF),
             pltpu.VMEM((4, 4, 48, 384), BF),
             pltpu.VMEM((4, 4, 48, 128), BF),
-            pltpu.VMEM((2, 8, wide), F32),
-            pltpu.VMEM((24, 768), F32),
             pltpu.VMEM((768, 512), BF),
             pltpu.VMEM((512, 768), BF),
             pltpu.VMEM((768, 512), BF),
@@ -690,13 +389,64 @@
             pltpu.VMEM((512, 768), BF),
             pltpu.VMEM((512, 768), BF),
             pltpu.VMEM((128, 768), F32),
+        ],
+        spaces=([VMEM] * 11, [VMEM] * 3),
+        name="last_sums",
+    )
+
+
+def finish(grad_one, grad_x_two, tokens, vec_rows, rows, proj_rows, result, state):
+    def kernel(*refs):
+        one_ref, gx_ref, t_ref, v_ref, rows_ref, p_ref, res_ref = refs[:7]
+        state_ref = refs[7:22]
+        out_ref, gin_ref = refs[22:24]
+        new_ref = refs[24:39]
+        g_qkv, g_out, g_fc = refs[39:]
+        out_ref[...] = res_ref[...]
+        normed, inverse = normalize(t_ref[...].astype(F32))
+        gin_ref[...] = gx_ref[...] + normalize_back(normed, inverse, v_ref[0:1], one_ref[...])
+        for b in range(4):
+            one_half = rows_ref[0, 0:6, 384 * b : 384 * b + 384]
+            two_half = rows_ref[1, 0:6, 384 * b : 384 * b + 384]
+            q = 192 * b
+            g_qkv[:, q : q + 192] = one_half[:, 0:192]
+            g_qkv[:, 768 + q : 864 + q] = one_half[:, 192:288]
+            g_qkv[:, 864 + q : 960 + q] = two_half[:, 0:96]
+            g_qkv[:, 1536 + q : 1728 + q] = two_half[:, 96:288]
+            g_out[:, q : q + 96] = one_half[:, 288:384]
+            g_out[:, q + 96 : q + 192] = two_half[:, 288:384]
+            for j in range(2):
+                at = 384 * (2 * b + j)
+                g_fc[:, at : at + 384] = rows_ref[j, 0:6, 1536 + 384 * b : 1920 + 384 * b]
+        g_vec = rows_ref[0, 0:6, 3072:3084] + rows_ref[1, 0:6, 3072:3084]
+        for i, (gradient, rate, decay) in enumerate(
+            (
+                (g_qkv[...], 0.1, 0.1),
+                (g_out[...], 0.3, 0.1),
+                (g_fc[...], 0.05, 0.1),
+                (p_ref[...], 0.03, 0.1),
+                (g_vec, 0.5, 0.0),
+            )
+        ):
+            w, m, v = state_ref[3 * i : 3 * i + 3]
+            results = adam_update(w[...], m[...], v[...], gradient, rate, decay)
+            for j in range(3):
+                new_ref[3 * i + j][...] = results[j]
+
+    return pl.pallas_call(
+        kernel,
+        out_shape=[jax.ShapeDtypeStruct((128, 768), F32)] * 2
+        + [jax.ShapeDtypeStruct(one.shape, F32) for one in state],
+        in_specs=[VMEM] * 22,
+        out_specs=[VMEM] * 17,
+        scratch_shapes=[
             pltpu.VMEM((6, 2304), F32),
             pltpu.VMEM((6, 768), F32),
             pltpu.VMEM((6, 3072), F32),
         ],
-        spaces=([VMEM] * 29, [VMEM] * 16),
-        name="last_sums",
-    )
+        compiler_params=pltpu.CompilerParams(vmem_limit_bytes=LIMIT),
+        name="finish",
+    )(grad_one, grad_x_two, tokens, vec_rows, rows, proj_rows, result, *state)
 
 
 def head_rows(matrix, head):
@@ -719,23 +469,258 @@
     return jnp.dot(a, b, preferred_element_type=F32)
 
 
-def attend(tokens, wq, bias, rows768, rows, fc, out, proj):
+def forward(w_qkv, w_fc, w_out, w_proj, vectors, tokens, cotangent):
+    wide_q, wide_r = 1280, 3456
+
     def kernel(
-        x_ref, wq_ref, b_ref, g_ref, r_ref, f_ref, o_ref, p_ref,
+        wq_ref, wf_ref, wo_ref, wp_ref, wv_ref, t_ref, r_ref,
         ho_ref, ot_ref, lse_ref, vo_ref, ro_ref, fo_ref, oo_ref, po_ref, q_ref, a_ref, n_ref,
-        qt, m_ref, l_ref, h_buf, v_ref,
+        q_out, x_ref, vec_ref,
+        wide_one, wide_two, packed_q, packed_r, got_q, got_r,
+        fc48, qkv48, out48, proj_wide, q_send, f_send, o_send, p_send, f_mid, o_mid, p_mid,
+        bias, qt, m_ref, l_ref, h_buf, v_ref,
+        mq_s, mq_r, fq_s, fq_r, mr_s, mr_r, fr_s, fr_r, s1, r1, s2, r2, ps, pr,
+        xs_s, xs_r, xf_s, xf_r, ts, tr, us, ur,
         vs, vr, rs, rr, cs, cr, ds, dr, ws, wr, os, orr, hs, hr, gs, gr, loc,
     ):
         y, z, k, x = coords()
+        me = y * 4 + z
+        t = k * 4 + x
         sib = device(y, z, 1 - k, x)
         steps = (1, 2, 3)
         greet(
             [sib]
-            + [device(ring(y, d), z, k, x) for d in steps]
-            + [device(y, ring(z, d), k, x) for d in steps]
             + [device(y, z, k, ring(x, d)) for d in steps]
+            + [
+                device(ring(y, a), ring(z, b), k, x)
+                for a in range(4)
+                for b in range(4)
+                if (a, b) != (0, 0)
+            ]
         )
 
+        def first(packed, got, send, recv):
+            copies = [
+                remote(packed, got.at[t], send.at[d], recv.at[d], device(y, z, k, ring(x, d)))
+                for d in steps
+            ]
+            for c in copies:
+                c.start()
+            return copies
+
+        def crossing(packed, got, copies, send, recv):
+            out = [remote(packed, got.at[t], send.at[0], recv.at[0], sib)]
+            out[0].start()
+            for d in steps:
+                copies[d - 1].wait_recv()
+                src = k * 4 + ring(x, 4 - d)
+                c = remote(got.at[src], got.at[src], send.at[d], recv.at[d], sib)
+                c.start()
+                out.append(c)
+            return out
+
+        wide_one[...] = jnp.zeros_like(wide_one)
+        wide_one[0:6, 0:1152] = wq_ref[:, 0:1152]
+        wide_one[6:12, 0:1152] = wq_ref[:, 1152:2304]
+        wide_one[0:6, 1152:1164] = wv_ref[...]
+        packed_q[...] = wide_one[...].astype(BF)
+        got_q[t] = packed_q[...]
+        message_q = first(packed_q, got_q, mq_s, mq_r)
+        token_copies = []
+        for d in steps:
+            c = remote(
+                t_ref, x_ref.at[k, z], ts.at[d], tr.at[d], device(y, ring(z, d), k, x)
+            )
+            c.start()
+            token_copies.append(c)
+        token_cross = [remote(t_ref, x_ref.at[k, z], us.at[0], ur.at[0], sib)]
+        token_cross[0].start()
+        x_ref[k, z] = t_ref[...]
+        wide_two[...] = jnp.zeros_like(wide_two)
+        wide_two[0:6, 0:1920] = wf_ref[:, 0:1920]
+        wide_two[6:12, 0:1152] = wf_ref[:, 1920:3072]
+        wide_two[6:12, 1152:1920] = wo_ref[...]
+        wide_two[0:12, 1920:2688] = wp_ref[0:12]
+        wide_two[0:12, 2688:3456] = wp_ref[12:24]
+        packed_r[...] = wide_two[...].astype(BF)
+        got_r[t] = packed_r[...]
+        cross_q = crossing(packed_q, got_q, message_q, fq_s, fq_r)
+        message_r = first(packed_r, got_r, mr_s, mr_r)
+        for c in cross_q:
+            c.wait_recv()
+        for i in range(8):
+            piece = got_q[i].astype(F32)
+            at = slice(6 * i, 6 * i + 6)
+            qkv48[at, 0:1152] = piece[0:6, 0:1152]
+            qkv48[at, 1152:2304] = piece[6:12, 0:1152]
+            qkv48[at, 2304:2432] = piece[0:6, 1152:1280]
+        for j in range(4):
+            q_send[j, :, 0:192] = qkv48[:, 192 * j : 192 * j + 192].astype(BF)
+            q_send[j, :, 192:384] = qkv48[:, 768 + 192 * j : 960 + 192 * j].astype(BF)
+            q_send[j, :, 384:576] = qkv48[:, 1536 + 192 * j : 1728 + 192 * j].astype(BF)
+            q_send[j, :, 576:640] = qkv48[:, 2304:2368].astype(BF)
+
+        group = pl.ds(pl.multiple_of(16 * jnp.minimum(x, 2), 16), 16)
+
+        def to_of(m):
+            return ring(y, m // 4), ring(z, m % 4)
+
+        def q_copy(m):
+            ty, tz = to_of(m)
+            return remote(
+                q_send.at[tz, group], q_out.at[me, group], s1.at[m], r1.at[m],
+                device(ty, tz, k, x),
+            )
+
+        def f_copy(m):
+            ty, tz = to_of(m)
+            return remote(
+                f_send.at[tz * 2 + k], f_mid.at[me], s2.at[m], r2.at[m], device(ty, tz, k, x)
+            )
+
+        def o_copy(m):
+            ty, tz = to_of(m)
+            return remote(o_send.at[k], o_mid.at[me], s2.at[m], r2.at[m], device(ty, tz, k, x))
+
+        def p_copy(a):
+            return remote(
+                p_send, p_mid.at[z % 2], ps.at[a], pr.at[z % 2], device(ring(y, a), y, k, x)
+            )
+
+        def each(copy, what):
+            def step(m, carry):
+                what(copy(m))
+                return carry
+
+            lax.fori_loop(1, 16, step, 0)
+
+        start = lambda c: c.start()
+        finish = lambda c: c.wait()
+
+        @pl.when(x < 3)
+        def _():
+            each(q_copy, start)
+            q_out[me, group] = q_send[z, group]
+
+        cross_r = crossing(packed_r, got_r, message_r, fr_s, fr_r)
+        for c in cross_r:
+            c.wait_recv()
+        for i in range(8):
+            piece = got_r[i].astype(F32)
+            at = slice(6 * i, 6 * i + 6)
+            fc48[at, 0:1920] = piece[0:6, 0:1920]
+            fc48[at, 1920:3072] = piece[6:12, 0:1152]
+            out48[at] = piece[6:12, 1152:1920]
+            proj_wide[24 * i : 24 * i + 12] = piece[0:12, 1920:2688]
+            proj_wide[24 * i + 12 : 24 * i + 24] = piece[0:12, 2688:3456]
+        for j in range(8):
+            f_send[j] = fc48[:, 384 * j : 384 * j + 384].astype(BF)
+        o_send[0] = out48[:, 0:384].astype(BF)
+        o_send[1] = out48[:, 384:768].astype(BF)
+        p_send[...] = proj_wide[...].astype(BF)
+
+        half = pl.ds(8 * k, 8)
+        other_half = pl.ds(8 * (1 - k), 8)
+
+        def rows_of(plane):
+            return pl.ds(pl.multiple_of(16 * plane, 16), 16)
+
+        def x_copy(d):
+            return remote(
+                q_out.at[half, group], q_out.at[half, group], xs_s.at[d], xs_r.at[x],
+                device(y, z, k, ring(x, d)),
+            )
+
+        @pl.when(x < 3)
+        def _():
+            each(q_copy, finish)
+            for d in steps:
+                x_copy(d).start()
+
+        @pl.when(x == 1)
+        def _():
+            each(f_copy, start)
+            f_mid[me] = f_send[z * 2 + k]
+
+        @pl.when(x == 2)
+        def _():
+            each(o_copy, start)
+            o_mid[me] = o_send[k]
+
+        @pl.when((x == 3) & (k == z // 2))
+        def _():
+            for a in range(1, 4):
+                p_copy(a).start()
+
+            @pl.when(z != y)
+            def _():
+                p_copy(0).start()
+
+            @pl.when(z == y)
+            def _():
+                p_mid[z % 2] = p_send[...]
+
+        def pass_q(a):
+            return remote(
+                q_out.at[half, rows_of(a)], q_out.at[half, rows_of(a)], xf_s.at[a], xf_r.at[a], sib
+            )
+
+        for a in range(3):
+
+            @pl.when(x != a)
+            def _():
+                remote(
+                    q_out.at[half, rows_of(a)], q_out.at[half, rows_of(a)], xs_s.at[0],
+                    xs_r.at[a], sib,
+                ).wait_recv()
+                pass_q(a).start()
+
+        for d in steps:
+            token_copies[d - 1].wait_recv()
+            src = ring(z, 4 - d)
+            c = remote(x_ref.at[k, src], x_ref.at[k, src], us.at[d], ur.at[d], sib)
+            c.start()
+            token_cross.append(c)
+        normed, _ = normalize(x_ref[k].reshape(512, 768).astype(F32))
+        n_ref[...] = normed.astype(BF)
+
+        for a in range(3):
+
+            @pl.when(x != a)
+            def _():
+                remote(
+                    q_out.at[other_half, rows_of(a)], q_out.at[other_half, rows_of(a)],
+                    xf_s.at[a], xf_r.at[a], sib,
+                ).wait_recv()
+
+        vec_ref[...] = q_out[:, :, 512:640].reshape(768, 128).astype(F32).T[64:80]
+        bias[...] = jnp.zeros_like(bias)
+        for b in range(4):
+
+            @pl.when(z == b)
+            def _():
+                bias[:, 0:192] = vec_ref[2:3, 192 * b : 192 * b + 192]
+                bias[:, 384:576] = vec_ref[3:4, 192 * b : 192 * b + 192]
+
+        act = (normed * vec_ref[0:1] + vec_ref[1:2]).astype(BF)
+        a_ref[...] = act
+        mixed = dot(act, q_out[...].reshape(768, 640)) + bias[...]
+        v_ref[...] = mixed[:, 192:576].astype(BF)
+
+        def kv_copy(d):
+            return remote(
+                v_ref, vo_ref.at[y, k], vs.at[d], vr.at[d], device(ring(y, d), z, k, x)
+            )
+
+        for d in steps:
+
+            @pl.when(y + d < 4)
+            def _():
+                kv_copy(d).start()
+
+        swap = remote(v_ref, vo_ref.at[y, k], cs.at[0], cr.at[0], sib)
+        swap.start()
+        vo_ref[y, k] = v_ref[...]
         own_r = pltpu.make_async_copy(r_ref, ro_ref.at[k, z], loc.at[0])
         own_r.start()
         row_copies = []
@@ -747,46 +732,6 @@
             row_copies.append(c)
         row_first = remote(r_ref, ro_ref.at[k, z], ds.at[0], dr.at[0], sib)
         row_first.start()
-
-        weights = ((1, f_ref, fo_ref), (2, o_ref, oo_ref.at[k]), (3, p_ref, po_ref))
-
-        def weight_copy(a, d):
-            _, src, dst = weights[a - 1]
-            return remote(src, dst, ws.at[d], wr.at[a], device(y, z, k, ring(x, d)))
-
-        def weight_own(a):
-            _, src, dst = weights[a - 1]
-            return pltpu.make_async_copy(src, dst, loc.at[1])
-
-        for a in steps:
-
-            @pl.when(x == a)
-            def _():
-                for d in steps:
-                    weight_copy(a, d).start()
-                weight_own(a).start()
-
-        normed, _ = normalize(x_ref[k].reshape(512, 768).astype(F32))
-        n_ref[...] = normed.astype(BF)
-        act = (normed * g_ref[0:1] + g_ref[1:2]).astype(BF)
-        a_ref[...] = act
-        mixed = dot(act, wq_ref[...]) + b_ref[...]
-        v_ref[...] = mixed[:, 192:576].astype(BF)
-
-        def kv_copy(d):
-            return remote(
-                v_ref, vo_ref.at[y, k], vs.at[d], vr.at[d], device(ring(y, d), z, k, x)
-            )
-
-        for d in steps:
-
-            @pl.when(y + d < 4)
-            def _():
-                kv_copy(d).start()
-
-        swap = remote(v_ref, vo_ref.at[y, k], cs.at[0], cr.at[0], sib)
-        swap.start()
-        vo_ref[y, k] = v_ref[...]
         query = mixed[:, :192].astype(BF) * jnp.asarray(0.125, BF)
         q_ref[...] = query
         q_t = query.T
@@ -818,12 +763,44 @@
                 at = slice(64 * head, 64 * head + 64)
                 ot_ref[at] = ot_ref[at] * scale + dot(values_t[at], e.astype(BF))
 
+        weights = ((1, f_mid, fo_ref), (2, o_mid, oo_ref.at[k]), (3, p_mid, po_ref))
+
+        def weight_copy(a, d):
+            _, src, dst = weights[a - 1]
+            return remote(src, dst, ws.at[d], wr.at[a], device(y, z, k, ring(x, d)))
+
+        def weight_own(a):
+            _, src, dst = weights[a - 1]
+            return pltpu.make_async_copy(src, dst, loc.at[1])
+
         def diagonal(j, carry):
             @pl.when(j == 1)
             def _():
                 remote(v_ref, vo_ref.at[y, 1 - k], cs.at[0], cr.at[0], sib).wait_recv()
 
             block(y, lax.rem(k + j, 2), True)
+
+            @pl.when((j == 0) & (x == 1))
+            def _():
+                each(f_copy, finish)
+
+            @pl.when((j == 0) & (x == 2))
+            def _():
+                each(o_copy, finish)
+
+            for i in range(2):
+                @pl.when((j == 0) & (x == 3) & jnp.logical_not((y == z) & (z == 2 * k + i)))
+                def _():
+                    remote(p_send, p_mid.at[i], ps.at[0], pr.at[i], sib).wait_recv()
+
+            for a in steps:
+
+                @pl.when((j == 0) & (x == a))
+                def _():
+                    for d in steps:
+                        weight_copy(a, d).start()
+                    weight_own(a).start()
+
             return carry
 
         lax.fori_loop(0, 2, diagonal, 0)
@@ -864,7 +841,7 @@
             heads_copies.append(c)
         c = remote(h_buf, ho_ref.at[z, k], gs.at[0], gr.at[0], sib)
         c.start()
-        forward = [c, row_first]
+        forward_copies = [c, row_first]
         own_h = pltpu.make_async_copy(h_buf, ho_ref.at[z, k], loc.at[2])
         own_h.start()
         for d in steps:
@@ -872,7 +849,7 @@
             src = ring(z, 4 - d)
             c = remote(ro_ref.at[k, src], ro_ref.at[k, src], ds.at[d], dr.at[d], sib)
             c.start()
-            forward.append(c)
+            forward_copies.append(c)
         for a in steps:
 
             @pl.when(x == a)
@@ -885,16 +862,18 @@
 
         c = remote(oo_ref.at[k], oo_ref.at[k], os.at[0], orr.at[0], sib)
         c.start()
-        forward.append(c)
+        forward_copies.append(c)
         for d in steps:
             heads_copies[d - 1].wait_recv()
             src = ring(z, 4 - d)
             c = remote(ho_ref.at[src, k], ho_ref.at[src, k], gs.at[d], gr.at[d], sib)
             c.start()
-            forward.append(c)
-        for c in forward:
+            forward_copies.append(c)
+        for c in forward_copies + token_cross:
             c.wait()
-        for c in row_copies + heads_copies + [swap]:
+        for c in row_copies + heads_copies + token_copies + [swap]:
+            c.wait_send()
+        for c in message_q + cross_q + message_r + cross_r:
             c.wait_send()
         for d in steps:
 
@@ -912,6 +891,26 @@
             def _():
                 for d in steps:
                     weight_copy(a, d).wait_send()
+
+        @pl.when((x == 3) & (k == z // 2))
+        def _():
+            for a in range(1, 4):
+                p_copy(a).wait_send()
+
+            @pl.when(z != y)
+            def _():
+                p_copy(0).wait_send()
+
+        @pl.when(x < 3)
+        def _():
+            for d in steps:
+                x_copy(d).wait_send()
+
+        for a in range(3):
+
+            @pl.when(x != a)
+            def _():
+                pass_q(a).wait_send()
 
         own_r.wait()
         own_h.wait()
@@ -930,11 +929,33 @@
             jax.ShapeDtypeStruct((512, 192), BF),
             jax.ShapeDtypeStruct((512, 768), BF),
             jax.ShapeDtypeStruct((512, 768), BF),
+            jax.ShapeDtypeStruct((16, 48, 640), BF),
+            jax.ShapeDtypeStruct((2, 4, 128, 768), BF),
+            jax.ShapeDtypeStruct((16, 768), F32),
         ],
-        2,
-        (4, 4, 4, 4, 4, 4, 4, 4, 4, 4, 1, 1, 4, 4, 4, 4, 3),
-        (tokens, wq, bias, rows768, rows, fc, out, proj),
+        0,
+        (4,) * 8 + (16,) * 4 + (4, 2) + (4,) * 8
+        + (4, 4, 4, 4, 4, 4, 4, 4, 4, 4, 1, 1, 4, 4, 4, 4, 3),
+        (w_qkv, w_fc, w_out, w_proj, vectors, tokens, cotangent),
         scratch=[
+            pltpu.VMEM((16, wide_q), F32),
+            pltpu.VMEM((16, wide_r), F32),
+            pltpu.VMEM((16, wide_q), BF),
+            pltpu.VMEM((16, wide_r), BF),
+            pltpu.VMEM((8, 16, wide_q), BF),
+            pltpu.VMEM((8, 16, wide_r), BF),
+            pltpu.VMEM((48, 3072), F32),
+            pltpu.VMEM((48, 2432), F32),
+            pltpu.VMEM((48, 768), F32),
+            pltpu.VMEM((192, 768), F32),
+            pltpu.VMEM((4, 48, 640), BF),
+            pltpu.VMEM((8, 48, 384), BF),
+            pltpu.VMEM((2, 48, 384), BF),
+            pltpu.VMEM((192, 768), BF),
+            pltpu.VMEM((16, 48, 384), BF),
+            pltpu.VMEM((16, 48, 384), BF),
+            pltpu.VMEM((2, 192, 768), BF),
+            pltpu.VMEM((1, 640), F32),
             pltpu.VMEM((3, 192, 512), BF),
             pltpu.VMEM((8, 512), F32),
             pltpu.VMEM((8, 512), F32),
@@ -942,19 +963,19 @@
             pltpu.VMEM((512, 384), BF),
         ],
         spaces=(
-            [VMEM, VMEM, VMEM, VMEM, ANY, ANY, ANY, ANY],
-            [ANY, VMEM, VMEM, VMEM, ANY, ANY, ANY, ANY, VMEM, VMEM, VMEM],
+            [VMEM] * 6 + [ANY],
+            [ANY, VMEM, VMEM, VMEM, ANY, ANY, ANY, ANY] + [VMEM] * 6,
         ),
-        name="attend",
+        name="forward",
     )
 
 
-def attend_back(query, branch, wo, kv_all, out_t, lse, fc, proj):
+def attend_back(query, branch, wo, kv_all, out_t, lse, fc, proj, base, result):
     def kernel(
-        q_ref, b_ref, w_ref, kv_ref, ot_ref, lse_ref, f_ref, p_ref,
-        dq_ref, dkv_ref, fo_ref, po_ref,
-        qt, gt, qm, gm, delta, dqt, out_buf, keep, got, far, f_far, p_far,
-        cs, cr, ys, yr, fs, fr, ps, pr,
+        q_ref, b_ref, w_ref, kv_ref, ot_ref, lse_ref, f_ref, p_ref, base_ref, res_ref,
+        dq_ref, dkv_ref, fo_ref, po_ref, out_ref,
+        qt, gt, qm, gm, delta, dqt, out_buf, keep, got, far, f_far, p_far, r_far,
+        cs, cr, ys, yr, fs, fr, ps, pr, rs, rr,
     ):
         y, z, k, x = coords()
         sib = device(y, z, 1 - k, x)
@@ -962,8 +983,17 @@
         greet(
             [sib]
             + [device(ring(y, d), z, k, x) for d in steps]
+            + [device(y, ring(z, d), k, x) for d in steps]
             + [device(y, z, k, ring(x, d)) for d in steps]
         )
+        results = []
+        for d in steps:
+            b = ring(z, d)
+            c = remote(
+                res_ref.at[b], r_far.at[d - 1], rs.at[d - 1], rr.at[d - 1], device(y, b, k, x)
+            )
+            c.start()
+            results.append(c)
         weights = []
         for d in steps:
             b = ring(x, d)
@@ -1059,6 +1089,15 @@
             + p_far[1].astype(F32)
             + p_far[2].astype(F32)
         ).astype(BF)
+        for c in results:
+            c.wait()
+        out_ref[...] = (
+            base_ref[...]
+            + res_ref[z].astype(F32)
+            + r_far[0].astype(F32)
+            + r_far[1].astype(F32)
+            + r_far[2].astype(F32)
+        )
         dkv_ref[...] = keep[0].astype(F32) + got[0].astype(F32)
         for d in (1, 2, 3):
 
@@ -1082,10 +1121,11 @@
             jax.ShapeDtypeStruct((512, 384), F32),
             jax.ShapeDtypeStruct((4, 48, 384), BF),
             jax.ShapeDtypeStruct((2, 48, 768), BF),
+            jax.ShapeDtypeStruct((128, 768), F32),
         ],
         5,
-        (4, 4, 4, 4, 3, 3, 3, 3),
-        (query, branch, wo, kv_all, out_t, lse, fc, proj),
+        (4, 4, 4, 4, 3, 3, 3, 3, 3, 3),
+        (query, branch, wo, kv_all, out_t, lse, fc, proj, base, result),
         scratch=[
             pltpu.VMEM((3, 192, 512), BF),
             pltpu.VMEM((3, 192, 512), BF),
@@ -1099,8 +1139,9 @@
             pltpu.VMEM((4, 512, 384), BF),
             pltpu.VMEM((3, 4, 48, 384), BF),
             pltpu.VMEM((3, 2, 48, 768), BF),
+            pltpu.VMEM((3, 128, 768), BF),
         ],
-        spaces=([VMEM] * 8, [VMEM] * 4),
+        spaces=([VMEM] * 10, [VMEM] * 5),
         name="attend_back",
     )
 
@@ -1120,19 +1161,23 @@
     )
 
 
-def feed_forward(heads_all, x_group, dy_group, wo, wf, wp, rows768, fc_bias):
+def feed_forward(heads_all, x_group, dy_group, wo, wf, wp, vec_rows):
     def kernel(
-        h_ref, x_ref, dy_ref, wo_ref, wf_ref, wp_ref, v_ref, fb_ref,
-        out_ref, gx_ref, bo_ref, gwf_ref, gwp_ref, gfb_ref, gv_ref,
-        a2, act, df, x_two, normed, inverse, norm_other, norm_mine, res_other, res_mine,
-        norm_got, res_got, norm_far, res_far, branch,
-        cs, cr, es, er, zs, zr, ws, wr, bs, br,
+        h_ref, x_ref, dy_ref, wo_ref, wf_ref, wp_ref, v_ref,
+        base_ref, res_mine, gx_ref, bo_ref, gwf_ref, gwp_ref, gfb_ref, gv_ref,
+        a2, act, df, x_two, normed, inverse, norm_other, norm_mine, res_other,
+        norm_got, res_got, norm_far, branch,
+        cs, cr, es, er, zs, zr, bs, br,
     ):
         y, z, k, x = coords()
         sib = device(y, z, 1 - k, x)
         steps = (1, 2, 3)
         greet([sib] + [device(y, ring(z, d), k, x) for d in steps])
-        out_bias, gain, shift, proj_bias = (v_ref[i : i + 1] for i in range(4))
+        out_bias, gain, shift, proj_bias = (v_ref[i : i + 1] for i in range(4, 8))
+        fc_bias = jnp.zeros((1, 384), F32)
+        for b in range(4):
+            row = v_ref[8 + b : 9 + b, pl.ds(pl.multiple_of(384 * k, 128), 384)]
+            fc_bias = fc_bias + jnp.where(z == b, row, 0.0)
 
         def half(kk, norm_ref, res_ref):
             two = x_ref[kk].reshape(512, 768).astype(F32) + out_bias
@@ -1147,7 +1192,7 @@
             inverse[...] = jnp.broadcast_to(inv, (512, 128))
             a = (n * gain + shift).astype(BF)
             a2[kk] = a
-            hidden = dot(a, wf_ref[...]) + fb_ref[...]
+            hidden = dot(a, wf_ref[...]) + fc_bias
             square = hidden * hidden
             t = jnp.tanh(0.7978845608028654 * (hidden + 0.044715 * square * hidden))
             act_blk = (0.5 * hidden * (1.0 + t)).astype(BF)
@@ -1181,25 +1226,23 @@
             swaps.append(c)
         half(k, norm_mine, res_mine)
         sends = []
-        for i, (mine, got, far, s, r) in enumerate(
-            ((norm_mine, norm_got, norm_far, zs, zr), (res_mine, res_got, res_far, ws, wr))
-        ):
-            for d in steps:
-                b = ring(z, d)
-                swaps[4 * i + d - 1].wait_recv()
-                mine[b] = (mine[b].astype(F32) + got[b].astype(F32)).astype(BF)
-                c = remote(
-                    mine.at[b], far.at[d - 1], s.at[d - 1], r.at[d - 1], device(y, b, k, x)
-                )
-                c.start()
-                sends.append(c)
+        for d in steps:
+            b = ring(z, d)
+            swaps[d - 1].wait_recv()
+            norm_mine[b] = (norm_mine[b].astype(F32) + norm_got[b].astype(F32)).astype(BF)
+            c = remote(
+                norm_mine.at[b], norm_far.at[d - 1], zs.at[d - 1], zr.at[d - 1],
+                device(y, b, k, x),
+            )
+            c.start()
+            sends.append(c)
         tn = (((0,), (0,)), ((), ()))
         gwf = lax.dot_general(a2[0], df[0], tn, preferred_element_type=F32)
         gwf += lax.dot_general(a2[1], df[1], tn, preferred_element_type=F32)
         gwf_ref[...] = gwf.astype(BF)
         own_rows = pl.ds(pl.multiple_of(128 * z, 128), 128)
         swaps[3].wait_recv()
-        for c in sends[:3]:
+        for c in sends:
             c.wait_recv()
         da = (
             norm_mine[z].astype(F32)
@@ -1236,18 +1279,10 @@
         gv_ref[1:2] = jnp.sum(da * n, 0, keepdims=True)
         gv_ref[2:3] = jnp.sum(da, 0, keepdims=True)
         gv_ref[3:4] = jnp.sum(dy, 0, keepdims=True)
-        swaps[7].wait_recv()
-        for c in sends[3:]:
+        for c in swaps[4:]:
             c.wait_recv()
-        out_ref[...] = (
-            x_two[own_rows]
-            + proj_bias
-            + res_mine[z].astype(F32)
-            + res_got[z].astype(F32)
-            + res_far[0].astype(F32)
-            + res_far[1].astype(F32)
-            + res_far[2].astype(F32)
-        )
+        res_mine[...] = (res_mine[...].astype(F32) + res_got[...].astype(F32)).astype(BF)
+        base_ref[...] = x_two[own_rows] + proj_bias
         for c in branches:
             c.wait()
         for c in swaps + sends:
@@ -1257,6 +1292,7 @@
         kernel,
         [
             jax.ShapeDtypeStruct((128, 768), F32),
+            jax.ShapeDtypeStruct((4, 128, 768), BF),
             jax.ShapeDtypeStruct((128, 768), F32),
             jax.ShapeDtypeStruct((4, 128, 768), BF),
             jax.ShapeDtypeStruct((768, 384), BF),
@@ -1265,8 +1301,8 @@
             jax.ShapeDtypeStruct((4, 768), F32),
         ],
         3,
-        (4, 4, 4, 4, 3, 3, 3, 3, 3, 3),
-        (heads_all, x_group, dy_group, wo, wf, wp, rows768, fc_bias),
+        (4, 4, 4, 4, 3, 3, 3, 3),
+        (heads_all, x_group, dy_group, wo, wf, wp, vec_rows),
         scratch=[
             pltpu.VMEM((2, 512, 768), BF),
             pltpu.VMEM((2, 512, 384), BF),
@@ -1275,10 +1311,10 @@
             pltpu.VMEM((512, 768), F32),
             pltpu.VMEM((512, 128), F32),
         ]
-        + [pltpu.VMEM((4, 128, 768), BF)] * 6
-        + [pltpu.VMEM((3, 128, 768), BF)] * 2
+        + [pltpu.VMEM((4, 128, 768), BF)] * 5
+        + [pltpu.VMEM((3, 128, 768), BF)]
         + [pltpu.VMEM((128, 768), BF)],
-        spaces=([VMEM] * 8, [VMEM] * 7),
+        spaces=([VMEM] * 7, [VMEM] * 8),
         name="feed_forward",
     )
 
@@ -1311,42 +1347,27 @@
     vec_m,
     vec_v,
 ):
-    y, z, k, x = coords()
     state = (
         w_qkv, qkv_m, qkv_v, w_out, out_m, out_v, w_fc, fc_m, fc_v, w_proj, proj_m, proj_v,
         vectors, vec_m, vec_v,
     )
-    wq, fc_part, out_part, proj_part, x_group = first_gather(
-        w_qkv, w_fc, w_out, w_proj, vectors, tokens[0]
-    )
+    (
+        heads_all, out_t, lse, kv_all, dy_group, wf, wo, wp, query, act_one, normed_core,
+        wq, x_group, vec_rows,
+    ) = forward(w_qkv, w_fc, w_out, w_proj, vectors, tokens[0], cotangent[0])
     wq = wq.reshape(768, 640)
-    vec_rows = wq[:, 576:592].astype(F32).T
-    bias = jnp.concatenate(
-        [
-            lax.dynamic_slice(vec_rows, (2, 192 * z), (1, 192)),
-            jnp.zeros((1, 192), F32),
-            lax.dynamic_slice(vec_rows, (3, 192 * z), (1, 192)),
-            jnp.zeros((1, 64), F32),
-        ],
-        1,
-    )
-    fc_bias = lax.dynamic_slice(vec_rows[8:12].reshape(1, 3072), (0, (2 * z + k) * 384), (1, 384))
-    heads_all, out_t, lse, kv_all, dy_group, wf, wo, wp, query, act_one, normed_core = attend(
-        x_group, wq, bias, vec_rows[0:2], cotangent[0], fc_part, out_part, proj_part
-    )
     wo = wo.reshape(2, 768, 384)
-    output, grad_x_two, branch_core, grad_w_fc, grad_w_proj, grad_fc_bias, vec_sums = feed_forward(
+    base, result, grad_x_two, branch_core, grad_w_fc, grad_w_proj, grad_fc_bias, vec_sums = feed_forward(
         heads_all,
         x_group,
         dy_group,
         wo,
         wf.reshape(768, 384),
         wp.reshape(384, 768),
-        vec_rows[4:8],
-        fc_bias,
+        vec_rows,
     )
     branch_core = branch_core.reshape(512, 768)
-    grad_query, grad_kv, fc_sum, proj_sum = attend_back(
+    grad_query, grad_kv, fc_sum, proj_sum, result_sum = attend_back(
         query,
         branch_core,
         wo,
@@ -1355,8 +1376,10 @@
         lse,
         grad_w_fc.reshape(4, 4, 48, 384),
         grad_w_proj.reshape(2, 4, 48, 768),
+        base,
+        result,
     )
-    grad_inputs, *new_state = last_sums(
+    grad_one, last_rows, proj_rows = last_sums(
         (
             act_one,
             normed_core,
@@ -1367,13 +1390,12 @@
             wq,
             vec_sums,
             grad_fc_bias,
-            tokens[0],
-            grad_x_two,
-            vec_rows[0:1],
         ),
         fc_sum,
         proj_sum,
-        state,
+    )
+    output, grad_inputs, *new_state = finish(
+        grad_one, grad_x_two, tokens[0], vec_rows, last_rows, proj_rows, result_sum, state
     )
     return (output[None], grad_inputs[None], *new_state)
 

time: 230 us -> 203 us (0.88)
  local copies, waits for them, and re-layouts: 15.6 us -> 0 us
  Pallas kernels: 213 us -> 202 us
    pallas_call x5 -> x4, Pallas kernels: 213 us -> 199 us  [comm(): pl.pallas_call(kernel, out_shape=outs, in_specs=[ANY] * len(args) if spac...]
    unnamed x52 -> x0, local copies, waits for them, and re-layouts: 12.6 us -> none
    pallas_call x0 -> x1, Pallas kernels: none -> 3.26 us  [finish(): pl.pallas_call(kernel, out_shape=[jax.ShapeDtypeStruct((128, 768), F32)]...]
where the time goes in v5:
time: 203 us
  Pallas kernels  202 us (100%)
    pallas_call x4, Pallas kernels, comm(): pl.pallas_call(kernel, out_shape=outs, in_specs=[ANY] * len(args) if spac...  199 us

profile of v5, /device:TPU:29, one launch (start us, length us, event | category | flops | bytes accessed | tf_op | source)
XLA Modules:
  0.0 202.9 jit_solution(15097077411288010392)
XLA Ops:
  0.7 75.4 %forward.1 = (bf16[4,2,512,192]{3,2,1,0:T(8,128)(2,1)}, f32[192,512]{1,0:T(8,128)}, f32[8,512]{1,0:T(8,128)}, bf16[4,2,512,384]{3,2,1,0:T(8,128)(2,1)}, bf16[2,4...) custom-call(f32[6,2304]{1,0:T(8,128)} %refs_7_.1, ...), custom_call_target="tpu_custom_call" | custom-call | tf_op jit(solution)/shard_map/forward/pallas_call | solution.py:48
  76.0 34.3 %feed_forward.1 = (f32[128,768]{1,0:T(8,128)}, bf16[4,128,768]{2,1,0:T(8,128)(2,1)}, f32[128,768]{1,0:T(8,128)}, bf16[4,128,768]{2,1,0:T(8,128)(2,1)}, bf16[768,...) custom-call(bf16[4,2,512,192]{3,2,1,0:T(8,128)(2,1)} %get-tuple-element.66.h_ref.refs_2_, ...), custom_call_target="tpu_custom_call" | custom-call | tf_op jit(solution)/shard_map/feed_forward/pallas_call | solution.py:48
  110.3 34.2 %attend_back.1 = (bf16[512,192]{1,0:T(8,128)(2,1)}, f32[512,384]{1,0:T(8,128)}, bf16[4,48,384]{2,1,0:T(8,128)(2,1)}, bf16[2,48,768]{2,1,0:T(8,128)(2,1)}, f32[128,768]{1,0:T(8,128)}) custom-call(bf16[512,192]{1,0:T(8,128)(2,1)} %get-tuple-element.67.q_ref, bf16[512,768]{1,0:T(8,128)(2,1)} %bitcast.13, bf16[2,768,384]{2,1,0:T(8,128)(2,1)} %bitcast.12, ...), custom_call_target="tpu_custom_call" | custom-call | tf_op jit(solution)/shard_map/attend_back/pallas_call | solution.py:48
  144.5 54.9 %last_sums.1 = (f32[128,768]{1,0:T(8,128)}, f32[2,8,3200]{2,1,0:T(8,128)}, f32[24,768]{1,0:T(8,128)}) custom-call(bf16[512,768]{1,0:T(8,128)(2,1)} %get-tuple-element.64.refs_0_, bf16[512,768]{1,0:T(8,128)(2,1)} %get-tuple-element.65.refs_1_, bf16[4,2,512,192]{3,2,1,0:T(8,128)(2,1)} %get-tuple-element.66.h_ref.refs_2_, ...), custom_call_target="tpu_custom_call" | custom-call | tf_op jit(solution)/shard_map/last_sums/pallas_call | solution.py:48
  199.4 3.3 %finish.1 = (f32[128,768]{1,0:T(8,128)}, f32[128,768]{1,0:T(8,128)}, f32[6,2304]{1,0:T(8,128)}, f32[6,2304]{1,0:T(8,128)}, f32[6,2304]{1,0:T(8,128)}, /*index=5*...) custom-call(f32[128,768]{1,0:T(8,128)} %get-tuple-element.89.refs_0_, ...), custom_call_target="tpu_custom_call" | custom-call | tf_op jit(solution)/shard_map/finish/pallas_call | solution.py:436

commit v6 on v5

--- a/solution.py
+++ b/solution.py
@@ -35,7 +35,7 @@
     barrier = pltpu.get_barrier_semaphore()
     for one in devices:
         pl.semaphore_signal(barrier, inc=1, device_id=one, device_id_type=MESH)
-    pl.semaphore_wait(barrier, len(devices))
+    return lambda: pl.semaphore_wait(barrier, len(devices))
 
 
 def remote(src, dst, send, recv, to):
@@ -59,28 +59,28 @@
 
 
 def last_sums(pieces, fc, proj):
-    wide = 3200
+    wide = 1664
 
     def kernel(*refs):
         (
             act_ref, n_ref, h_ref, gq_ref, gkv_ref, br_ref, wq_ref, vs_ref, fb_ref,
             fc_ref, proj_ref,
         ) = refs[:11]
-        one_out, rows_out, proj_out = refs[11:14]
+        one_out, rows_out, proj_out, fc_out = refs[11:15]
         (
             one_far, mix_got, mix_sum, mix_far, vec_far, mix_mine, vec_mine,
-            mix_all, fc_all, vec_all, proj_all, proj_sum, out_send,
+            mix_all, vec_all, proj_sum, out_send, fc_send,
             one_ref, mix_other, mix_ref, vec_ref,
             act_t, heads, heads_t, d_ref, right_one, right_two, vec_rows,
-        ) = refs[14:38]
+        ) = refs[15:38]
         (
-        zs, zr, cs, cr, s1, r1, s2, r2, s3, r3, s4, r4, s5, r5, s6, r6, s7, r7, s8, r8, loc,
+        zs, zr, cs, cr, s1, r1, s2, r2, s3, r3, s4, r4, s5, r5, s7, r7, s8, r8, loc,
         ) = refs[38:]
         y, z, k, x = coords()
         me = y * 4 + z
         sib = device(y, z, 1 - k, x)
         steps = (1, 2, 3)
-        greet(
+        everyone = greet(
             [sib]
             + [device(y, z, j, ring(x, d)) for d in steps for j in (k, 1 - k)]
             + [
@@ -121,12 +121,59 @@
             return total.reshape(4, 4, 48, 384)
 
         mix_other[...] = product(1 - k).astype(BF)
+        everyone()
         swap = []
         for d in (1, 2, 3, 0):
             b = ring(x, d)
             c = remote(mix_other.at[:, b], mix_got.at[b], cs.at[d], cr.at[d], sib)
             c.start()
             swap.append(c)
+        def proj_last(i):
+            return remote(
+                proj_sum.at[i], proj_out, s8.at[i], r8.at[0],
+                device(y, z, x // 2, lax.rem(2 * x + i, 4)),
+            )
+
+        def proj_here(i):
+            return (k == x // 2) & (x == lax.rem(2 * x + i, 4))
+
+        holder = k == z // 2
+
+        @pl.when(holder)
+        def _():
+            for i in range(2):
+                proj_sum[i] = proj_ref[24 * i : 24 * i + 24]
+
+                @pl.when(jnp.logical_not(proj_here(i)))
+                def _():
+                    proj_last(i).start()
+
+                @pl.when(proj_here(i))
+                def _():
+                    proj_out[...] = proj_sum[i]
+
+        def last_here(i):
+            return k * 4 + x == i
+
+        def fc_last(i):
+            return remote(
+                fc_send.at[i], fc_out.at[k], s4.at[i], r4.at[k], device(y, z, i // 4, i % 4)
+            )
+
+        @pl.when(z == x)
+        def _():
+            for i in range(8):
+                fc_send[i, 0:6] = fc_ref[6 * i : 6 * i + 6]
+                fc_send[i, 6:8] = jnp.zeros((2, 1536), F32)
+
+                @pl.when(jnp.logical_not(last_here(i)))
+                def _():
+                    fc_last(i).start()
+
+                @pl.when(last_here(i))
+                def _():
+                    fc_out[k] = fc_send[i]
+
         mix_ref[...] = product(k).astype(BF)
         one = lax.dot_general(
             d_ref[...], wq_ref[...], (((1,), (1,)), ((), ())), preferred_element_type=F32
@@ -189,26 +236,6 @@
                 return carry
 
             lax.fori_loop(0, 16, step, 0)
-
-        all_start(fc_ref, fc_all, s4, r4)
-
-        def proj_copy(j):
-            return remote(
-                proj_ref.at[j], proj_all.at[y], s6.at[j], r6.at[y], device(z, 2 * k + j, k, x)
-            )
-
-        for j in range(2):
-            here = (y == z) & (z == 2 * k + j)
-
-            @pl.when(jnp.logical_not(here))
-            def _():
-                proj_copy(j).start()
-
-            @pl.when(here)
-            def _():
-                c = pltpu.make_async_copy(proj_ref.at[j], proj_all.at[y], loc.at[1])
-                c.start()
-                c.wait()
 
         swap[3].wait_recv()
         for c in along:
@@ -237,54 +264,13 @@
             + one_far[2].astype(F32)
         )
 
-        def proj_last(i):
-            return remote(
-                proj_sum.at[i], proj_out, s8.at[i], r8.at[0],
-                device(y, z, x // 2, lax.rem(2 * x + i, 4)),
-            )
-
-        def proj_here(i):
-            return (k == x // 2) & (x == lax.rem(2 * x + i, 4))
-
-        holder = k == z // 2
-        for a in range(4):
-
-            @pl.when(holder & jnp.logical_not((a == y) & (z == y)))
-            def _():
-                remote(proj_ref.at[0], proj_all.at[a], s6.at[0], r6.at[a], sib).wait_recv()
-
-        @pl.when(holder)
-        def _():
-            total = (
-                proj_all[0].astype(F32)
-                + proj_all[1].astype(F32)
-                + proj_all[2].astype(F32)
-                + proj_all[3].astype(F32)
-            )
-            for i in range(2):
-                proj_sum[i] = total[24 * i : 24 * i + 24]
-
-                @pl.when(jnp.logical_not(proj_here(i)))
-                def _():
-                    proj_last(i).start()
-
-                @pl.when(proj_here(i))
-                def _():
-                    c = pltpu.make_async_copy(proj_sum.at[i], proj_out, loc.at[2])
-                    c.start()
-                    c.wait()
-
         def last_copy(i):
             return remote(
                 out_send.at[i], rows_out.at[k], s7.at[i], r7.at[k], device(y, z, i // 4, i % 4)
             )
 
-        def last_here(i):
-            return k * 4 + x == i
-
         @pl.when(z == x)
         def _():
-            all_receive(fc_ref, fc_all, s4, r4)
             all_receive(mix_mine, mix_all, s3, r3)
             all_receive(vec_mine, vec_all, s5, r5)
 
@@ -297,14 +283,13 @@
                 )
 
             for b in range(4):
-                m, f = four(mix_all, b), four(fc_all, b)
+                m = four(mix_all, b)
                 for i in range(8):
                     rows = slice(6 * i, 6 * i + 6)
                     out_send[i, 0:6, 384 * b : 384 * b + 384] = m[rows]
-                    out_send[i, 0:6, 1536 + 384 * b : 1920 + 384 * b] = f[rows]
             v = four(vec_all, 0) + four(vec_all, 1) + four(vec_all, 2) + four(vec_all, 3)
             for i in range(8):
-                out_send[i, 0:6, 3072:3200] = v[6 * i : 6 * i + 6]
+                out_send[i, 0:6, 1536:1664] = v[6 * i : 6 * i + 6]
                 out_send[i, 6:8, :] = jnp.zeros((2, wide), F32)
             for i in range(8):
 
@@ -323,6 +308,7 @@
             @pl.when(jnp.logical_not((z == x) & (k == j)))
             def _():
                 remote(out_send.at[0], rows_out.at[j], s7.at[0], r7.at[j], sib).wait_recv()
+                remote(fc_send.at[0], fc_out.at[j], s4.at[0], r4.at[j], sib).wait_recv()
 
         @pl.when(jnp.logical_not((k == z // 2) & (x == (4 * k + x) // 2)))
         def _():
@@ -335,6 +321,7 @@
                 @pl.when(jnp.logical_not(last_here(i)))
                 def _():
                     last_copy(i).wait_send()
+                    fc_last(i).wait_send()
 
         for i in range(2):
 
@@ -342,13 +329,6 @@
             def _():
                 proj_last(i).wait_send()
 
-        for j in range(2):
-
-            @pl.when(jnp.logical_not((y == z) & (z == 2 * k + j)))
-            def _():
-                proj_copy(j).wait_send()
-
-        all_finish(fc_ref, fc_all, s4, r4)
         all_finish(mix_mine, mix_all, s3, r3)
         all_finish(vec_mine, vec_all, s5, r5)
         for c in swap + along + ones:
@@ -360,9 +340,10 @@
             jax.ShapeDtypeStruct((128, 768), F32),
             jax.ShapeDtypeStruct((2, 8, wide), F32),
             jax.ShapeDtypeStruct((24, 768), F32),
+            jax.ShapeDtypeStruct((2, 8, 1536), F32),
         ],
         6,
-        (3, 3, 4, 4, 3, 3, 3, 3, 4, 16, 4, 16, 4, 16, 2, 4, 8, 2, 2, 1, 4),
+        (3, 3, 4, 4, 3, 3, 3, 3, 4, 16, 8, 2, 4, 16, 8, 2, 2, 1, 4),
         (*pieces, fc, proj),
         scratch=[
             pltpu.VMEM((3, 128, 768), BF),
@@ -373,11 +354,10 @@
             pltpu.VMEM((4, 48, 384), BF),
             pltpu.VMEM((4, 48, 128), BF),
             pltpu.VMEM((16, 48, 384), BF),
-            pltpu.VMEM((16, 48, 384), BF),
             pltpu.VMEM((16, 48, 128), BF),
-            pltpu.VMEM((4, 48, 768), BF),
             pltpu.VMEM((2, 24, 768), F32),
             pltpu.VMEM((8, 8, wide), F32),
+            pltpu.VMEM((8, 8, 1536), F32),
             pltpu.VMEM((4, 128, 768), BF),
             pltpu.VMEM((4, 4, 48, 384), BF),
             pltpu.VMEM((4, 4, 48, 384), BF),
@@ -390,18 +370,18 @@
             pltpu.VMEM((512, 768), BF),
             pltpu.VMEM((128, 768), F32),
         ],
-        spaces=([VMEM] * 11, [VMEM] * 3),
+        spaces=([VMEM] * 11, [VMEM] * 4),
         name="last_sums",
     )
 
 
-def finish(grad_one, grad_x_two, tokens, vec_rows, rows, proj_rows, result, state):
+def finish(grad_one, grad_x_two, tokens, vec_rows, rows, proj_rows, fc_rows, result, state):
     def kernel(*refs):
-        one_ref, gx_ref, t_ref, v_ref, rows_ref, p_ref, res_ref = refs[:7]
-        state_ref = refs[7:22]
-        out_ref, gin_ref = refs[22:24]
-        new_ref = refs[24:39]
-        g_qkv, g_out, g_fc = refs[39:]
+        one_ref, gx_ref, t_ref, v_ref, rows_ref, p_ref, f_ref, res_ref = refs[:8]
+        state_ref = refs[8:23]
+        out_ref, gin_ref = refs[23:25]
+        new_ref = refs[25:40]
+        g_qkv, g_out, g_fc = refs[40:]
         out_ref[...] = res_ref[...]
         normed, inverse = normalize(t_ref[...].astype(F32))
         gin_ref[...] = gx_ref[...] + normalize_back(normed, inverse, v_ref[0:1], one_ref[...])
@@ -417,8 +397,8 @@
             g_out[:, q + 96 : q + 192] = two_half[:, 288:384]
             for j in range(2):
                 at = 384 * (2 * b + j)
-                g_fc[:, at : at + 384] = rows_ref[j, 0:6, 1536 + 384 * b : 1920 + 384 * b]
-        g_vec = rows_ref[0, 0:6, 3072:3084] + rows_ref[1, 0:6, 3072:3084]
+                g_fc[:, at : at + 384] = f_ref[j, 0:6, 384 * b : 384 * b + 384]
+        g_vec = rows_ref[0, 0:6, 1536:1548] + rows_ref[1, 0:6, 1536:1548]
         for i, (gradient, rate, decay) in enumerate(
             (
                 (g_qkv[...], 0.1, 0.1),
@@ -437,7 +417,7 @@
         kernel,
         out_shape=[jax.ShapeDtypeStruct((128, 768), F32)] * 2
         + [jax.ShapeDtypeStruct(one.shape, F32) for one in state],
-        in_specs=[VMEM] * 22,
+        in_specs=[VMEM] * 23,
         out_specs=[VMEM] * 17,
         scratch_shapes=[
             pltpu.VMEM((6, 2304), F32),
@@ -446,7 +426,7 @@
         ],
         compiler_params=pltpu.CompilerParams(vmem_limit_bytes=LIMIT),
         name="finish",
-    )(grad_one, grad_x_two, tokens, vec_rows, rows, proj_rows, result, *state)
+    )(grad_one, grad_x_two, tokens, vec_rows, rows, proj_rows, fc_rows, result, *state)
 
 
 def head_rows(matrix, head):
@@ -481,14 +461,14 @@
         bias, qt, m_ref, l_ref, h_buf, v_ref,
         mq_s, mq_r, fq_s, fq_r, mr_s, mr_r, fr_s, fr_r, s1, r1, s2, r2, ps, pr,
         xs_s, xs_r, xf_s, xf_r, ts, tr, us, ur,
-        vs, vr, rs, rr, cs, cr, ds, dr, ws, wr, os, orr, hs, hr, gs, gr, loc,
+        vs, vr, rs, rr, cs, cr, ds, dr, ws, wr, wf, os, orr, hs, hr, gs, gr, loc,
     ):
         y, z, k, x = coords()
         me = y * 4 + z
         t = k * 4 + x
         sib = device(y, z, 1 - k, x)
         steps = (1, 2, 3)
-        greet(
+        everyone = greet(
             [sib]
             + [device(y, z, k, ring(x, d)) for d in steps]
             + [
@@ -525,6 +505,7 @@
         wide_one[0:6, 1152:1164] = wv_ref[...]
         packed_q[...] = wide_one[...].astype(BF)
         got_q[t] = packed_q[...]
+        everyone()
         message_q = first(packed_q, got_q, mq_s, mq_r)
         token_copies = []
         for d in steps:
@@ -684,6 +665,63 @@
         normed, _ = normalize(x_ref[k].reshape(512, 768).astype(F32))
         n_ref[...] = normed.astype(BF)
 
+        weights = ((1, f_mid, fo_ref, 8), (2, o_mid, oo_ref, 8), (3, p_mid, po_ref, 1))
+
+        def ends(a, half):
+            _, src, dst, n = weights[a - 1]
+            at = pl.ds(n * half, n)
+            return src.at[at], (dst.at[k, at] if a == 2 else dst.at[at])
+
+        def direct(a, half, d):
+            src, dst = ends(a, half)
+            return remote(
+                src, dst, ws.at[4 * half + d], wr.at[2 * a + half], device(y, z, k, ring(x, d))
+            )
+
+        def onward(a, half, d):
+            _, dst = ends(a, half)
+            return remote(
+                dst, dst, wf.at[a], wr.at[2 * a + half], device(y, z, k, ring(x, d))
+            )
+
+        def weight_own(a):
+            _, src, dst, _ = weights[a - 1]
+            return pltpu.make_async_copy(src, dst.at[k] if a == 2 else dst, loc.at[1])
+
+        @pl.when(x == 1)
+        def _():
+            each(f_copy, finish)
+
+        @pl.when(x == 2)
+        def _():
+            each(o_copy, finish)
+
+        for i in range(2):
+            @pl.when((x == 3) & jnp.logical_not((y == z) & (z == 2 * k + i)))
+            def _():
+                remote(p_send, p_mid.at[i], ps.at[0], pr.at[i], sib).wait_recv()
+
+        for a in steps:
+
+            @pl.when(x == a)
+            def _():
+                for half_at, d in ((0, 1), (1, 3), (1, 1), (0, 3)):
+                    direct(a, half_at, d).start()
+                weight_own(a).start()
+
+        def move_on():
+            for a in steps:
+
+                @pl.when(x == (a + 1) % 4)
+                def _():
+                    direct(a, 0, 1).wait_recv()
+                    onward(a, 0, 1).start()
+
+                @pl.when(x == (a + 3) % 4)
+                def _():
+                    direct(a, 1, 1).wait_recv()
+                    onward(a, 1, 3).start()
+
         for a in range(3):
 
             @pl.when(x != a)
@@ -763,43 +801,12 @@
                 at = slice(64 * head, 64 * head + 64)
                 ot_ref[at] = ot_ref[at] * scale + dot(values_t[at], e.astype(BF))
 
-        weights = ((1, f_mid, fo_ref), (2, o_mid, oo_ref.at[k]), (3, p_mid, po_ref))
-
-        def weight_copy(a, d):
-            _, src, dst = weights[a - 1]
-            return remote(src, dst, ws.at[d], wr.at[a], device(y, z, k, ring(x, d)))
-
-        def weight_own(a):
-            _, src, dst = weights[a - 1]
-            return pltpu.make_async_copy(src, dst, loc.at[1])
-
         def diagonal(j, carry):
             @pl.when(j == 1)
             def _():
                 remote(v_ref, vo_ref.at[y, 1 - k], cs.at[0], cr.at[0], sib).wait_recv()
 
             block(y, lax.rem(k + j, 2), True)
-
-            @pl.when((j == 0) & (x == 1))
-            def _():
-                each(f_copy, finish)
-
-            @pl.when((j == 0) & (x == 2))
-            def _():
-                each(o_copy, finish)
-
-            for i in range(2):
-                @pl.when((j == 0) & (x == 3) & jnp.logical_not((y == z) & (z == 2 * k + i)))
-                def _():
-                    remote(p_send, p_mid.at[i], ps.at[0], pr.at[i], sib).wait_recv()
-
-            for a in steps:
-
-                @pl.when((j == 0) & (x == a))
-                def _():
-                    for d in steps:
-                        weight_copy(a, d).start()
-                    weight_own(a).start()
 
             return carry
 
@@ -823,7 +830,16 @@
                 remote(v_ref, vo_ref.at[y - d, 1 - k], cs.at[d], cr.at[d], sib).wait_recv()
 
             block(y - d, lax.rem(k + j, 2), False)
+
+            @pl.when(i == jnp.minimum(2, 2 * y - 1))
+            def _():
+                move_on()
+
             return carry
+
+        @pl.when(y == 0)
+        def _():
+            move_on()
 
         lax.fori_loop(0, 2 * y, earlier, 0)
         for head in range(3):
@@ -856,9 +872,18 @@
             def _():
                 weight_own(a).wait()
 
-            @pl.when(x != a)
-            def _():
-                weight_copy(a, 1).wait_recv()
+            @pl.when(x == (a + 1) % 4)
+            def _():
+                direct(a, 1, 1).wait_recv()
+
+            @pl.when(x == (a + 3) % 4)
+            def _():
+                direct(a, 0, 1).wait_recv()
+
+            @pl.when(x == (a + 2) % 4)
+            def _():
+                direct(a, 0, 1).wait_recv()
+                direct(a, 1, 1).wait_recv()
 
         c = remote(oo_ref.at[k], oo_ref.at[k], os.at[0], orr.at[0], sib)
         c.start()
@@ -889,8 +914,16 @@
 
             @pl.when(x == a)
             def _():
-                for d in steps:
-                    weight_copy(a, d).wait_send()
+                for half_at, d in ((0, 1), (1, 3), (1, 1), (0, 3)):
+                    direct(a, half_at, d).wait_send()
+
+            @pl.when(x == (a + 1) % 4)
+            def _():
+                onward(a, 0, 1).wait_send()
+
+            @pl.when(x == (a + 3) % 4)
+            def _():
+                onward(a, 1, 3).wait_send()
 
         @pl.when((x == 3) & (k == z // 2))
         def _():
@@ -935,7 +968,7 @@
         ],
         0,
         (4,) * 8 + (16,) * 4 + (4, 2) + (4,) * 8
-        + (4, 4, 4, 4, 4, 4, 4, 4, 4, 4, 1, 1, 4, 4, 4, 4, 3),
+        + (4, 4, 4, 4, 4, 4, 4, 4, 8, 8, 4, 1, 1, 4, 4, 4, 4, 3),
         (w_qkv, w_fc, w_out, w_proj, vectors, tokens, cotangent),
         scratch=[
             pltpu.VMEM((16, wide_q), F32),
@@ -975,37 +1008,23 @@
         q_ref, b_ref, w_ref, kv_ref, ot_ref, lse_ref, f_ref, p_ref, base_ref, res_ref,
         dq_ref, dkv_ref, fo_ref, po_ref, out_ref,
         qt, gt, qm, gm, delta, dqt, out_buf, keep, got, far, f_far, p_far, r_far,
-        cs, cr, ys, yr, fs, fr, ps, pr, rs, rr,
+        f_sum, p_sum, f_all, p_all,
+        cs, cr, ys, yr, fs, fr, ps, pr, rs, rr, s4, r4, s6, r6,
     ):
         y, z, k, x = coords()
         sib = device(y, z, 1 - k, x)
         steps = (1, 2, 3)
-        greet(
+        me = y * 4 + z
+        everyone = greet(
             [sib]
-            + [device(ring(y, d), z, k, x) for d in steps]
-            + [device(y, ring(z, d), k, x) for d in steps]
             + [device(y, z, k, ring(x, d)) for d in steps]
+            + [
+                device(ring(y, a), ring(z, b), k, x)
+                for a in range(4)
+                for b in range(4)
+                if (a, b) != (0, 0)
+            ]
         )
-        results = []
-        for d in steps:
-            b = ring(z, d)
-            c = remote(
-                res_ref.at[b], r_far.at[d - 1], rs.at[d - 1], rr.at[d - 1], device(y, b, k, x)
-            )
-            c.start()
-            results.append(c)
-        weights = []
-        for d in steps:
-            b = ring(x, d)
-            to = device(y, z, k, b)
-            weights.append(
-                remote(f_ref.at[:, b], f_far.at[d - 1], fs.at[d - 1], fr.at[d - 1], to)
-            )
-            weights.append(
-                remote(p_ref.at[:, b], p_far.at[d - 1], ps.at[d - 1], pr.at[d - 1], to)
-            )
-        for c in weights:
-            c.start()
         query_blk = q_ref[...]
         q_t = query_blk.T
         for head in range(3):
@@ -1028,6 +1047,27 @@
             gm[head] = head_cols(grad_blk, head)
             delta[head : head + 1] = jnp.sum(g_t[at].astype(F32) * ot_ref[at], 0, keepdims=True)
 
+        everyone()
+        results = []
+        for d in steps:
+            b = ring(z, d)
+            c = remote(
+                res_ref.at[b], r_far.at[d - 1], rs.at[d - 1], rr.at[d - 1], device(y, b, k, x)
+            )
+            c.start()
+            results.append(c)
+        weights = []
+        for d in steps:
+            b = ring(x, d)
+            to = device(y, z, k, b)
+            weights.append(
+                remote(f_ref.at[:, b], f_far.at[d - 1], fs.at[d - 1], fr.at[d - 1], to)
+            )
+            weights.append(
+                remote(p_ref.at[:, b], p_far.at[d - 1], ps.at[d - 1], pr.at[d - 1], to)
+            )
+        for c in weights:
+            c.start()
         def block(by, bk, masked, to_ref, to):
             keys = kv_ref[by, bk, :, :192]
             values = kv_ref[by, bk, :, 192:]
@@ -1072,23 +1112,57 @@
         lax.fori_loop(0, y, earlier, 0)
         block(y, 1 - k, True, out_buf, 0)
         cross(0).start()
-        block(y, k, True, keep, 0)
-        dq_ref[...] = (dqt[...].T * 0.125).astype(BF)
-        cross(0).wait_recv()
+
         for c in weights:
             c.wait()
-        fo_ref[...] = (
+        f_sum[...] = (
             f_ref[:, x].astype(F32)
             + f_far[0].astype(F32)
             + f_far[1].astype(F32)
             + f_far[2].astype(F32)
         ).astype(BF)
-        po_ref[...] = (
+        p_sum[...] = (
             p_ref[:, x].astype(F32)
             + p_far[0].astype(F32)
             + p_far[1].astype(F32)
             + p_far[2].astype(F32)
         ).astype(BF)
+
+        def f_copy(a):
+            return remote(
+                f_sum.at[a], f_all.at[me], s4.at[a], r4.at[me], device(a, x, k, x)
+            )
+
+        def p_copy(j):
+            return remote(
+                p_sum.at[j], p_all.at[y], s6.at[j], r6.at[y], device(z, 2 * k + j, k, x)
+            )
+
+        f_here = [(a == y) & (z == x) for a in range(4)]
+        p_here = [(y == z) & (z == 2 * k + j) for j in range(2)]
+        for a in range(4):
+
+            @pl.when(jnp.logical_not(f_here[a]))
+            def _():
+                f_copy(a).start()
+
+            @pl.when(f_here[a])
+            def _():
+                f_all[me] = f_sum[a]
+
+        for j in range(2):
+
+            @pl.when(jnp.logical_not(p_here[j]))
+            def _():
+                p_copy(j).start()
+
+            @pl.when(p_here[j])
+            def _():
+                p_all[y] = p_sum[j]
+
+        block(y, k, True, keep, 0)
+        dq_ref[...] = (dqt[...].T * 0.125).astype(BF)
+        cross(0).wait_recv()
         for c in results:
             c.wait()
         out_ref[...] = (
@@ -1106,6 +1180,51 @@
                 remote(keep.at[d], far.at[d], ys.at[d], yr.at[d], sib).wait_recv()
                 dkv_ref[...] += far[d].astype(F32)
 
+        @pl.when(z == x)
+        def _():
+            def arrive(i, carry):
+                @pl.when(i != me)
+                def _():
+                    remote(f_sum.at[0], f_all.at[i], s4.at[0], r4.at[i], sib).wait_recv()
+
+                return carry
+
+            lax.fori_loop(0, 16, arrive, 0)
+            for b in range(4):
+                fo_ref[:, 384 * b : 384 * b + 384] = (
+                    f_all[b].astype(F32)
+                    + f_all[4 + b].astype(F32)
+                    + f_all[8 + b].astype(F32)
+                    + f_all[12 + b].astype(F32)
+                )
+
+        for a in range(4):
+
+            @pl.when((k == z // 2) & jnp.logical_not((a == y) & (z == y)))
+            def _():
+                remote(p_sum.at[0], p_all.at[a], s6.at[0], r6.at[a], sib).wait_recv()
+
+        @pl.when(k == z // 2)
+        def _():
+            po_ref[...] = (
+                p_all[0].astype(F32)
+                + p_all[1].astype(F32)
+                + p_all[2].astype(F32)
+                + p_all[3].astype(F32)
+            )
+
+        for a in range(4):
+
+            @pl.when(jnp.logical_not(f_here[a]))
+            def _():
+                f_copy(a).wait_send()
+
+        for j in range(2):
+
+            @pl.when(jnp.logical_not(p_here[j]))
+            def _():
+                p_copy(j).wait_send()
+
         cross(0).wait_send()
         for d in (1, 2, 3):
 
@@ -1119,12 +1238,12 @@
         [
             jax.ShapeDtypeStruct((512, 192), BF),
             jax.ShapeDtypeStruct((512, 384), F32),
-            jax.ShapeDtypeStruct((4, 48, 384), BF),
-            jax.ShapeDtypeStruct((2, 48, 768), BF),
+            jax.ShapeDtypeStruct((48, 1536), F32),
+            jax.ShapeDtypeStruct((48, 768), F32),
             jax.ShapeDtypeStruct((128, 768), F32),
         ],
         5,
-        (4, 4, 4, 4, 3, 3, 3, 3, 3, 3),
+        (4, 4, 4, 4, 3, 3, 3, 3, 3, 3, 4, 16, 2, 4),
         (query, branch, wo, kv_all, out_t, lse, fc, proj, base, result),
         scratch=[
             pltpu.VMEM((3, 192, 512), BF),
@@ -1140,6 +1259,10 @@
             pltpu.VMEM((3, 4, 48, 384), BF),
             pltpu.VMEM((3, 2, 48, 768), BF),
             pltpu.VMEM((3, 128, 768), BF),
+            pltpu.VMEM((4, 48, 384), BF),
+            pltpu.VMEM((2, 48, 768), BF),
+            pltpu.VMEM((16, 48, 384), BF),
+            pltpu.VMEM((4, 48, 768), BF),
         ],
         spaces=([VMEM] * 10, [VMEM] * 5),
         name="attend_back",
@@ -1172,14 +1295,14 @@
         y, z, k, x = coords()
         sib = device(y, z, 1 - k, x)
         steps = (1, 2, 3)
-        greet([sib] + [device(y, ring(z, d), k, x) for d in steps])
+        everyone = greet([sib] + [device(y, ring(z, d), k, x) for d in steps])
         out_bias, gain, shift, proj_bias = (v_ref[i : i + 1] for i in range(4, 8))
         fc_bias = jnp.zeros((1, 384), F32)
         for b in range(4):
             row = v_ref[8 + b : 9 + b, pl.ds(pl.multiple_of(384 * k, 128), 384)]
             fc_bias = fc_bias + jnp.where(z == b, row, 0.0)
 
-        def half(kk, norm_ref, res_ref):
+        def half(kk, norm_ref):
             two = x_ref[kk].reshape(512, 768).astype(F32) + out_bias
             for g in range(4):
                 h = h_ref[g, kk]
@@ -1210,21 +1333,19 @@
                 df_blk, wf_ref[...], (((1,), (1,)), ((), ())), preferred_element_type=F32
             )
             norm_ref[...] = norm_part.astype(BF).reshape(4, 128, 768)
-            res_ref[...] = dot(act_blk, wp_ref[...]).astype(BF).reshape(4, 128, 768)
-
-        half(1 - k, norm_other, res_other)
+
+        def result(kk, res_ref):
+            res_ref[...] = dot(act[kk], wp_ref[...]).astype(BF).reshape(4, 128, 768)
+
+        half(1 - k, norm_other)
+        everyone()
         swaps = []
         for d in (1, 2, 3, 0):
             b = ring(z, d)
             c = remote(norm_other.at[b], norm_got.at[b], cs.at[d], cr.at[d], sib)
             c.start()
             swaps.append(c)
-        for d in (1, 2, 3, 0):
-            b = ring(z, d)
-            c = remote(res_other.at[b], res_got.at[b], es.at[d], er.at[d], sib)
-            c.start()
-            swaps.append(c)
-        half(k, norm_mine, res_mine)
+        half(k, norm_mine)
         sends = []
         for d in steps:
             b = ring(z, d)
@@ -1236,6 +1357,12 @@
             )
             c.start()
             sends.append(c)
+        result(1 - k, res_other)
+        for d in (1, 2, 3, 0):
+            b = ring(z, d)
+            c = remote(res_other.at[b], res_got.at[b], es.at[d], er.at[d], sib)
+            c.start()
+            swaps.append(c)
         tn = (((0,), (0,)), ((), ()))
         gwf = lax.dot_general(a2[0], df[0], tn, preferred_element_type=F32)
         gwf += lax.dot_general(a2[1], df[1], tn, preferred_element_type=F32)
@@ -1265,6 +1392,7 @@
             )
             c.start()
             branches.append(c)
+        result(k, res_mine)
         gwp = lax.dot_general(
             act[0], dy_ref[0].reshape(512, 768), tn, preferred_element_type=F32
         )
@@ -1379,7 +1507,7 @@
         base,
         result,
     )
-    grad_one, last_rows, proj_rows = last_sums(
+    grad_one, last_rows, proj_rows, fc_rows = last_sums(
         (
             act_one,
             normed_core,
@@ -1395,7 +1523,7 @@
         proj_sum,
     )
     output, grad_inputs, *new_state = finish(
-        grad_one, grad_x_two, tokens[0], vec_rows, last_rows, proj_rows, result_sum, state
+        grad_one, grad_x_two, tokens[0], vec_rows, last_rows, proj_rows, fc_rows, result_sum, state
     )
     return (output[None], grad_inputs[None], *new_state)
 

time: 203 us -> 196 us (0.966)
  Pallas kernels: 202 us -> 194 us
    pallas_call x4, Pallas kernels: 199 us -> 191 us  [comm(): pl.pallas_call(kernel, out_shape=outs, in_specs=[ANY] * len(args) if spac...]
where the time goes in v6:
time: 196 us; the launch traced here: 195 us
  Pallas kernels  194 us (99%)
    pallas_call x4, Pallas kernels, comm(): pl.pallas_call(kernel, out_shape=outs, in_specs=[ANY] * len(args) if spac...  191 us

profile of v6, /device:TPU:29, one launch (start us, length us, event | category | flops | bytes accessed | tf_op | source)
XLA Modules:
  0.0 194.9 jit_solution(2864670325037060512)
XLA Ops:
  0.7 75.8 %forward.1 = (bf16[4,2,512,192]{3,2,1,0:T(8,128)(2,1)}, f32[192,512]{1,0:T(8,128)}, f32[8,512]{1,0:T(8,128)}, bf16[4,2,512,384]{3,2,1,0:T(8,128)(2,1)}, bf16[2,4...) custom-call(f32[6,2304]{1,0:T(8,128)} %refs_8_.1, ...), custom_call_target="tpu_custom_call" | custom-call | tf_op jit(solution)/shard_map/forward/pallas_call | solution.py:48
  76.4 33.8 %feed_forward.1 = (f32[128,768]{1,0:T(8,128)}, bf16[4,128,768]{2,1,0:T(8,128)(2,1)}, f32[128,768]{1,0:T(8,128)}, bf16[4,128,768]{2,1,0:T(8,128)(2,1)}, bf16[768,...) custom-call(bf16[4,2,512,192]{3,2,1,0:T(8,128)(2,1)} %get-tuple-element.67.h_ref.refs_2_, ...), custom_call_target="tpu_custom_call" | custom-call | tf_op jit(solution)/shard_map/feed_forward/pallas_call | solution.py:48
  110.3 37.8 %attend_back.1 = (bf16[512,192]{1,0:T(8,128)(2,1)}, f32[512,384]{1,0:T(8,128)}, f32[48,1536]{1,0:T(8,128)}, f32[48,768]{1,0:T(8,128)}, f32[128,768]{1,0:T(8,128)}) custom-call(bf16[512,192]{1,0:T(8,128)(2,1)} %get-tuple-element.68.q_ref, bf16[512,768]{1,0:T(8,128)(2,1)} %bitcast.13, bf16[2,768,384]{2,1,0:T(8,128)(2,1)} %bitcast.12, ...), custom_call_target="tpu_custom_call" | custom-call | tf_op jit(solution)/shard_map/attend_back/pallas_call | solution.py:48
  148.0 43.4 %last_sums.1 = (f32[128,768]{1,0:T(8,128)}, f32[2,8,1664]{2,1,0:T(8,128)}, f32[24,768]{1,0:T(8,128)}, f32[2,8,1536]{2,1,0:T(8,128)}) custom-call(bf16[512,768]{1,0:T(8,128)(2,1)} %get-tuple-element.65.refs_0_, bf16[512,768]{1,0:T(8,128)(2,1)} %get-tuple-element.66.refs_1_, bf16[4,2,512,192]{3,2,1,0:T(8,128)(2,1)} %get-tuple-element.67.h_ref.refs_2_, ...), custom_call_target="tpu_custom_call" | custom-call | tf_op jit(solution)/shard_map/last_sums/pallas_call | solution.py:48
  191.4 3.3 %finish.1 = (f32[128,768]{1,0:T(8,128)}, f32[128,768]{1,0:T(8,128)}, f32[6,2304]{1,0:T(8,128)}, f32[6,2304]{1,0:T(8,128)}, f32[6,2304]{1,0:T(8,128)}, /*index=5*...) custom-call(f32[128,768]{1,0:T(8,128)} %get-tuple-element.90.refs_0_, ...), custom_call_target="tpu_custom_call" | custom-call | tf_op jit(solution)/shard_map/finish/pallas_call | solution.py:416

commit v7 on v6

--- a/solution.py
+++ b/solution.py
@@ -68,14 +68,13 @@
         ) = refs[:11]
         one_out, rows_out, proj_out, fc_out = refs[11:15]
         (
-            one_far, mix_got, mix_sum, mix_far, vec_far, mix_mine, vec_mine,
-            mix_all, vec_all, proj_sum, out_send, fc_send,
+            one_far, mix_got, mix_sum, mix_all, vec_all, proj_sum, out_send, fc_send,
             one_ref, mix_other, mix_ref, vec_ref,
             act_t, heads, heads_t, d_ref, right_one, right_two, vec_rows,
-        ) = refs[15:38]
+        ) = refs[15:34]
         (
-        zs, zr, cs, cr, s1, r1, s2, r2, s3, r3, s4, r4, s5, r5, s7, r7, s8, r8, loc,
-        ) = refs[38:]
+        zs, zr, cs, cr, s3, r3, s4, r4, s5, r5, s7, r7, s8, r8, loc,
+        ) = refs[34:]
         y, z, k, x = coords()
         me = y * 4 + z
         sib = device(y, z, 1 - k, x)
@@ -124,8 +123,8 @@
         everyone()
         swap = []
         for d in (1, 2, 3, 0):
-            b = ring(x, d)
-            c = remote(mix_other.at[:, b], mix_got.at[b], cs.at[d], cr.at[d], sib)
+            b = ring(y, d)
+            c = remote(mix_other.at[b], mix_got.at[b], cs.at[d], cr.at[d], sib)
             c.start()
             swap.append(c)
         def proj_last(i):
@@ -182,18 +181,6 @@
         vec_rows[0:1] = jnp.sum(one * n_ref[...].astype(F32), 0, keepdims=True)
         vec_rows[1:2] = jnp.sum(one, 0, keepdims=True)
         vec_ref[...] = vec_rows[...].T.astype(BF).reshape(4, 4, 48, 128)
-        along = []
-        for d in steps:
-            b = ring(x, d)
-            to = device(y, z, k, b)
-            swap[d - 1].wait_recv()
-            mix_sum[d] = (mix_ref[:, b].astype(F32) + mix_got[b].astype(F32)).astype(BF)
-            c = remote(mix_sum.at[d], mix_far.at[d - 1], s1.at[d - 1], r1.at[d - 1], to)
-            c.start()
-            along.append(c)
-            c = remote(vec_ref.at[:, b], vec_far.at[d - 1], s2.at[d - 1], r2.at[d - 1], to)
-            c.start()
-            along.append(c)
         ones = []
         for d in steps:
             c = remote(
@@ -203,58 +190,35 @@
             c.start()
             ones.append(c)
 
-        def plane(src, dst, send, recv, a):
-            return remote(src.at[a], dst.at[me], send.at[a], recv.at[me], device(a, x, k, x))
-
-        def all_start(src, dst, send, recv):
-            for a in range(4):
-                here = (a == y) & (z == x)
-
-                @pl.when(jnp.logical_not(here))
-                def _():
-                    plane(src, dst, send, recv, a).start()
-
-                @pl.when(here)
-                def _():
-                    c = pltpu.make_async_copy(src.at[a], dst.at[me], loc.at[0])
-                    c.start()
-                    c.wait()
-
-        def all_finish(src, dst, send, recv):
-            for a in range(4):
-
-                @pl.when(jnp.logical_not((a == y) & (z == x)))
-                def _():
-                    plane(src, dst, send, recv, a).wait_send()
-
-        def all_receive(src, dst, send, recv):
-            def step(i, carry):
-                @pl.when(i != me)
-                def _():
-                    remote(src.at[0], dst.at[i], send.at[0], recv.at[i], sib).wait_recv()
-
+        def plane(src, dst, send, recv, m):
+            ty, tz = ring(y, m // 4), ring(z, m % 4)
+            return remote(
+                src.at[ty, tz], dst.at[me], send.at[m], recv.at[m], device(ty, tz, k, x)
+            )
+
+        def vec_copy(m):
+            return plane(vec_ref, vec_all, s5, r5, m)
+
+        def mix_copy(m):
+            return plane(mix_sum, mix_all, s3, r3, m)
+
+        def each(copy, what, first, last):
+            def step(m, carry):
+                what(copy(m))
                 return carry
 
-            lax.fori_loop(0, 16, step, 0)
-
-        swap[3].wait_recv()
-        for c in along:
-            c.wait_recv()
-        mix_mine[...] = (
-            mix_ref[:, x].astype(F32)
-            + mix_got[x].astype(F32)
-            + mix_far[0].astype(F32)
-            + mix_far[1].astype(F32)
-            + mix_far[2].astype(F32)
-        ).astype(BF)
-        vec_mine[...] = (
-            vec_ref[:, x].astype(F32)
-            + vec_far[0].astype(F32)
-            + vec_far[1].astype(F32)
-            + vec_far[2].astype(F32)
-        ).astype(BF)
-        all_start(mix_mine, mix_all, s3, r3)
-        all_start(vec_mine, vec_all, s5, r5)
+            lax.fori_loop(first, last, step, 0)
+
+        start = lambda c: c.start()
+        finish_all = lambda c: c.wait()
+        each(vec_copy, start, 1, 16)
+        vec_all[me] = vec_ref[y, z]
+        for d in (1, 2, 3, 0):
+            b = ring(y, d)
+            swap[d - 1].wait_recv()
+            mix_sum[b] = (mix_ref[b].astype(F32) + mix_got[b].astype(F32)).astype(BF)
+            each(mix_copy, start, max(4 * d, 1), 4 * d + 4)
+        mix_all[me] = mix_sum[y, z]
         for c in ones:
             c.wait_recv()
         one_out[...] = (
@@ -266,49 +230,51 @@
 
         def last_copy(i):
             return remote(
-                out_send.at[i], rows_out.at[k], s7.at[i], r7.at[k], device(y, z, i // 4, i % 4)
-            )
-
-        @pl.when(z == x)
-        def _():
-            all_receive(mix_mine, mix_all, s3, r3)
-            all_receive(vec_mine, vec_all, s5, r5)
-
-            def four(ref, b):
-                return (
-                    ref[b].astype(F32)
-                    + ref[4 + b].astype(F32)
-                    + ref[8 + b].astype(F32)
-                    + ref[12 + b].astype(F32)
-                )
-
-            for b in range(4):
-                m = four(mix_all, b)
-                for i in range(8):
-                    rows = slice(6 * i, 6 * i + 6)
-                    out_send[i, 0:6, 384 * b : 384 * b + 384] = m[rows]
-            v = four(vec_all, 0) + four(vec_all, 1) + four(vec_all, 2) + four(vec_all, 3)
+                out_send.at[i], rows_out.at[k * 4 + x], s7.at[i], r7.at[k * 4 + x],
+                device(y, z, i // 4, i % 4),
+            )
+
+        each(vec_copy, finish_all, 1, 16)
+        each(mix_copy, finish_all, 1, 16)
+
+        def four(ref, b):
+            return (
+                ref[b].astype(F32)
+                + ref[4 + b].astype(F32)
+                + ref[8 + b].astype(F32)
+                + ref[12 + b].astype(F32)
+            )
+
+        for b in range(4):
+            m = four(mix_all, b)
             for i in range(8):
-                out_send[i, 0:6, 1536:1664] = v[6 * i : 6 * i + 6]
-                out_send[i, 6:8, :] = jnp.zeros((2, wide), F32)
-            for i in range(8):
-
-                @pl.when(jnp.logical_not(last_here(i)))
-                def _():
-                    last_copy(i).start()
-
-                @pl.when(last_here(i))
-                def _():
-                    c = pltpu.make_async_copy(out_send.at[i], rows_out.at[k], loc.at[3])
-                    c.start()
-                    c.wait()
+                out_send[i, 0:6, 384 * b : 384 * b + 384] = m[6 * i : 6 * i + 6]
+        v = four(vec_all, 0) + four(vec_all, 1) + four(vec_all, 2) + four(vec_all, 3)
+        for i in range(8):
+            out_send[i, 0:6, 1536:1664] = v[6 * i : 6 * i + 6]
+            out_send[i, 6:8, :] = jnp.zeros((2, wide), F32)
+        for i in range(8):
+
+            @pl.when(jnp.logical_not(last_here(i)))
+            def _():
+                last_copy(i).start()
+
+            @pl.when(last_here(i))
+            def _():
+                rows_out[i] = out_send[i]
 
         for j in range(2):
 
             @pl.when(jnp.logical_not((z == x) & (k == j)))
             def _():
-                remote(out_send.at[0], rows_out.at[j], s7.at[0], r7.at[j], sib).wait_recv()
                 remote(fc_send.at[0], fc_out.at[j], s4.at[0], r4.at[j], sib).wait_recv()
+
+        for i in range(8):
+
+            @pl.when(jnp.logical_not(last_here(i)))
+            def _():
+                remote(out_send.at[0], rows_out.at[i], s7.at[0], r7.at[i], sib).wait_recv()
+                last_copy(i).wait_send()
 
         @pl.when(jnp.logical_not((k == z // 2) & (x == (4 * k + x) // 2)))
         def _():
@@ -320,7 +286,6 @@
 
                 @pl.when(jnp.logical_not(last_here(i)))
                 def _():
-                    last_copy(i).wait_send()
                     fc_last(i).wait_send()
 
         for i in range(2):
@@ -329,30 +294,24 @@
             def _():
                 proj_last(i).wait_send()
 
-        all_finish(mix_mine, mix_all, s3, r3)
-        all_finish(vec_mine, vec_all, s5, r5)
-        for c in swap + along + ones:
+        for c in swap + ones:
             c.wait_send()
 
     return comm(
         kernel,
         [
             jax.ShapeDtypeStruct((128, 768), F32),
-            jax.ShapeDtypeStruct((2, 8, wide), F32),
+            jax.ShapeDtypeStruct((8, 8, wide), F32),
             jax.ShapeDtypeStruct((24, 768), F32),
             jax.ShapeDtypeStruct((2, 8, 1536), F32),
         ],
         6,
-        (3, 3, 4, 4, 3, 3, 3, 3, 4, 16, 8, 2, 4, 16, 8, 2, 2, 1, 4),
+        (3, 3, 4, 4, 16, 16, 8, 2, 16, 16, 8, 8, 2, 1, 4),
         (*pieces, fc, proj),
         scratch=[
             pltpu.VMEM((3, 128, 768), BF),
             pltpu.VMEM((4, 4, 48, 384), BF),
             pltpu.VMEM((4, 4, 48, 384), BF),
-            pltpu.VMEM((3, 4, 48, 384), BF),
-            pltpu.VMEM((3, 4, 48, 128), BF),
-            pltpu.VMEM((4, 48, 384), BF),
-            pltpu.VMEM((4, 48, 128), BF),
             pltpu.VMEM((16, 48, 384), BF),
             pltpu.VMEM((16, 48, 128), BF),
             pltpu.VMEM((2, 24, 768), F32),
@@ -386,8 +345,9 @@
         normed, inverse = normalize(t_ref[...].astype(F32))
         gin_ref[...] = gx_ref[...] + normalize_back(normed, inverse, v_ref[0:1], one_ref[...])
         for b in range(4):
-            one_half = rows_ref[0, 0:6, 384 * b : 384 * b + 384]
-            two_half = rows_ref[1, 0:6, 384 * b : 384 * b + 384]
+            at_z = slice(384 * b, 384 * b + 384)
+            one_half = jnp.sum(rows_ref[0:4, 0:6, at_z], 0)
+            two_half = jnp.sum(rows_ref[4:8, 0:6, at_z], 0)
             q = 192 * b
             g_qkv[:, q : q + 192] = one_half[:, 0:192]
             g_qkv[:, 768 + q : 864 + q] = one_half[:, 192:288]
@@ -398,7 +358,7 @@
             for j in range(2):
                 at = 384 * (2 * b + j)
                 g_fc[:, at : at + 384] = f_ref[j, 0:6, 384 * b : 384 * b + 384]
-        g_vec = rows_ref[0, 0:6, 1536:1548] + rows_ref[1, 0:6, 1536:1548]
+        g_vec = jnp.sum(rows_ref[:, 0:6, 1536:1548], 0)
         for i, (gradient, rate, decay) in enumerate(
             (
                 (g_qkv[...], 0.1, 0.1),
@@ -583,6 +543,24 @@
             each(q_copy, start)
             q_out[me, group] = q_send[z, group]
 
+        half = pl.ds(8 * k, 8)
+        other_half = pl.ds(8 * (1 - k), 8)
+
+        def rows_of(plane):
+            return pl.ds(pl.multiple_of(16 * plane, 16), 16)
+
+        def x_copy(d):
+            return remote(
+                q_out.at[half, group], q_out.at[half, group], xs_s.at[d], xs_r.at[x],
+                device(y, z, k, ring(x, d)),
+            )
+
+        @pl.when(x < 3)
+        def _():
+            each(q_copy, finish)
+            for d in steps:
+                x_copy(d).start()
+
         cross_r = crossing(packed_r, got_r, message_r, fr_s, fr_r)
         for c in cross_r:
             c.wait_recv()
@@ -599,24 +577,6 @@
         o_send[0] = out48[:, 0:384].astype(BF)
         o_send[1] = out48[:, 384:768].astype(BF)
         p_send[...] = proj_wide[...].astype(BF)
-
-        half = pl.ds(8 * k, 8)
-        other_half = pl.ds(8 * (1 - k), 8)
-
-        def rows_of(plane):
-            return pl.ds(pl.multiple_of(16 * plane, 16), 16)
-
-        def x_copy(d):
-            return remote(
-                q_out.at[half, group], q_out.at[half, group], xs_s.at[d], xs_r.at[x],
-                device(y, z, k, ring(x, d)),
-            )
-
-        @pl.when(x < 3)
-        def _():
-            each(q_copy, finish)
-            for d in steps:
-                x_copy(d).start()
 
         @pl.when(x == 1)
         def _():

time: 196 us -> 196 us (level)
  no operation moved by 1% of the time
where the time goes in v7:
time: 196 us; the launch traced here: 194 us
  Pallas kernels  193 us (98%)
    pallas_call x4, Pallas kernels, comm(): pl.pallas_call(kernel, out_shape=outs, in_specs=[ANY] * len(args) if spac...  190 us

profile of v7, /device:TPU:29, one launch (start us, length us, event | category | flops | bytes accessed | tf_op | source)
XLA Modules:
  0.0 194.3 jit_solution(6057371276444359125)
XLA Ops:
  0.7 77.3 %forward.1 = (bf16[4,2,512,192]{3,2,1,0:T(8,128)(2,1)}, f32[192,512]{1,0:T(8,128)}, f32[8,512]{1,0:T(8,128)}, bf16[4,2,512,384]{3,2,1,0:T(8,128)(2,1)}, bf16[2,4...) custom-call(f32[6,2304]{1,0:T(8,128)} %refs_8_.1, ...), custom_call_target="tpu_custom_call" | custom-call | tf_op jit(solution)/shard_map/forward/pallas_call | solution.py:48
  78.0 33.8 %feed_forward.1 = (f32[128,768]{1,0:T(8,128)}, bf16[4,128,768]{2,1,0:T(8,128)(2,1)}, f32[128,768]{1,0:T(8,128)}, bf16[4,128,768]{2,1,0:T(8,128)(2,1)}, bf16[768,...) custom-call(bf16[4,2,512,192]{3,2,1,0:T(8,128)(2,1)} %get-tuple-element.67.h_ref.refs_2_, ...), custom_call_target="tpu_custom_call" | custom-call | tf_op jit(solution)/shard_map/feed_forward/pallas_call | solution.py:48
  111.8 37.1 %attend_back.1 = (bf16[512,192]{1,0:T(8,128)(2,1)}, f32[512,384]{1,0:T(8,128)}, f32[48,1536]{1,0:T(8,128)}, f32[48,768]{1,0:T(8,128)}, f32[128,768]{1,0:T(8,128)}) custom-call(bf16[512,192]{1,0:T(8,128)(2,1)} %get-tuple-element.68.q_ref, bf16[512,768]{1,0:T(8,128)(2,1)} %bitcast.13, bf16[2,768,384]{2,1,0:T(8,128)(2,1)} %bitcast.12, ...), custom_call_target="tpu_custom_call" | custom-call | tf_op jit(solution)/shard_map/attend_back/pallas_call | solution.py:48
  148.9 41.9 %last_sums.1 = (f32[128,768]{1,0:T(8,128)}, f32[8,8,1664]{2,1,0:T(8,128)}, f32[24,768]{1,0:T(8,128)}, f32[2,8,1536]{2,1,0:T(8,128)}) custom-call(bf16[512,768]{1,0:T(8,128)(2,1)} %get-tuple-element.65.refs_0_, bf16[512,768]{1,0:T(8,128)(2,1)} %get-tuple-element.66.refs_1_, bf16[4,2,512,192]{3,2,1,0:T(8,128)(2,1)} %get-tuple-element.67.h_ref.refs_2_, ...), custom_call_target="tpu_custom_call" | custom-call | tf_op jit(solution)/shard_map/last_sums/pallas_call | solution.py:48
  190.8 3.3 %finish.1 = (f32[128,768]{1,0:T(8,128)}, f32[128,768]{1,0:T(8,128)}, f32[6,2304]{1,0:T(8,128)}, f32[6,2304]{1,0:T(8,128)}, f32[6,2304]{1,0:T(8,128)}, /*index=5*...) custom-call(f32[128,768]{1,0:T(8,128)} %get-tuple-element.90.refs_0_, ...), custom_call_target="tpu_custom_call" | custom-call | tf_op jit(solution)/shard_map/finish/pallas_call | solution.py:376

commit v8 on v7

--- a/solution.py
+++ b/solution.py
@@ -963,21 +963,385 @@
     )
 
 
-def attend_back(query, branch, wo, kv_all, out_t, lse, fc, proj, base, result):
-    def kernel(
-        q_ref, b_ref, w_ref, kv_ref, ot_ref, lse_ref, f_ref, p_ref, base_ref, res_ref,
-        dq_ref, dkv_ref, fo_ref, po_ref, out_ref,
-        qt, gt, qm, gm, delta, dqt, out_buf, keep, got, far, f_far, p_far, r_far,
-        f_sum, p_sum, f_all, p_all,
-        cs, cr, ys, yr, fs, fr, ps, pr, rs, rr, s4, r4, s6, r6,
-    ):
+def normalize(rows):
+    centered = rows - jnp.mean(rows, -1, keepdims=True)
+    inverse = lax.rsqrt(jnp.mean(centered * centered, -1, keepdims=True) + EPSILON)
+    return centered * inverse, inverse
+
+
+def normalize_back(normed, inverse, gain, grad):
+    scaled = grad * gain
+    return inverse * (
+        scaled
+        - jnp.mean(scaled, -1, keepdims=True)
+        - normed * jnp.mean(scaled * normed, -1, keepdims=True)
+    )
+
+
+def feed_body(
+    h_ref, x_ref, dy_ref, wo_ref, wf_ref, wp_ref, v_ref,
+    base_ref, res_mine, gx_ref, bo_ref, gwf_ref, gwp_ref, gfb_ref, gv_ref,
+    a2, act, df, x_two, normed, inverse, norm_other, norm_mine, res_other,
+    norm_got, res_got, norm_far, branch,
+    cs, cr, es, er, zs, zr, bs, br, everyone,
+):
+    y, z, k, x = coords()
+    sib = device(y, z, 1 - k, x)
+    steps = (1, 2, 3)
+    out_bias, gain, shift, proj_bias = (v_ref[i : i + 1] for i in range(4, 8))
+    fc_bias = jnp.zeros((1, 384), F32)
+    for b in range(4):
+        row = v_ref[8 + b : 9 + b, pl.ds(pl.multiple_of(384 * k, 128), 384)]
+        fc_bias = fc_bias + jnp.where(z == b, row, 0.0)
+
+    def half(kk, norm_ref):
+        two = x_ref[kk].reshape(512, 768).astype(F32) + out_bias
+        for g in range(4):
+            h = h_ref[g, kk]
+            at = slice(192 * g, 192 * g + 192)
+            part = jnp.concatenate([dot(h, wo_ref[0, at]), dot(h, wo_ref[1, at])], 1)
+            two = two + part
+        x_two[...] = two
+        n, inv = normalize(two)
+        normed[...] = n
+        inverse[...] = jnp.broadcast_to(inv, (512, 128))
+        a = (n * gain + shift).astype(BF)
+        a2[kk] = a
+        hidden = dot(a, wf_ref[...]) + fc_bias
+        square = hidden * hidden
+        t = jnp.tanh(0.7978845608028654 * (hidden + 0.044715 * square * hidden))
+        act_blk = (0.5 * hidden * (1.0 + t)).astype(BF)
+        act[kk] = act_blk
+        slope = 0.5 * (1.0 + t) + 0.5 * hidden * (1.0 - t * t) * (
+            0.7978845608028654 * (1.0 + 3 * 0.044715 * square)
+        )
+        dy = dy_ref[kk].reshape(512, 768)
+        back = lax.dot_general(
+            dy, wp_ref[...], (((1,), (1,)), ((), ())), preferred_element_type=F32
+        )
+        df_blk = (back * slope).astype(BF)
+        df[kk] = df_blk
+        norm_part = lax.dot_general(
+            df_blk, wf_ref[...], (((1,), (1,)), ((), ())), preferred_element_type=F32
+        )
+        norm_ref[...] = norm_part.astype(BF).reshape(4, 128, 768)
+
+    def result(kk, res_ref):
+        res_ref[...] = dot(act[kk], wp_ref[...]).astype(BF).reshape(4, 128, 768)
+
+    half(1 - k, norm_other)
+    everyone()
+    swaps = []
+    for d in (1, 2, 3, 0):
+        b = ring(z, d)
+        c = remote(norm_other.at[b], norm_got.at[b], cs.at[d], cr.at[d], sib)
+        c.start()
+        swaps.append(c)
+    half(k, norm_mine)
+    sends = []
+    for d in steps:
+        b = ring(z, d)
+        swaps[d - 1].wait_recv()
+        norm_mine[b] = (norm_mine[b].astype(F32) + norm_got[b].astype(F32)).astype(BF)
+        c = remote(
+            norm_mine.at[b], norm_far.at[d - 1], zs.at[d - 1], zr.at[d - 1],
+            device(y, b, k, x),
+        )
+        c.start()
+        sends.append(c)
+    result(1 - k, res_other)
+    for d in (1, 2, 3, 0):
+        b = ring(z, d)
+        c = remote(res_other.at[b], res_got.at[b], es.at[d], er.at[d], sib)
+        c.start()
+        swaps.append(c)
+    tn = (((0,), (0,)), ((), ()))
+    gwf = lax.dot_general(a2[0], df[0], tn, preferred_element_type=F32)
+    gwf += lax.dot_general(a2[1], df[1], tn, preferred_element_type=F32)
+    gwf_ref[...] = gwf.astype(BF).reshape(4, 4, 48, 384)
+    own_rows = pl.ds(pl.multiple_of(128 * z, 128), 128)
+    swaps[3].wait_recv()
+    for c in sends:
+        c.wait_recv()
+    da = (
+        norm_mine[z].astype(F32)
+        + norm_got[z].astype(F32)
+        + norm_far[0].astype(F32)
+        + norm_far[1].astype(F32)
+        + norm_far[2].astype(F32)
+    )
+    n = normed[own_rows]
+    dy = dy_ref[k, z].astype(F32)
+    gx = dy + normalize_back(n, inverse[own_rows, 0:1], gain, da)
+    gx_ref[...] = gx
+    low = gx.astype(BF)
+    branch[...] = low
+    bo_ref[z] = low
+    branches = []
+    for d in steps:
+        c = remote(
+            branch, bo_ref.at[z], bs.at[d - 1], br.at[d - 1], device(y, ring(z, d), k, x)
+        )
+        c.start()
+        branches.append(c)
+    result(k, res_mine)
+    gwp = lax.dot_general(
+        act[0], dy_ref[0].reshape(512, 768), tn, preferred_element_type=F32
+    )
+    gwp += lax.dot_general(
+        act[1], dy_ref[1].reshape(512, 768), tn, preferred_element_type=F32
+    )
+    gwp_ref[...] = gwp.astype(BF).reshape(2, 4, 48, 768)
+    gfb_ref[...] = jnp.sum(df[0].astype(F32), 0, keepdims=True) + jnp.sum(
+        df[1].astype(F32), 0, keepdims=True
+    )
+    gv_ref[0:1] = jnp.sum(low.astype(F32), 0, keepdims=True)
+    gv_ref[1:2] = jnp.sum(da * n, 0, keepdims=True)
+    gv_ref[2:3] = jnp.sum(da, 0, keepdims=True)
+    gv_ref[3:4] = jnp.sum(dy, 0, keepdims=True)
+    for c in swaps[4:]:
+        c.wait_recv()
+    res_mine[...] = (res_mine[...].astype(F32) + res_got[...].astype(F32)).astype(BF)
+    base_ref[...] = x_two[own_rows] + proj_bias
+    for c in branches:
+        c.wait()
+    for c in swaps + sends:
+        c.wait_send()
+
+
+def back_body(
+    q_ref, b_ref, w_ref, kv_ref, ot_ref, lse_ref, f_ref, p_ref, base_ref, res_ref,
+    dq_ref, dkv_ref, fo_ref, po_ref, out_ref,
+    qt, gt, qm, gm, delta, dqt, out_buf, keep, got, far, f_far, p_far, r_far,
+    f_sum, p_sum, f_all, p_all,
+    cs, cr, ys, yr, fs, fr, ps, pr, rs, rr, s4, r4, s6, r6,
+):
+    y, z, k, x = coords()
+    sib = device(y, z, 1 - k, x)
+    steps = (1, 2, 3)
+    me = y * 4 + z
+    results = []
+    for d in steps:
+        b = ring(z, d)
+        c = remote(
+            res_ref.at[b], r_far.at[d - 1], rs.at[d - 1], rr.at[d - 1], device(y, b, k, x)
+        )
+        c.start()
+        results.append(c)
+    weights = []
+    for d in steps:
+        b = ring(x, d)
+        to = device(y, z, k, b)
+        weights.append(
+            remote(f_ref.at[:, b], f_far.at[d - 1], fs.at[d - 1], fr.at[d - 1], to)
+        )
+        weights.append(
+            remote(p_ref.at[:, b], p_far.at[d - 1], ps.at[d - 1], pr.at[d - 1], to)
+        )
+    for c in weights:
+        c.start()
+    query_blk = q_ref[...]
+    q_t = query_blk.T
+    for head in range(3):
+        qt[head] = head_rows(q_t, head)
+        qm[head] = head_cols(query_blk, head)
+    dqt[...] = jnp.zeros_like(dqt)
+    nt = (((1,), (1,)), ((), ()))
+    branch = b_ref[...].reshape(512, 768)
+    own_heads = pl.ds(pl.multiple_of(192 * z, 64), 192)
+    grad_blk = lax.dot_general(
+        branch[:, :384], w_ref[0, own_heads], nt, preferred_element_type=F32
+    )
+    grad_blk += lax.dot_general(
+        branch[:, 384:], w_ref[1, own_heads], nt, preferred_element_type=F32
+    )
+    grad_blk = grad_blk.astype(BF)
+    g_t = grad_blk.T
+    for head in range(3):
+        at = slice(64 * head, 64 * head + 64)
+        gt[head] = head_rows(g_t, head)
+        gm[head] = head_cols(grad_blk, head)
+        delta[head : head + 1] = jnp.sum(g_t[at].astype(F32) * ot_ref[at], 0, keepdims=True)
+
+    def block(by, bk, masked, to_ref, to):
+        keys = kv_ref[by, bk, :, :192]
+        values = kv_ref[by, bk, :, 192:]
+        keys_t = keys.T
+        if masked:
+            key_at = place(lax.broadcasted_iota(jnp.int32, (512, 512), 0)) + 128 * bk
+            query_at = place(lax.broadcasted_iota(jnp.int32, (512, 512), 1)) + 128 * k
+            visible = query_at >= key_at
+        dk = dv = None
+        for head in range(3):
+            s = dot(keys, qt[head])
+            p = jnp.exp(s - lse_ref[head : head + 1])
+            if masked:
+                p = jnp.where(visible, p, 0.0)
+            dp = dot(values, gt[head])
+            ds = (p * (dp - delta[head : head + 1])).astype(BF)
+            pv = dot(p.astype(BF), gm[head])
+            pk = dot(ds, qm[head])
+            dv = pv if dv is None else dv + pv
+            dk = pk if dk is None else dk + pk
+            at = slice(64 * head, 64 * head + 64)
+            dqt[at] += dot(keys_t[at], ds)
+        to_ref[to, :, :192] = dk.astype(BF)
+        to_ref[to, :, 192:] = dv.astype(BF)
+
+    def cross(d):
+        return remote(out_buf.at[d], got.at[d], cs.at[d], cr.at[d], sib)
+
+    def up(d):
+        return remote(keep.at[d], far.at[d], ys.at[d], yr.at[d], device(y - d, z, k, x))
+
+    def earlier(i, carry):
+        d = y - i
+        block(y - d, 1 - k, False, out_buf, d)
+        cross(d).start()
+        block(y - d, k, False, keep, d)
+        cross(d).wait_recv()
+        keep[d] = (keep[d].astype(F32) + got[d].astype(F32)).astype(BF)
+        up(d).start()
+        return carry
+
+    lax.fori_loop(0, y, earlier, 0)
+    block(y, 1 - k, True, out_buf, 0)
+    cross(0).start()
+
+    for c in weights:
+        c.wait()
+    f_sum[...] = (
+        f_ref[:, x].astype(F32)
+        + f_far[0].astype(F32)
+        + f_far[1].astype(F32)
+        + f_far[2].astype(F32)
+    ).astype(BF)
+    p_sum[...] = (
+        p_ref[:, x].astype(F32)
+        + p_far[0].astype(F32)
+        + p_far[1].astype(F32)
+        + p_far[2].astype(F32)
+    ).astype(BF)
+
+    def f_copy(a):
+        return remote(
+            f_sum.at[a], f_all.at[me], s4.at[a], r4.at[me], device(a, x, k, x)
+        )
+
+    def p_copy(j):
+        return remote(
+            p_sum.at[j], p_all.at[y], s6.at[j], r6.at[y], device(z, 2 * k + j, k, x)
+        )
+
+    f_here = [(a == y) & (z == x) for a in range(4)]
+    p_here = [(y == z) & (z == 2 * k + j) for j in range(2)]
+    for a in range(4):
+
+        @pl.when(jnp.logical_not(f_here[a]))
+        def _():
+            f_copy(a).start()
+
+        @pl.when(f_here[a])
+        def _():
+            f_all[me] = f_sum[a]
+
+    for j in range(2):
+
+        @pl.when(jnp.logical_not(p_here[j]))
+        def _():
+            p_copy(j).start()
+
+        @pl.when(p_here[j])
+        def _():
+            p_all[y] = p_sum[j]
+
+    block(y, k, True, keep, 0)
+    dq_ref[...] = (dqt[...].T * 0.125).astype(BF)
+    cross(0).wait_recv()
+    for c in results:
+        c.wait()
+    out_ref[...] = (
+        base_ref[...]
+        + res_ref[z].astype(F32)
+        + r_far[0].astype(F32)
+        + r_far[1].astype(F32)
+        + r_far[2].astype(F32)
+    )
+    dkv_ref[...] = keep[0].astype(F32) + got[0].astype(F32)
+    for d in (1, 2, 3):
+
+        @pl.when(y + d < 4)
+        def _():
+            remote(keep.at[d], far.at[d], ys.at[d], yr.at[d], sib).wait_recv()
+            dkv_ref[...] += far[d].astype(F32)
+
+    @pl.when(z == x)
+    def _():
+        def arrive(i, carry):
+            @pl.when(i != me)
+            def _():
+                remote(f_sum.at[0], f_all.at[i], s4.at[0], r4.at[i], sib).wait_recv()
+
+            return carry
+
+        lax.fori_loop(0, 16, arrive, 0)
+        for b in range(4):
+            fo_ref[:, 384 * b : 384 * b + 384] = (
+                f_all[b].astype(F32)
+                + f_all[4 + b].astype(F32)
+                + f_all[8 + b].astype(F32)
+                + f_all[12 + b].astype(F32)
+            )
+
+    for a in range(4):
+
+        @pl.when((k == z // 2) & jnp.logical_not((a == y) & (z == y)))
+        def _():
+            remote(p_sum.at[0], p_all.at[a], s6.at[0], r6.at[a], sib).wait_recv()
+
+    @pl.when(k == z // 2)
+    def _():
+        po_ref[...] = (
+            p_all[0].astype(F32)
+            + p_all[1].astype(F32)
+            + p_all[2].astype(F32)
+            + p_all[3].astype(F32)
+        )
+
+    for a in range(4):
+
+        @pl.when(jnp.logical_not(f_here[a]))
+        def _():
+            f_copy(a).wait_send()
+
+    for j in range(2):
+
+        @pl.when(jnp.logical_not(p_here[j]))
+        def _():
+            p_copy(j).wait_send()
+
+    cross(0).wait_send()
+    for d in (1, 2, 3):
+
+        @pl.when(y >= d)
+        def _():
+            cross(d).wait_send()
+            up(d).wait_send()
+
+
+def middle(heads_all, x_group, dy_group, wo, wf, wp, vec_rows, query, kv_all, out_t, lse):
+    def kernel(*refs):
+        (h_ref, x_ref, dy_ref, wo_ref, wf_ref, wp_ref, v_ref) = refs[:7]
+        (q_ref, kv_ref, ot_ref, lse_ref) = refs[7:11]
+        (gx_ref, bo_ref, gfb_ref, gv_ref) = refs[11:15]
+        back_outs = refs[15:20]
+        (base_ref, res_ref, gwf_ref, gwp_ref) = refs[20:24]
+        feed_rest = refs[24:45]
+        back_rest = refs[45:]
         y, z, k, x = coords()
-        sib = device(y, z, 1 - k, x)
-        steps = (1, 2, 3)
-        me = y * 4 + z
         everyone = greet(
-            [sib]
-            + [device(y, z, k, ring(x, d)) for d in steps]
+            [device(y, z, 1 - k, x)]
+            + [device(y, z, k, ring(x, d)) for d in (1, 2, 3)]
             + [
                 device(ring(y, a), ring(z, b), k, x)
                 for a in range(4)
@@ -985,227 +1349,27 @@
                 if (a, b) != (0, 0)
             ]
         )
-        query_blk = q_ref[...]
-        q_t = query_blk.T
-        for head in range(3):
-            qt[head] = head_rows(q_t, head)
-            qm[head] = head_cols(query_blk, head)
-        dqt[...] = jnp.zeros_like(dqt)
-        nt = (((1,), (1,)), ((), ()))
-        own_heads = pl.ds(pl.multiple_of(192 * z, 64), 192)
-        grad_blk = lax.dot_general(
-            b_ref[:, :384], w_ref[0, own_heads], nt, preferred_element_type=F32
-        )
-        grad_blk += lax.dot_general(
-            b_ref[:, 384:], w_ref[1, own_heads], nt, preferred_element_type=F32
-        )
-        grad_blk = grad_blk.astype(BF)
-        g_t = grad_blk.T
-        for head in range(3):
-            at = slice(64 * head, 64 * head + 64)
-            gt[head] = head_rows(g_t, head)
-            gm[head] = head_cols(grad_blk, head)
-            delta[head : head + 1] = jnp.sum(g_t[at].astype(F32) * ot_ref[at], 0, keepdims=True)
-
-        everyone()
-        results = []
-        for d in steps:
-            b = ring(z, d)
-            c = remote(
-                res_ref.at[b], r_far.at[d - 1], rs.at[d - 1], rr.at[d - 1], device(y, b, k, x)
-            )
-            c.start()
-            results.append(c)
-        weights = []
-        for d in steps:
-            b = ring(x, d)
-            to = device(y, z, k, b)
-            weights.append(
-                remote(f_ref.at[:, b], f_far.at[d - 1], fs.at[d - 1], fr.at[d - 1], to)
-            )
-            weights.append(
-                remote(p_ref.at[:, b], p_far.at[d - 1], ps.at[d - 1], pr.at[d - 1], to)
-            )
-        for c in weights:
-            c.start()
-        def block(by, bk, masked, to_ref, to):
-            keys = kv_ref[by, bk, :, :192]
-            values = kv_ref[by, bk, :, 192:]
-            keys_t = keys.T
-            if masked:
-                key_at = place(lax.broadcasted_iota(jnp.int32, (512, 512), 0)) + 128 * bk
-                query_at = place(lax.broadcasted_iota(jnp.int32, (512, 512), 1)) + 128 * k
-                visible = query_at >= key_at
-            dk = dv = None
-            for head in range(3):
-                s = dot(keys, qt[head])
-                p = jnp.exp(s - lse_ref[head : head + 1])
-                if masked:
-                    p = jnp.where(visible, p, 0.0)
-                dp = dot(values, gt[head])
-                ds = (p * (dp - delta[head : head + 1])).astype(BF)
-                pv = dot(p.astype(BF), gm[head])
-                pk = dot(ds, qm[head])
-                dv = pv if dv is None else dv + pv
-                dk = pk if dk is None else dk + pk
-                at = slice(64 * head, 64 * head + 64)
-                dqt[at] += dot(keys_t[at], ds)
-            to_ref[to, :, :192] = dk.astype(BF)
-            to_ref[to, :, 192:] = dv.astype(BF)
-
-        def cross(d):
-            return remote(out_buf.at[d], got.at[d], cs.at[d], cr.at[d], sib)
-
-        def up(d):
-            return remote(keep.at[d], far.at[d], ys.at[d], yr.at[d], device(y - d, z, k, x))
-
-        def earlier(i, carry):
-            d = y - i
-            block(y - d, 1 - k, False, out_buf, d)
-            cross(d).start()
-            block(y - d, k, False, keep, d)
-            cross(d).wait_recv()
-            keep[d] = (keep[d].astype(F32) + got[d].astype(F32)).astype(BF)
-            up(d).start()
-            return carry
-
-        lax.fori_loop(0, y, earlier, 0)
-        block(y, 1 - k, True, out_buf, 0)
-        cross(0).start()
-
-        for c in weights:
-            c.wait()
-        f_sum[...] = (
-            f_ref[:, x].astype(F32)
-            + f_far[0].astype(F32)
-            + f_far[1].astype(F32)
-            + f_far[2].astype(F32)
-        ).astype(BF)
-        p_sum[...] = (
-            p_ref[:, x].astype(F32)
-            + p_far[0].astype(F32)
-            + p_far[1].astype(F32)
-            + p_far[2].astype(F32)
-        ).astype(BF)
-
-        def f_copy(a):
-            return remote(
-                f_sum.at[a], f_all.at[me], s4.at[a], r4.at[me], device(a, x, k, x)
-            )
-
-        def p_copy(j):
-            return remote(
-                p_sum.at[j], p_all.at[y], s6.at[j], r6.at[y], device(z, 2 * k + j, k, x)
-            )
-
-        f_here = [(a == y) & (z == x) for a in range(4)]
-        p_here = [(y == z) & (z == 2 * k + j) for j in range(2)]
-        for a in range(4):
-
-            @pl.when(jnp.logical_not(f_here[a]))
-            def _():
-                f_copy(a).start()
-
-            @pl.when(f_here[a])
-            def _():
-                f_all[me] = f_sum[a]
-
-        for j in range(2):
-
-            @pl.when(jnp.logical_not(p_here[j]))
-            def _():
-                p_copy(j).start()
-
-            @pl.when(p_here[j])
-            def _():
-                p_all[y] = p_sum[j]
-
-        block(y, k, True, keep, 0)
-        dq_ref[...] = (dqt[...].T * 0.125).astype(BF)
-        cross(0).wait_recv()
-        for c in results:
-            c.wait()
-        out_ref[...] = (
-            base_ref[...]
-            + res_ref[z].astype(F32)
-            + r_far[0].astype(F32)
-            + r_far[1].astype(F32)
-            + r_far[2].astype(F32)
-        )
-        dkv_ref[...] = keep[0].astype(F32) + got[0].astype(F32)
-        for d in (1, 2, 3):
-
-            @pl.when(y + d < 4)
-            def _():
-                remote(keep.at[d], far.at[d], ys.at[d], yr.at[d], sib).wait_recv()
-                dkv_ref[...] += far[d].astype(F32)
-
-        @pl.when(z == x)
-        def _():
-            def arrive(i, carry):
-                @pl.when(i != me)
-                def _():
-                    remote(f_sum.at[0], f_all.at[i], s4.at[0], r4.at[i], sib).wait_recv()
-
-                return carry
-
-            lax.fori_loop(0, 16, arrive, 0)
-            for b in range(4):
-                fo_ref[:, 384 * b : 384 * b + 384] = (
-                    f_all[b].astype(F32)
-                    + f_all[4 + b].astype(F32)
-                    + f_all[8 + b].astype(F32)
-                    + f_all[12 + b].astype(F32)
-                )
-
-        for a in range(4):
-
-            @pl.when((k == z // 2) & jnp.logical_not((a == y) & (z == y)))
-            def _():
-                remote(p_sum.at[0], p_all.at[a], s6.at[0], r6.at[a], sib).wait_recv()
-
-        @pl.when(k == z // 2)
-        def _():
-            po_ref[...] = (
-                p_all[0].astype(F32)
-                + p_all[1].astype(F32)
-                + p_all[2].astype(F32)
-                + p_all[3].astype(F32)
-            )
-
-        for a in range(4):
-
-            @pl.when(jnp.logical_not(f_here[a]))
-            def _():
-                f_copy(a).wait_send()
-
-        for j in range(2):
-
-            @pl.when(jnp.logical_not(p_here[j]))
-            def _():
-                p_copy(j).wait_send()
-
-        cross(0).wait_send()
-        for d in (1, 2, 3):
-
-            @pl.when(y >= d)
-            def _():
-                cross(d).wait_send()
-                up(d).wait_send()
-
-    return comm(
-        kernel,
-        [
-            jax.ShapeDtypeStruct((512, 192), BF),
-            jax.ShapeDtypeStruct((512, 384), F32),
-            jax.ShapeDtypeStruct((48, 1536), F32),
-            jax.ShapeDtypeStruct((48, 768), F32),
-            jax.ShapeDtypeStruct((128, 768), F32),
-        ],
-        5,
-        (4, 4, 4, 4, 3, 3, 3, 3, 3, 3, 4, 16, 2, 4),
-        (query, branch, wo, kv_all, out_t, lse, fc, proj, base, result),
-        scratch=[
+        feed_body(
+            h_ref, x_ref, dy_ref, wo_ref, wf_ref, wp_ref, v_ref,
+            base_ref, res_ref, gx_ref, bo_ref, gwf_ref, gwp_ref, gfb_ref, gv_ref,
+            *feed_rest, everyone,
+        )
+        back_body(
+            q_ref, bo_ref, wo_ref, kv_ref, ot_ref, lse_ref, gwf_ref, gwp_ref, base_ref, res_ref,
+            *back_outs, *back_rest,
+        )
+
+    feed_scratch = ([pltpu.VMEM((2, 512, 768), BF),
+            pltpu.VMEM((2, 512, 384), BF),
+            pltpu.VMEM((2, 512, 384), BF),
+            pltpu.VMEM((512, 768), F32),
+            pltpu.VMEM((512, 768), F32),
+            pltpu.VMEM((512, 128), F32),
+        ]
+        + [pltpu.VMEM((4, 128, 768), BF)] * 5
+        + [pltpu.VMEM((3, 128, 768), BF)]
+        + [pltpu.VMEM((128, 768), BF)])
+    back_scratch = [
             pltpu.VMEM((3, 192, 512), BF),
             pltpu.VMEM((3, 192, 512), BF),
             pltpu.VMEM((3, 512, 192), BF),
@@ -1223,188 +1387,38 @@
             pltpu.VMEM((2, 48, 768), BF),
             pltpu.VMEM((16, 48, 384), BF),
             pltpu.VMEM((4, 48, 768), BF),
-        ],
-        spaces=([VMEM] * 10, [VMEM] * 5),
-        name="attend_back",
-    )
-
-
-def normalize(rows):
-    centered = rows - jnp.mean(rows, -1, keepdims=True)
-    inverse = lax.rsqrt(jnp.mean(centered * centered, -1, keepdims=True) + EPSILON)
-    return centered * inverse, inverse
-
-
-def normalize_back(normed, inverse, gain, grad):
-    scaled = grad * gain
-    return inverse * (
-        scaled
-        - jnp.mean(scaled, -1, keepdims=True)
-        - normed * jnp.mean(scaled * normed, -1, keepdims=True)
-    )
-
-
-def feed_forward(heads_all, x_group, dy_group, wo, wf, wp, vec_rows):
-    def kernel(
-        h_ref, x_ref, dy_ref, wo_ref, wf_ref, wp_ref, v_ref,
-        base_ref, res_mine, gx_ref, bo_ref, gwf_ref, gwp_ref, gfb_ref, gv_ref,
-        a2, act, df, x_two, normed, inverse, norm_other, norm_mine, res_other,
-        norm_got, res_got, norm_far, branch,
-        cs, cr, es, er, zs, zr, bs, br,
-    ):
-        y, z, k, x = coords()
-        sib = device(y, z, 1 - k, x)
-        steps = (1, 2, 3)
-        everyone = greet([sib] + [device(y, ring(z, d), k, x) for d in steps])
-        out_bias, gain, shift, proj_bias = (v_ref[i : i + 1] for i in range(4, 8))
-        fc_bias = jnp.zeros((1, 384), F32)
-        for b in range(4):
-            row = v_ref[8 + b : 9 + b, pl.ds(pl.multiple_of(384 * k, 128), 384)]
-            fc_bias = fc_bias + jnp.where(z == b, row, 0.0)
-
-        def half(kk, norm_ref):
-            two = x_ref[kk].reshape(512, 768).astype(F32) + out_bias
-            for g in range(4):
-                h = h_ref[g, kk]
-                at = slice(192 * g, 192 * g + 192)
-                part = jnp.concatenate([dot(h, wo_ref[0, at]), dot(h, wo_ref[1, at])], 1)
-                two = two + part
-            x_two[...] = two
-            n, inv = normalize(two)
-            normed[...] = n
-            inverse[...] = jnp.broadcast_to(inv, (512, 128))
-            a = (n * gain + shift).astype(BF)
-            a2[kk] = a
-            hidden = dot(a, wf_ref[...]) + fc_bias
-            square = hidden * hidden
-            t = jnp.tanh(0.7978845608028654 * (hidden + 0.044715 * square * hidden))
-            act_blk = (0.5 * hidden * (1.0 + t)).astype(BF)
-            act[kk] = act_blk
-            slope = 0.5 * (1.0 + t) + 0.5 * hidden * (1.0 - t * t) * (
-                0.7978845608028654 * (1.0 + 3 * 0.044715 * square)
-            )
-            dy = dy_ref[kk].reshape(512, 768)
-            back = lax.dot_general(
-                dy, wp_ref[...], (((1,), (1,)), ((), ())), preferred_element_type=F32
-            )
-            df_blk = (back * slope).astype(BF)
-            df[kk] = df_blk
-            norm_part = lax.dot_general(
-                df_blk, wf_ref[...], (((1,), (1,)), ((), ())), preferred_element_type=F32
-            )
-            norm_ref[...] = norm_part.astype(BF).reshape(4, 128, 768)
-
-        def result(kk, res_ref):
-            res_ref[...] = dot(act[kk], wp_ref[...]).astype(BF).reshape(4, 128, 768)
-
-        half(1 - k, norm_other)
-        everyone()
-        swaps = []
-        for d in (1, 2, 3, 0):
-            b = ring(z, d)
-            c = remote(norm_other.at[b], norm_got.at[b], cs.at[d], cr.at[d], sib)
-            c.start()
-            swaps.append(c)
-        half(k, norm_mine)
-        sends = []
-        for d in steps:
-            b = ring(z, d)
-            swaps[d - 1].wait_recv()
-            norm_mine[b] = (norm_mine[b].astype(F32) + norm_got[b].astype(F32)).astype(BF)
-            c = remote(
-                norm_mine.at[b], norm_far.at[d - 1], zs.at[d - 1], zr.at[d - 1],
-                device(y, b, k, x),
-            )
-            c.start()
-            sends.append(c)
-        result(1 - k, res_other)
-        for d in (1, 2, 3, 0):
-            b = ring(z, d)
-            c = remote(res_other.at[b], res_got.at[b], es.at[d], er.at[d], sib)
-            c.start()
-            swaps.append(c)
-        tn = (((0,), (0,)), ((), ()))
-        gwf = lax.dot_general(a2[0], df[0], tn, preferred_element_type=F32)
-        gwf += lax.dot_general(a2[1], df[1], tn, preferred_element_type=F32)
-        gwf_ref[...] = gwf.astype(BF)
-        own_rows = pl.ds(pl.multiple_of(128 * z, 128), 128)
-        swaps[3].wait_recv()
-        for c in sends:
-            c.wait_recv()
-        da = (
-            norm_mine[z].astype(F32)
-            + norm_got[z].astype(F32)
-            + norm_far[0].astype(F32)
-            + norm_far[1].astype(F32)
-            + norm_far[2].astype(F32)
-        )
-        n = normed[own_rows]
-        dy = dy_ref[k, z].astype(F32)
-        gx = dy + normalize_back(n, inverse[own_rows, 0:1], gain, da)
-        gx_ref[...] = gx
-        low = gx.astype(BF)
-        branch[...] = low
-        bo_ref[z] = low
-        branches = []
-        for d in steps:
-            c = remote(
-                branch, bo_ref.at[z], bs.at[d - 1], br.at[d - 1], device(y, ring(z, d), k, x)
-            )
-            c.start()
-            branches.append(c)
-        result(k, res_mine)
-        gwp = lax.dot_general(
-            act[0], dy_ref[0].reshape(512, 768), tn, preferred_element_type=F32
-        )
-        gwp += lax.dot_general(
-            act[1], dy_ref[1].reshape(512, 768), tn, preferred_element_type=F32
-        )
-        gwp_ref[...] = gwp.astype(BF)
-        gfb_ref[...] = jnp.sum(df[0].astype(F32), 0, keepdims=True) + jnp.sum(
-            df[1].astype(F32), 0, keepdims=True
-        )
-        gv_ref[0:1] = jnp.sum(low.astype(F32), 0, keepdims=True)
-        gv_ref[1:2] = jnp.sum(da * n, 0, keepdims=True)
-        gv_ref[2:3] = jnp.sum(da, 0, keepdims=True)
-        gv_ref[3:4] = jnp.sum(dy, 0, keepdims=True)
-        for c in swaps[4:]:
-            c.wait_recv()
-        res_mine[...] = (res_mine[...].astype(F32) + res_got[...].astype(F32)).astype(BF)
-        base_ref[...] = x_two[own_rows] + proj_bias
-        for c in branches:
-            c.wait()
-        for c in swaps + sends:
-            c.wait_send()
-
-    return comm(
+    ]
+    dma = pltpu.SemaphoreType.DMA
+    return pl.pallas_call(
         kernel,
-        [
+        out_shape=[
             jax.ShapeDtypeStruct((128, 768), F32),
             jax.ShapeDtypeStruct((4, 128, 768), BF),
-            jax.ShapeDtypeStruct((128, 768), F32),
-            jax.ShapeDtypeStruct((4, 128, 768), BF),
-            jax.ShapeDtypeStruct((768, 384), BF),
-            jax.ShapeDtypeStruct((384, 768), BF),
             jax.ShapeDtypeStruct((1, 384), F32),
             jax.ShapeDtypeStruct((4, 768), F32),
+            jax.ShapeDtypeStruct((512, 192), BF),
+            jax.ShapeDtypeStruct((512, 384), F32),
+            jax.ShapeDtypeStruct((48, 1536), F32),
+            jax.ShapeDtypeStruct((48, 768), F32),
+            jax.ShapeDtypeStruct((128, 768), F32),
         ],
-        3,
-        (4, 4, 4, 4, 3, 3, 3, 3),
-        (heads_all, x_group, dy_group, wo, wf, wp, vec_rows),
-        scratch=[
-            pltpu.VMEM((2, 512, 768), BF),
-            pltpu.VMEM((2, 512, 384), BF),
-            pltpu.VMEM((2, 512, 384), BF),
-            pltpu.VMEM((512, 768), F32),
-            pltpu.VMEM((512, 768), F32),
-            pltpu.VMEM((512, 128), F32),
+        in_specs=[VMEM] * 11,
+        out_specs=[VMEM] * 9,
+        scratch_shapes=[
+            pltpu.VMEM((128, 768), F32),
+            pltpu.VMEM((4, 128, 768), BF),
+            pltpu.VMEM((4, 4, 48, 384), BF),
+            pltpu.VMEM((2, 4, 48, 768), BF),
         ]
-        + [pltpu.VMEM((4, 128, 768), BF)] * 5
-        + [pltpu.VMEM((3, 128, 768), BF)]
-        + [pltpu.VMEM((128, 768), BF)],
-        spaces=([VMEM] * 7, [VMEM] * 8),
-        name="feed_forward",
-    )
+        + feed_scratch
+        + [dma((n,)) for n in (4, 4, 4, 4, 3, 3, 3, 3)]
+        + back_scratch
+        + [dma((n,)) for n in (4, 4, 4, 4, 3, 3, 3, 3, 3, 3, 4, 16, 2, 4)],
+        compiler_params=pltpu.CompilerParams(
+            collective_id=3, has_side_effects=True, vmem_limit_bytes=LIMIT
+        ),
+        name="middle",
+    )(heads_all, x_group, dy_group, wo, wf, wp, vec_rows, query, kv_all, out_t, lse)
 
 
 def adam_update(weight, moment_one, moment_two, gradient, rate, decay):
@@ -1445,7 +1459,10 @@
     ) = forward(w_qkv, w_fc, w_out, w_proj, vectors, tokens[0], cotangent[0])
     wq = wq.reshape(768, 640)
     wo = wo.reshape(2, 768, 384)
-    base, result, grad_x_two, branch_core, grad_w_fc, grad_w_proj, grad_fc_bias, vec_sums = feed_forward(
+    (
+        grad_x_two, branch_core, grad_fc_bias, vec_sums, grad_query, grad_kv, fc_sum, proj_sum,
+        result_sum,
+    ) = middle(
         heads_all,
         x_group,
         dy_group,
@@ -1453,20 +1470,12 @@
         wf.reshape(768, 384),
         wp.reshape(384, 768),
         vec_rows,
-    )
-    branch_core = branch_core.reshape(512, 768)
-    grad_query, grad_kv, fc_sum, proj_sum, result_sum = attend_back(
         query,
-        branch_core,
-        wo,
         kv_all,
         out_t,
         lse,
-        grad_w_fc.reshape(4, 4, 48, 384),
-        grad_w_proj.reshape(2, 4, 48, 768),
-        base,
-        result,
     )
+    branch_core = branch_core.reshape(512, 768)
     grad_one, last_rows, proj_rows, fc_rows = last_sums(
         (
             act_one,

time: 196 us -> 193 us (0.985); the launches traced: 194 us -> 189 us
  Pallas kernels: 193 us -> 188 us
    pallas_call x4 -> x2, Pallas kernels: 190 us -> 119 us  [comm(): pl.pallas_call(kernel, out_shape=outs, in_specs=[ANY] * len(args) if spac...]
    pallas_call x0 -> x1, Pallas kernels: none -> 65.5 us  [middle(): pl.pallas_call(kernel, out_shape=[jax.ShapeDtypeStruct((128, 768), F32),...]
where the time goes in v8:
time: 193 us; the launch traced here: 189 us
  Pallas kernels  188 us (97%)
    pallas_call x2, Pallas kernels, comm(): pl.pallas_call(kernel, out_shape=outs, in_specs=[ANY] * len(args) if spac...  119 us
    pallas_call x1, Pallas kernels, middle(): pl.pallas_call(kernel, out_shape=[jax.ShapeDtypeStruct((128, 768), F32),...  65.5 us

profile of v8, /device:TPU:29, one launch (start us, length us, event | category | flops | bytes accessed | tf_op | source)
XLA Modules:
  0.0 189.1 jit_solution(14823490377179009588)
XLA Ops:
  0.7 77.3 %forward.1 = (bf16[4,2,512,192]{3,2,1,0:T(8,128)(2,1)}, f32[192,512]{1,0:T(8,128)}, f32[8,512]{1,0:T(8,128)}, bf16[4,2,512,384]{3,2,1,0:T(8,128)(2,1)}, bf16[2,4...) custom-call(f32[6,2304]{1,0:T(8,128)} %refs_8_.1, ...), custom_call_target="tpu_custom_call" | custom-call | tf_op jit(solution)/shard_map/forward/pallas_call | solution.py:48
  77.9 65.5 %middle.1 = (f32[128,768]{1,0:T(8,128)}, bf16[4,128,768]{2,1,0:T(8,128)(2,1)}, f32[1,384]{1,0:T(1,128)}, f32[4,768]{1,0:T(4,128)}, bf16[512,192]{1,0:T(8,128)(2,...) custom-call(bf16[4,2,512,192]{3,2,1,0:T(8,128)(2,1)} %get-tuple-element.63.refs_0_.refs_2_, ...), custom_call_target="tpu_custom_call" | custom-call | tf_op jit(solution)/shard_map/middle/pallas_call | solution.py:1392
  143.5 42.1 %last_sums.1 = (f32[128,768]{1,0:T(8,128)}, f32[8,8,1664]{2,1,0:T(8,128)}, f32[24,768]{1,0:T(8,128)}, f32[2,8,1536]{2,1,0:T(8,128)}) custom-call(bf16[512,768]{1,0:T(8,128)(2,1)} %get-tuple-element.61.refs_0_, bf16[512,768]{1,0:T(8,128)(2,1)} %get-tuple-element.62.refs_1_, bf16[4,2,512,192]{3,2,1,0:T(8,128)(2,1)} %get-tuple-element.63.refs_0_.refs_2_, ...), custom_call_target="tpu_custom_call" | custom-call | tf_op jit(solution)/shard_map/last_sums/pallas_call | solution.py:48
  185.6 3.3 %finish.1 = (f32[128,768]{1,0:T(8,128)}, f32[128,768]{1,0:T(8,128)}, f32[6,2304]{1,0:T(8,128)}, f32[6,2304]{1,0:T(8,128)}, f32[6,2304]{1,0:T(8,128)}, /*index=5*...) custom-call(f32[128,768]{1,0:T(8,128)} %get-tuple-element.82.refs_0_, ...), custom_call_target="tpu_custom_call" | custom-call | tf_op jit(solution)/shard_map/finish/pallas_call | solution.py:376

commit v9 on v8

--- a/solution.py
+++ b/solution.py
@@ -983,7 +983,7 @@
     base_ref, res_mine, gx_ref, bo_ref, gwf_ref, gwp_ref, gfb_ref, gv_ref,
     a2, act, df, x_two, normed, inverse, norm_other, norm_mine, res_other,
     norm_got, res_got, norm_far, branch,
-    cs, cr, es, er, zs, zr, bs, br, everyone,
+    cs, cr, es, er, zs, zr, bs, br, everyone, gradients_done,
 ):
     y, z, k, x = coords()
     sib = device(y, z, 1 - k, x)
@@ -1092,6 +1092,7 @@
         act[1], dy_ref[1].reshape(512, 768), tn, preferred_element_type=F32
     )
     gwp_ref[...] = gwp.astype(BF).reshape(2, 4, 48, 768)
+    gradients_done()
     gfb_ref[...] = jnp.sum(df[0].astype(F32), 0, keepdims=True) + jnp.sum(
         df[1].astype(F32), 0, keepdims=True
     )
@@ -1114,7 +1115,7 @@
     dq_ref, dkv_ref, fo_ref, po_ref, out_ref,
     qt, gt, qm, gm, delta, dqt, out_buf, keep, got, far, f_far, p_far, r_far,
     f_sum, p_sum, f_all, p_all,
-    cs, cr, ys, yr, fs, fr, ps, pr, rs, rr, s4, r4, s6, r6,
+    cs, cr, ys, yr, fs, fr, ps, pr, rs, rr, s4, r4, s6, r6, weights,
 ):
     y, z, k, x = coords()
     sib = device(y, z, 1 - k, x)
@@ -1128,18 +1129,6 @@
         )
         c.start()
         results.append(c)
-    weights = []
-    for d in steps:
-        b = ring(x, d)
-        to = device(y, z, k, b)
-        weights.append(
-            remote(f_ref.at[:, b], f_far.at[d - 1], fs.at[d - 1], fr.at[d - 1], to)
-        )
-        weights.append(
-            remote(p_ref.at[:, b], p_far.at[d - 1], ps.at[d - 1], pr.at[d - 1], to)
-        )
-    for c in weights:
-        c.start()
     query_blk = q_ref[...]
     q_t = query_blk.T
     for head in range(3):
@@ -1194,10 +1183,63 @@
     def up(d):
         return remote(keep.at[d], far.at[d], ys.at[d], yr.at[d], device(y - d, z, k, x))
 
+    def f_copy(a):
+        return remote(
+            f_sum.at[a], f_all.at[me], s4.at[a], r4.at[me], device(a, x, k, x)
+        )
+
+    def p_copy(j):
+        return remote(
+            p_sum.at[j], p_all.at[y], s6.at[j], r6.at[y], device(z, 2 * k + j, k, x)
+        )
+
+    f_here = [(a == y) & (z == x) for a in range(4)]
+    p_here = [(y == z) & (z == 2 * k + j) for j in range(2)]
+    def over_plane():
+        for c in weights:
+            c.wait()
+        f_sum[...] = (
+            f_ref[:, x].astype(F32)
+            + f_far[0].astype(F32)
+            + f_far[1].astype(F32)
+            + f_far[2].astype(F32)
+        ).astype(BF)
+        p_sum[...] = (
+            p_ref[:, x].astype(F32)
+            + p_far[0].astype(F32)
+            + p_far[1].astype(F32)
+            + p_far[2].astype(F32)
+        ).astype(BF)
+
+        for a in range(4):
+
+            @pl.when(jnp.logical_not(f_here[a]))
+            def _():
+                f_copy(a).start()
+
+            @pl.when(f_here[a])
+            def _():
+                f_all[me] = f_sum[a]
+
+        for j in range(2):
+
+            @pl.when(jnp.logical_not(p_here[j]))
+            def _():
+                p_copy(j).start()
+
+            @pl.when(p_here[j])
+            def _():
+                p_all[y] = p_sum[j]
+
     def earlier(i, carry):
         d = y - i
         block(y - d, 1 - k, False, out_buf, d)
         cross(d).start()
+
+        @pl.when(i == 0)
+        def _():
+            over_plane()
+
         block(y - d, k, False, keep, d)
         cross(d).wait_recv()
         keep[d] = (keep[d].astype(F32) + got[d].astype(F32)).astype(BF)
@@ -1208,52 +1250,10 @@
     block(y, 1 - k, True, out_buf, 0)
     cross(0).start()
 
-    for c in weights:
-        c.wait()
-    f_sum[...] = (
-        f_ref[:, x].astype(F32)
-        + f_far[0].astype(F32)
-        + f_far[1].astype(F32)
-        + f_far[2].astype(F32)
-    ).astype(BF)
-    p_sum[...] = (
-        p_ref[:, x].astype(F32)
-        + p_far[0].astype(F32)
-        + p_far[1].astype(F32)
-        + p_far[2].astype(F32)
-    ).astype(BF)
-
-    def f_copy(a):
-        return remote(
-            f_sum.at[a], f_all.at[me], s4.at[a], r4.at[me], device(a, x, k, x)
-        )
-
-    def p_copy(j):
-        return remote(
-            p_sum.at[j], p_all.at[y], s6.at[j], r6.at[y], device(z, 2 * k + j, k, x)
-        )
-
-    f_here = [(a == y) & (z == x) for a in range(4)]
-    p_here = [(y == z) & (z == 2 * k + j) for j in range(2)]
-    for a in range(4):
-
-        @pl.when(jnp.logical_not(f_here[a]))
-        def _():
-            f_copy(a).start()
-
-        @pl.when(f_here[a])
-        def _():
-            f_all[me] = f_sum[a]
-
-    for j in range(2):
-
-        @pl.when(jnp.logical_not(p_here[j]))
-        def _():
-            p_copy(j).start()
-
-        @pl.when(p_here[j])
-        def _():
-            p_all[y] = p_sum[j]
+    @pl.when(y == 0)
+    def _():
+        over_plane()
+
 
     block(y, k, True, keep, 0)
     dq_ref[...] = (dqt[...].T * 0.125).astype(BF)
@@ -1349,14 +1349,27 @@
                 if (a, b) != (0, 0)
             ]
         )
+        f_far, p_far = back_rest[10], back_rest[11]
+        fs, fr, ps, pr = back_rest[21:25]
+        steps = (1, 2, 3)
+        weights = []
+        for d in steps:
+            b = ring(x, d)
+            to = device(y, z, k, b)
+            weights.append(
+                remote(gwf_ref.at[:, b], f_far.at[d - 1], fs.at[d - 1], fr.at[d - 1], to)
+            )
+            weights.append(
+                remote(gwp_ref.at[:, b], p_far.at[d - 1], ps.at[d - 1], pr.at[d - 1], to)
+            )
         feed_body(
             h_ref, x_ref, dy_ref, wo_ref, wf_ref, wp_ref, v_ref,
             base_ref, res_ref, gx_ref, bo_ref, gwf_ref, gwp_ref, gfb_ref, gv_ref,
-            *feed_rest, everyone,
+            *feed_rest, everyone, lambda: [c.start() for c in weights],
         )
         back_body(
             q_ref, bo_ref, wo_ref, kv_ref, ot_ref, lse_ref, gwf_ref, gwp_ref, base_ref, res_ref,
-            *back_outs, *back_rest,
+            *back_outs, *back_rest, weights,
         )
 
     feed_scratch = ([pltpu.VMEM((2, 512, 768), BF),

time: 193 us -> 186 us (0.964); the launches traced: 189 us -> 184 us
  Pallas kernels: 188 us -> 184 us
    pallas_call x2, Pallas kernels: 119 us -> 116 us  [comm(): pl.pallas_call(kernel, out_shape=outs, in_specs=[ANY] * len(args) if spac...]
where the time goes in v9:
time: 186 us; the launch traced here: 184 us
  Pallas kernels  184 us (99%)
    pallas_call x2, Pallas kernels, comm(): pl.pallas_call(kernel, out_shape=outs, in_specs=[ANY] * len(args) if spac...  116 us
    pallas_call x1, Pallas kernels, middle(): pl.pallas_call(kernel, out_shape=[jax.ShapeDtypeStruct((128, 768), F32),...  64.2 us

profile of v9, /device:TPU:29, one launch (start us, length us, event | category | flops | bytes accessed | tf_op | source)
XLA Modules:
  0.0 184.5 jit_solution(2361064988898045587)
XLA Ops:
  0.7 77.3 %forward.1 = (bf16[4,2,512,192]{3,2,1,0:T(8,128)(2,1)}, f32[192,512]{1,0:T(8,128)}, f32[8,512]{1,0:T(8,128)}, bf16[4,2,512,384]{3,2,1,0:T(8,128)(2,1)}, bf16[2,4...) custom-call(f32[6,2304]{1,0:T(8,128)} %refs_8_.1, ...), custom_call_target="tpu_custom_call" | custom-call | tf_op jit(solution)/shard_map/forward/pallas_call | solution.py:48
  77.9 64.2 %middle.1 = (f32[128,768]{1,0:T(8,128)}, bf16[4,128,768]{2,1,0:T(8,128)(2,1)}, f32[1,384]{1,0:T(1,128)}, f32[4,768]{1,0:T(4,128)}, bf16[512,192]{1,0:T(8,128)(2,...) custom-call(bf16[4,2,512,192]{3,2,1,0:T(8,128)(2,1)} %get-tuple-element.63.refs_0_.refs_2_, ...), custom_call_target="tpu_custom_call" | custom-call | tf_op jit(solution)/shard_map/middle/pallas_call | solution.py:1405
  142.2 38.7 %last_sums.1 = (f32[128,768]{1,0:T(8,128)}, f32[8,8,1664]{2,1,0:T(8,128)}, f32[24,768]{1,0:T(8,128)}, f32[2,8,1536]{2,1,0:T(8,128)}) custom-call(bf16[512,768]{1,0:T(8,128)(2,1)} %get-tuple-element.61.refs_0_, bf16[512,768]{1,0:T(8,128)(2,1)} %get-tuple-element.62.refs_1_, bf16[4,2,512,192]{3,2,1,0:T(8,128)(2,1)} %get-tuple-element.63.refs_0_.refs_2_, ...), custom_call_target="tpu_custom_call" | custom-call | tf_op jit(solution)/shard_map/last_sums/pallas_call | solution.py:48
  180.9 3.3 %finish.1 = (f32[128,768]{1,0:T(8,128)}, f32[128,768]{1,0:T(8,128)}, f32[6,2304]{1,0:T(8,128)}, f32[6,2304]{1,0:T(8,128)}, f32[6,2304]{1,0:T(8,128)}, /*index=5*...) custom-call(f32[128,768]{1,0:T(8,128)} %get-tuple-element.82.refs_0_, ...), custom_call_target="tpu_custom_call" | custom-call | tf_op jit(solution)/shard_map/finish/pallas_call | solution.py:376
